TPU v7x, 128 devices: a whole 4x4x4 slice. The times are simulated.
128 devices in a mesh: gx: 8 (over z, y_hi), gy: 16 (over x, y_lo, core).
Axes of the slice: x: 4, y: 4 (y_hi: 2, y_lo: 2; y = y_hi * 2 + y_lo), z: 4, core: 2. Of those that a mesh axis runs over, the one named last changes fastest.
Arguments:
- forcing: float32 [16, 256, 1024], P(None, 'gy', 'gx'), may hold values from -6 to 6
- pressure_in: float32 [16, 256, 1024], P(None, 'gy', 'gx'), may hold values from -6 to 6
- x_coupling: float32 [16, 256, 1024], P(None, 'gy', 'gx'), may hold values from 0.5 to 2000
- y_coupling: float32 [16, 256, 1024], P(None, 'gy', 'gx'), may hold values from 0.5 to 2000
- z_coupling: float32 [16, 256, 1024], P(None, 'gy', 'gx'), may hold values from 0.05 to 0.5
- damping: float32 [16, 256, 1024], P(None, 'gy', 'gx'), may hold values from 0.2 to 2
Outputs:
- pressure: float32 [16, 256, 1024], P(None, 'gy', 'gx')
- coarse_residual: float32 [8, 128, 512], P(None, 'gy', 'gx')
- coarse_correction: float32 [8, 128, 512], P(None, 'gy')
All inputs are finite; a program needn't handle non-finite values.
Results may differ from a plain program's by a relative error of at most 0.0001.
Values sent between devices are 32-bit elements; how exact they have to be, the bound alone decides.
No kernel may reach another device: no remote copies, remote signals or barrier semaphores. Data moves between devices by JAX's collectives and lax.ppermute only.
A program may use at most 128 MiB of HBM per device.

v0:
```python
import jax
import jax.numpy as jnp
from jax import lax
from jax.sharding import PartitionSpec as P

COARSE = 3


RELAX = 0.8


def extended(value, sides, width):
    for axis, dim in sides:
        peers, length = (lax.axis_size(axis), value.shape[dim])
        up = [(i, (i + 1) % peers) for i in range(peers - 1)]
        down = [(j, i) for i, j in up]
        last = lax.slice_in_dim(value, length - width, length, axis=dim)
        leading = lax.slice_in_dim(value, 0, width, axis=dim)
        before = lax.ppermute(last, axis, up)
        after = lax.ppermute(leading, axis, down)
        value = jnp.concatenate([before, value, after], axis=dim)
    return value


def from_behind(value, axis, steps):
    count = lax.axis_size(axis)
    leading, last = (max(0, -steps), min(count, count - steps))
    return lax.ppermute(value, axis, [(source, source + steps) for source in range(leading, last)])


def shifted(values, offset, axis_dim, filler):
    length = values.shape[axis_dim]
    if offset > 0:
        border = jnp.full_like(lax.slice_in_dim(values, 0, offset, axis=axis_dim), filler)
        return jnp.concatenate(
            [border, lax.slice_in_dim(values, 0, length - offset, axis=axis_dim)], axis=axis_dim
        )
    amount = -offset
    border = jnp.full_like(lax.slice_in_dim(values, 0, amount, axis=axis_dim), filler)
    return jnp.concatenate(
        [lax.slice_in_dim(values, amount, length, axis=axis_dim), border], axis=axis_dim
    )


def line_solve(low_band, diagonal, up_band, right_side, axis_dim):
    length = right_side.shape[axis_dim]
    stride = 1
    while stride < length:
        before = shifted(diagonal, stride, axis_dim, 1.0)
        after = shifted(diagonal, -stride, axis_dim, 1.0)
        weight_low = -low_band / before
        weight_up = -up_band / after
        new_diag = (
            diagonal
            + weight_low * shifted(up_band, stride, axis_dim, 0.0)
            + weight_up * shifted(low_band, -stride, axis_dim, 0.0)
        )
        new_right = (
            right_side
            + weight_low * shifted(right_side, stride, axis_dim, 0.0)
            + weight_up * shifted(right_side, -stride, axis_dim, 0.0)
        )
        low_band = weight_low * shifted(low_band, stride, axis_dim, 0.0)
        up_band = weight_up * shifted(up_band, -stride, axis_dim, 0.0)
        diagonal = new_diag
        right_side = new_right
        stride = stride * 2
    return right_side / diagonal


def top_masked(coupling):
    levels = coupling.shape[0]
    keep = (jnp.arange(levels) < levels - 1)[:, None, None]
    return jnp.where(keep, coupling, jnp.zeros_like(coupling))


def vertical(field, z_low, z_top):
    return z_low * shifted(field, 1, 0, 0.0) + z_top * shifted(field, -1, 0, 0.0)


def restrict(field):
    levels, rows, columns = field.shape
    blocks = field.reshape(levels // 2, 2, rows // 2, 2, columns // 2, 2)
    return jnp.sum(blocks, axis=(1, 3, 5)) * 0.125


def y_rim(field):
    return extended(field, (("gy", 1),), 1)


def x_return(solved):
    return lax.all_to_all(solved, "gx", split_axis=2, concat_axis=0, tiled=True)


def y_return(solved):
    return lax.all_to_all(solved, "gy", split_axis=1, concat_axis=0, tiled=True)


def x_solve(diag_lines, band_lines, source_lines):
    return line_solve(-shifted(band_lines, 1, 2, 0.0), diag_lines, -band_lines, source_lines, 2)


def y_solve(diag_lines, band_lines, source_lines):
    return line_solve(-shifted(band_lines, 1, 1, 0.0), diag_lines, -band_lines, source_lines, 1)


def body(forcing, pressure_in, x_coupling, y_coupling, z_coupling, damping):
    z_top = top_masked(z_coupling)
    z_low = shifted(z_top, 1, 0, 0.0)
    x_left = jnp.concatenate(
        [from_behind(x_coupling[:, :, -1:], "gx", 1), x_coupling[:, :, :-1]], axis=2
    )
    y_left = jnp.concatenate(
        [from_behind(y_coupling[:, -1:, :], "gy", 1), y_coupling[:, :-1, :]], axis=1
    )
    diagonal = x_left + x_coupling + y_left + y_coupling + z_low + z_top + damping
    field = pressure_in
    for repeat in range(2):
        padded = y_rim(field)
        source = (
            forcing
            + y_left * padded[:, :-2, :]
            + y_coupling * padded[:, 2:, :]
            + vertical(field, z_low, z_top)
        )
        source_lines, diag_lines, band_lines = (
            lax.all_to_all(source, "gx", split_axis=0, concat_axis=2, tiled=True),
            lax.all_to_all(diagonal, "gx", split_axis=0, concat_axis=2, tiled=True),
            lax.all_to_all(x_coupling, "gx", split_axis=0, concat_axis=2, tiled=True),
        )
        field = x_return(x_solve(diag_lines, band_lines, source_lines))
        padded = extended(field, (("gx", 2),), 1)
        source = (
            forcing
            + x_left * padded[:, :, :-2]
            + x_coupling * padded[:, :, 2:]
            + vertical(field, z_low, z_top)
        )
        source_lines, diag_lines, band_lines = (
            lax.all_to_all(source, "gy", split_axis=0, concat_axis=1, tiled=True),
            lax.all_to_all(diagonal, "gy", split_axis=0, concat_axis=1, tiled=True),
            lax.all_to_all(y_coupling, "gy", split_axis=0, concat_axis=1, tiled=True),
        )
        field = y_return(y_solve(diag_lines, band_lines, source_lines))
    padded = extended(field, (("gy", 1), ("gx", 2)), 1)
    applied = (
        diagonal * field
        - x_left * padded[:, 1:-1, :-2]
        - x_coupling * padded[:, 1:-1, 2:]
        - y_left * padded[:, :-2, 1:-1]
        - y_coupling * padded[:, 2:, 1:-1]
        - vertical(field, z_low, z_top)
    )
    coarse_residual = restrict(forcing - applied)
    coarse_x = restrict(x_coupling)
    coarse_y = restrict(y_coupling)
    coarse_z = restrict(z_coupling)
    coarse_damp = restrict(damping)
    whole_res, whole_x, whole_y, whole_z, whole_damp = (
        lax.all_gather(coarse_residual, "gx", axis=2, tiled=True),
        lax.all_gather(coarse_x, "gx", axis=2, tiled=True),
        lax.all_gather(coarse_y, "gx", axis=2, tiled=True),
        lax.all_gather(coarse_z, "gx", axis=2, tiled=True),
        lax.all_gather(coarse_damp, "gx", axis=2, tiled=True),
    )
    cz_top = top_masked(whole_z)
    cz_low = shifted(cz_top, 1, 0, 0.0)
    cx_left = shifted(whole_x, 1, 2, 0.0)
    cy_left = jnp.concatenate(
        [from_behind(whole_y[:, -1:, :], "gy", 1), whole_y[:, :-1, :]], axis=1
    )
    coarse_diag = cx_left + whole_x + cy_left + whole_y + cz_low + cz_top + whole_damp
    correction = RELAX * whole_res / coarse_diag
    for repeat in range(COARSE - 1):
        padded = extended(correction, (("gy", 1),), 1)
        applied_coarse = (
            coarse_diag * correction
            - cx_left * shifted(correction, 1, 2, 0.0)
            - whole_x * shifted(correction, -1, 2, 0.0)
            - cy_left * padded[:, :-2, :]
            - whole_y * padded[:, 2:, :]
            - vertical(correction, cz_low, cz_top)
        )
        correction = correction + RELAX * (whole_res - applied_coarse) / coarse_diag
    return (field, coarse_residual, correction)


def solution(mesh):
    in_specs = (
        P(None, "gy", "gx"),
        P(None, "gy", "gx"),
        P(None, "gy", "gx"),
        P(None, "gy", "gx"),
        P(None, "gy", "gx"),
        P(None, "gy", "gx"),
    )
    out_specs = (P(None, "gy", "gx"), P(None, "gy", "gx"), P(None, "gy", None))
    return jax.shard_map(body, mesh=mesh, in_specs=in_specs, out_specs=out_specs, check_vma=False)
```

profile of v0, /device:TPU:4, one launch (start us, length us, event | category | flops | bytes accessed | tf_op | source)
XLA Modules:
  0.0 578.2 jit_solution(13382535518700490269)
XLA Ops:
  0.6 8.1 %all-to-all-start.1 = ((f32[16,16,128]{2,1,0:T(8,128)}), f32[16,16,128]{2,1,0:T(8,128)S(1)}, u32[]{:S(2)}, u32[]{:S(2)}) async-start(f32[16,16,128]{2,1,0:T(8,128)} %param.8), calls=%async_computation.1 | async-start | bytes 262144 | tf_op jit(solution)/shard_map/all_to_all | solution.py:129
  9.6 1.9 collective-permute-start.2
  11.5 4.5 collective-permute-start.3
  16.9 1.9 collective-permute-start.1
  19.9 5.4 collective-permute-start
  27.9 5.8 all-to-all-start.5
  33.7 2.2 add_add_fusion
  35.9 2.0 all-to-all-done.5
  37.9 6.1 %all-to-all-start = ((f32[16,16,128]{2,1,0:T(8,128)}), f32[16,16,128]{2,1,0:T(8,128)S(1)}, u32[]{:S(2)}, u32[]{:S(2)}) async-start(f32[16,16,128]{2,1,0:T(8,128)} %get-tuple-element.88), calls=%async_computation | async-start | bytes 262144 | tf_op jit(solution)/shard_map/all_to_all | solution.py:127
  44.0 9.7 %reshape.65 = f32[8,2,8,2,64,2]{5,4,3,2,1,0:T(8,128)} reshape(f32[16,16,128]{2,1,0:T(8,128)S(1)} %copy-done) | data formatting | bytes 262144 | tf_op jit(solution)/shard_map/reshape | solution.py:83
  53.7 4.0 reduce_sum.47
  57.7 7.2 %all-to-all-start.2 = ((f32[16,16,128]{2,1,0:T(8,128)}), f32[16,16,128]{2,1,0:T(8,128)S(1)}, u32[]{:S(2)}, u32[]{:S(2)}) async-start(f32[16,16,128]{2,1,0:T(8,128)} %get-tuple-element.86), calls=%async_computation.2 | async-start | bytes 262144 | tf_op jit(solution)/shard_map/all_to_all | solution.py:128
  65.1 49.1 %all_gather.17 = f32[8,8,512]{1,0,2:T(8,128)S(1)} all-gather(f32[8,8,64]{1,0,2:T(8,128)S(1)} %copy.197), channel_id=1, replica_groups=mesh['gx'=8,'gy'=16] {'gx'}, dimensions={2}, use_global_device_ids=true | all-gather | bytes 147456 | tf_op jit(solution)/shard_map/all_gather | solution.py:162
  114.2 1.9 slice.1282
  116.1 2.2 copy.198
  118.4 2.5 collective-permute-start.14
  120.8 9.7 %reshape.66 = f32[8,2,8,2,64,2]{5,4,3,2,1,0:T(8,128)} reshape(f32[16,16,128]{2,1,0:T(8,128)S(1)} %copy-done.3) | data formatting | bytes 262144 | tf_op jit(solution)/shard_map/reshape | solution.py:83
  130.5 4.6 reduce_sum.48
  144.5 2.1 copy.176
  146.6 3.3 reshape.68
  149.9 3.7 all-to-all-start.3
  153.6 2.0 slice_negate_fusion.1
  155.5 6.4 %all-to-all-done.3 = f32[8,1,4096]{2,1,0:T(1,128)S(1)} async-done(((f32[8,1,4096]{2,1,0:T(1,128)}), f32[8,1,4096]{2,1,0:T(1,128)S(1)}, u32[]{:S(2)}, u32[]{:S(2)}) %all-to-all-start.3) | async-done | bytes 131104 | tf_op jit(solution)/shard_map/all_to_all | solution.py:92
  161.9 6.2 %all-to-all-start.6 = ((f32[16,16,128]{2,1,0:T(8,128)}), f32[16,16,128]{2,1,0:T(8,128)}, u32[]{:S(2)}, u32[]{:S(2)}) async-start(f32[16,16,128]{2,1,0:T(8,128)} %get-tuple-element.86), calls=%async_computation.6 | async-start | bytes 262144 | tf_op jit(solution)/shard_map/all_to_all | solution.py:141
  170.6 2.4 reshape.69
  174.5 2.7 collective-permute-start.4
  180.3 5.8 %collective-permute-done.5 = f32[16,16,1]{2,1,0:T(8,128)S(1)} collective-permute-done((f32[16,16,1]{2,1,0:T(8,128)S(1)}, f32[16,16,1]{2,1,0:T(8,128)S(1)}, u32[]{:S(2)}, u32[]{:S(2)}) %collective-permute-start.5) | collective-permute-done | bytes 1056 | tf_op jit(solution)/shard_map/ppermute | solution.py:20
  187.7 6.0 %all-to-all-start.4 = ((f32[16,16,128]{2,1,0:T(8,128)}), f32[16,16,128]{2,1,0:T(8,128)S(1)}, u32[]{:S(2)}, u32[]{:S(2)}) async-start(f32[16,16,128]{2,1,0:T(8,128)} %fusion.44), calls=%async_computation.4 | async-start | bytes 262144 | tf_op jit(solution)/shard_map/all_to_all | solution.py:140
  195.4 2.4 all-to-all-done.4
  213.4 5.7 all-to-all-start.7
  220.6 2.7 all-to-all-done.7
  223.3 2.3 collective-permute-start.6
  225.6 4.4 collective-permute-start.7
  232.8 6.6 %all-to-all-start.8 = ((f32[16,16,128]{2,1,0:T(8,128)}), f32[16,16,128]{2,1,0:T(8,128)S(1)}, u32[]{:S(2)}, u32[]{:S(2)}) async-start(f32[16,16,128]{2,1,0:T(8,128)} %fusion.39), calls=%async_computation.8 | async-start | bytes 262144 | tf_op jit(solution)/shard_map/all_to_all | solution.py:127
  239.4 50.2 %all_gather.18 = f32[8,8,512]{1,0,2:T(8,128)} all-gather(f32[8,8,64]{1,0,2:T(8,128)} %copy.202), channel_id=1, replica_groups=mesh['gx'=8,'gy'=16] {'gx'}, dimensions={2}, use_global_device_ids=true | all-gather | bytes 147456 | tf_op jit(solution)/shard_map/all_gather | solution.py:163
  289.6 2.2 copy.203
  299.9 3.3 reshape.70
  303.2 3.9 all-to-all-start.9
  307.8 9.7 %reshape.67 = f32[8,2,8,2,64,2]{5,4,3,2,1,0:T(8,128)} reshape(f32[16,16,128]{2,1,0:T(8,128)S(1)} %copy-done.59) | data formatting | bytes 262144 | tf_op jit(solution)/shard_map/reshape | solution.py:83
  317.5 9.7 %reshape.64 = f32[8,2,8,2,64,2]{5,4,3,2,1,0:T(8,128)} reshape(f32[16,16,128]{2,1,0:T(8,128)S(1)} %copy-done.1) | data formatting | bytes 262144 | tf_op jit(solution)/shard_map/reshape | solution.py:83
  327.2 4.6 reduce_sum.49
  331.8 4.6 reduce_sum.46
  337.4 2.4 reshape.71
  341.3 5.4 collective-permute-start.8
  349.3 5.9 %collective-permute-done.9 = f32[16,16,1]{2,1,0:T(8,128)S(1)} collective-permute-done((f32[16,16,1]{2,1,0:T(8,128)S(1)}, f32[16,16,1]{2,1,0:T(8,128)S(1)}, u32[]{:S(2)}, u32[]{:S(2)}) %collective-permute-start.9) | collective-permute-done | bytes 1056 | tf_op jit(solution)/shard_map/ppermute | solution.py:20
  356.7 5.2 all-to-all-start.10
  363.2 2.8 all-to-all-done.10
  373.2 5.7 all-to-all-start.11
  379.8 47.4 %all_gather.19 = f32[8,8,512]{1,0,2:T(8,128)} all-gather(f32[8,8,64]{1,0,2:T(8,128)} %copy.204), channel_id=1, replica_groups=mesh['gx'=8,'gy'=16] {'gx'}, dimensions={2}, use_global_device_ids=true | all-gather | bytes 147456 | tf_op jit(solution)/shard_map/all_gather | solution.py:164
  427.8 1.9 collective-permute-start.10
  429.7 4.5 collective-permute-start.11
  434.3 46.5 %all_gather.16 = f32[8,8,512]{1,0,2:T(8,128)} all-gather(f32[8,8,64]{1,0,2:T(8,128)S(1)} %copy.194), channel_id=1, replica_groups=mesh['gx'=8,'gy'=16] {'gx'}, dimensions={2}, use_global_device_ids=true | all-gather | bytes 147456 | tf_op jit(solution)/shard_map/all_gather | solution.py:161
  481.5 2.3 copy.205
  486.8 2.1 collective-permute-start.12
  492.0 5.9 %collective-permute-done.13 = f32[16,18,1]{2,1,0:T(8,128)S(1)} collective-permute-done((f32[16,18,1]{2,1,0:T(8,128)S(1)}, f32[16,18,1]{2,1,0:T(8,128)S(1)}, u32[]{:S(2)}, u32[]{:S(2)}) %collective-permute-start.13) | collective-permute-done | bytes 1184 | tf_op jit(solution)/shard_map/ppermute | solution.py:20
  499.2 9.7 %reshape.63 = f32[8,2,8,2,64,2]{5,4,3,2,1,0:T(8,128)} reshape(f32[16,16,128]{2,1,0:T(8,128)S(1)} %fusion.25) | data formatting | bytes 262144 | tf_op jit(solution)/shard_map/reshape | solution.py:83
  508.9 4.0 reduce_sum.45
  513.1 45.9 %all_gather.15 = f32[8,8,512]{1,0,2:T(8,128)S(1)} all-gather(f32[8,8,64]{1,0,2:T(8,128)S(1)} %copy.192), channel_id=1, replica_groups=mesh['gx'=8,'gy'=16] {'gx'}, dimensions={2}, use_global_device_ids=true | all-gather | bytes 147456 | tf_op jit(solution)/shard_map/all_gather | solution.py:160
  560.0 1.9 collective-permute-start.16
  561.9 2.4 collective-permute-start.15
  564.4 3.5 collective-permute-done.15
  568.3 1.9 collective-permute-start.18
  570.3 2.4 collective-permute-start.17
  572.7 3.5 collective-permute-done.17
  (433 shorter events, 79.7 us)
Async XLA Ops:
  0.6 43.4 %copy-start = (f32[16,16,128]{2,1,0:T(8,128)S(1)}, f32[16,16,128]{2,1,0:T(8,128)}, u32[]{:S(2)}) copy-start(f32[16,16,128]{2,1,0:T(8,128)} %param.9) | copy-start | bytes 393220
  0.6 27.3 %all-to-all-start.1 = ((f32[16,16,128]{2,1,0:T(8,128)}), f32[16,16,128]{2,1,0:T(8,128)S(1)}, u32[]{:S(2)}, u32[]{:S(2)}) async-start(f32[16,16,128]{2,1,0:T(8,128)} %param.8), calls=%async_computation.1 | async-start | bytes 262144 | tf_op jit(solution)/shard_map/all_to_all | solution.py:129
  9.6 24.1 %collective-permute-start.2 = (f32[16,1,128]{2,1,0:T(1,128)S(1)}, f32[16,1,128]{2,1,0:T(1,128)S(1)}, u32[]{:S(2)}, u32[]{:S(2)}) collective-permute-start(f32[16,1,128]{2,1,0:T(1,128)S(1)} %get-tuple-element.305), channel_id=1, source_target_pairs={{0,1},{1,2},{2,3},{3,4},{4,5},{5,6},{6,7},{7,8},{8,9},{9,10},{10,1... | collective-permute-start | bytes 24584 | tf_op jit(solution)/shard_map/ppermute | solution.py:19
  11.5 22.2 %collective-permute-start.3 = (f32[16,1,128]{2,1,0:T(1,128)S(1)}, f32[16,1,128]{2,1,0:T(1,128)S(1)}, u32[]{:S(2)}, u32[]{:S(2)}) collective-permute-start(f32[16,1,128]{2,1,0:T(1,128)S(1)} %get-tuple-element.306), channel_id=1, source_target_pairs={{1,0},{2,1},{3,2},{4,3},{5,4},{6,5},{7,6},{8,7},{9,8},{10,9},{11,1... | collective-permute-start | bytes 24584 | tf_op jit(solution)/shard_map/ppermute | solution.py:20
  16.9 16.8 %collective-permute-start.1 = (f32[16,1,128]{2,1,0:T(1,128)S(1)}, f32[16,1,128]{2,1,0:T(1,128)S(1)}, u32[]{:S(2)}, u32[]{:S(2)}) collective-permute-start(f32[16,1,128]{2,1,0:T(1,128)S(1)} %slice.847), channel_id=1, source_target_pairs={{0,1},{1,2},{2,3},{3,4},{4,5},{5,6},{6,7},{7,8},{8,9},{9,10},{10,1... | collective-permute-start | bytes 24584 | tf_op jit(solution)/shard_map/ppermute | solution.py:28
  19.9 13.8 %collective-permute-start = (f32[16,16,1]{2,1,0:T(8,128)S(1)}, f32[16,16,1]{2,1,0:T(8,128)S(1)}, u32[]{:S(2)}, u32[]{:S(2)}) collective-permute-start(f32[16,16,1]{2,1,0:T(8,128)S(1)} %slice.845), channel_id=1, source_target_pairs={{0,16},{16,32},{32,48},{48,64},{64,80},{80,96},{96,112},{1,17},{17... | collective-permute-start | bytes 3080 | tf_op jit(solution)/shard_map/ppermute | solution.py:28
  27.9 10.0 %all-to-all-start.5 = ((f32[16,16,128]{2,1,0:T(8,128)}), f32[16,16,128]{2,1,0:T(8,128)S(1)}, u32[]{:S(2)}, u32[]{:S(2)}) async-start(f32[16,16,128]{2,1,0:T(8,128)} %param.9), calls=%async_computation.5 | async-start | bytes 262144 | tf_op jit(solution)/shard_map/all_to_all | solution.py:142
  37.9 97.3 %copy-start.72 = (f32[16,16,128]{2,1,0:T(8,128)}, f32[16,16,128]{2,1,0:T(8,128)S(1)}, u32[]{:S(2)}) copy-start(f32[16,16,128]{2,1,0:T(8,128)S(1)} %all-to-all-done.5) | copy-start | bytes 393220
  37.9 19.8 %all-to-all-start = ((f32[16,16,128]{2,1,0:T(8,128)}), f32[16,16,128]{2,1,0:T(8,128)S(1)}, u32[]{:S(2)}, u32[]{:S(2)}) async-start(f32[16,16,128]{2,1,0:T(8,128)} %get-tuple-element.88), calls=%async_computation | async-start | bytes 262144 | tf_op jit(solution)/shard_map/all_to_all | solution.py:127
  57.7 78.4 %all-to-all-start.2 = ((f32[16,16,128]{2,1,0:T(8,128)}), f32[16,16,128]{2,1,0:T(8,128)S(1)}, u32[]{:S(2)}, u32[]{:S(2)}) async-start(f32[16,16,128]{2,1,0:T(8,128)} %get-tuple-element.86), calls=%async_computation.2 | async-start | bytes 262144 | tf_op jit(solution)/shard_map/all_to_all | solution.py:128
  116.1 4.7 copy-start.3
  118.4 366.8 %collective-permute-start.14 = (f32[8,1,512]{2,0,1:T(8,128)S(1)}, f32[8,1,512]{2,0,1:T(8,128)}, u32[]{:S(2)}, u32[]{:S(2)}) collective-permute-start(f32[8,1,512]{2,0,1:T(8,128)S(1)} %copy.198), channel_id=1, source_target_pairs={{0,1},{1,2},{2,3},{3,4},{4,5},{5,6},{6,7},{7,8},{8,9},{9,10},{10,1... | collective-permute-start | bytes 49160 | tf_op jit(solution)/shard_map/ppermute | solution.py:28
  141.8 2.7 copy-start.39
  141.8 2.7 copy-start.51
  142.3 7.6 %copy-start.45 = (f32[2,16,1024]{2,1,0:T(8,128)}, f32[2,16,1024]{2,1,0:T(8,128)S(1)}, u32[]{:S(2)}) copy-start(f32[2,16,1024]{2,1,0:T(8,128)S(1)} %get-tuple-element.46) | copy-start | bytes 393220
  149.9 12.1 %all-to-all-start.3 = ((f32[8,1,4096]{2,1,0:T(1,128)}), f32[8,1,4096]{2,1,0:T(1,128)S(1)}, u32[]{:S(2)}, u32[]{:S(2)}) async-start(f32[8,1,4096]{2,1,0:T(1,128)} %reshape.68), calls=%async_computation.3 | async-start | bytes 262144 | tf_op jit(solution)/shard_map/all_to_all | solution.py:92
  153.5 32.5 %copy-start.1 = (f32[16,16,128]{2,1,0:T(8,128)S(1)}, f32[16,16,128]{2,1,0:T(8,128)}, u32[]{:S(2)}) copy-start(f32[16,16,128]{2,1,0:T(8,128)} %param.8) | copy-start | bytes 393220
  153.6 32.5 %copy-start.4 = (f32[16,16,128]{2,1,0:T(8,128)S(1)}, f32[16,16,128]{2,1,0:T(8,128)}, u32[]{:S(2)}) copy-start(f32[16,16,128]{2,1,0:T(8,128)} %param.6) | copy-start | bytes 393220
  153.6 32.5 %copy-start.17 = (f32[16,16,128]{2,1,0:T(8,128)S(1)}, f32[16,16,128]{2,1,0:T(8,128)}, u32[]{:S(2)}) copy-start(f32[16,16,128]{2,1,0:T(8,128)} %get-tuple-element.87) | copy-start | bytes 393220
  161.9 6.2 %copy-start.89 = (f32[8,1,4096]{2,1,0:T(1,128)}, f32[8,1,4096]{2,1,0:T(1,128)S(1)}, u32[]{:S(2)}) copy-start(f32[8,1,4096]{2,1,0:T(1,128)S(1)} %all-to-all-done.3) | copy-start | bytes 393220
  161.9 25.7 %all-to-all-start.6 = ((f32[16,16,128]{2,1,0:T(8,128)}), f32[16,16,128]{2,1,0:T(8,128)}, u32[]{:S(2)}, u32[]{:S(2)}) async-start(f32[16,16,128]{2,1,0:T(8,128)} %get-tuple-element.86), calls=%async_computation.6 | async-start | bytes 262144 | tf_op jit(solution)/shard_map/all_to_all | solution.py:141
  174.5 5.8 %collective-permute-start.4 = (f32[16,16,1]{2,1,0:T(8,128)S(1)}, f32[16,16,1]{2,1,0:T(8,128)S(1)}, u32[]{:S(2)}, u32[]{:S(2)}) collective-permute-start(f32[16,16,1]{2,1,0:T(8,128)S(1)} %get-tuple-element.218), channel_id=1, source_target_pairs={{0,16},{16,32},{32,48},{48,64},{64,80},{80,96},{96,112},{1,17},{17... | collective-permute-start | bytes 3080 | tf_op jit(solution)/shard_map/ppermute | solution.py:19
  177.2 8.9 %collective-permute-start.5 = (f32[16,16,1]{2,1,0:T(8,128)S(1)}, f32[16,16,1]{2,1,0:T(8,128)S(1)}, u32[]{:S(2)}, u32[]{:S(2)}) collective-permute-start(f32[16,16,1]{2,1,0:T(8,128)S(1)} %get-tuple-element.219), channel_id=1, source_target_pairs={{16,0},{32,16},{48,32},{64,48},{80,64},{96,80},{112,96},{17,1},{33... | collective-permute-start | bytes 3080 | tf_op jit(solution)/shard_map/ppermute | solution.py:20
  187.7 10.1 %all-to-all-start.4 = ((f32[16,16,128]{2,1,0:T(8,128)}), f32[16,16,128]{2,1,0:T(8,128)S(1)}, u32[]{:S(2)}, u32[]{:S(2)}) async-start(f32[16,16,128]{2,1,0:T(8,128)} %fusion.44), calls=%async_computation.4 | async-start | bytes 262144 | tf_op jit(solution)/shard_map/all_to_all | solution.py:140
  197.8 4.1 copy-start.90
  200.2 2.4 copy-start.34
  200.2 2.4 copy-start.36
  210.3 3.1 copy-start.43
  210.9 2.5 copy-start.47
  213.4 9.9 %all-to-all-start.7 = ((f32[1,256,128]{2,0,1:T(1,128)}), f32[1,256,128]{2,0,1:T(1,128)S(1)}, u32[]{:S(2)}, u32[]{:S(2)}) async-start(f32[1,256,128]{2,0,1:T(1,128)} %add_divide_fusion.2), calls=%async_computation.7 | async-start | bytes 262144 | tf_op jit(solution)/shard_map/all_to_all | solution.py:96
  223.3 6.8 %collective-permute-start.6 = (f32[16,1,128]{2,1,0:T(1,128)S(1)}, f32[16,1,128]{2,1,0:T(1,128)S(1)}, u32[]{:S(2)}, u32[]{:S(2)}) collective-permute-start(f32[16,1,128]{2,1,0:T(1,128)S(1)} %get-tuple-element.149), channel_id=1, source_target_pairs={{0,1},{1,2},{2,3},{3,4},{4,5},{5,6},{6,7},{7,8},{8,9},{9,10},{10,1... | collective-permute-start | bytes 24584 | tf_op jit(solution)/shard_map/ppermute | solution.py:19
  225.6 5.7 collective-permute-start.7
  232.8 59.6 %all-to-all-start.8 = ((f32[16,16,128]{2,1,0:T(8,128)}), f32[16,16,128]{2,1,0:T(8,128)S(1)}, u32[]{:S(2)}, u32[]{:S(2)}) async-start(f32[16,16,128]{2,1,0:T(8,128)} %fusion.39), calls=%async_computation.8 | async-start | bytes 262144 | tf_op jit(solution)/shard_map/all_to_all | solution.py:127
  294.8 1.8 copy-start.6
  298.2 8.9 %copy-start.95 = (pred[8]{0:T(512)(128)(4,1)S(1)}, pred[8]{0:T(512)(128)(4,1)}, u32[]{:S(2)}) copy-start(pred[8]{0:T(512)(128)(4,1)} %iota_compare_fusion) | copy-start | bytes 28
  298.2 9.6 %copy-start.59 = (f32[16,16,128]{2,1,0:T(8,128)S(1)}, f32[16,16,128]{2,1,0:T(8,128)}, u32[]{:S(2)}) copy-start(f32[16,16,128]{2,1,0:T(8,128)} %param.11) | copy-start | bytes 393220
  303.2 33.3 %all-to-all-start.9 = ((f32[8,1,4096]{2,1,0:T(1,128)}), f32[8,1,4096]{2,1,0:T(1,128)S(1)}, u32[]{:S(2)}, u32[]{:S(2)}) async-start(f32[8,1,4096]{2,1,0:T(1,128)} %reshape.70), calls=%async_computation.9 | async-start | bytes 262144 | tf_op jit(solution)/shard_map/all_to_all | solution.py:92
  336.4 18.7 %copy-start.18 = (f32[16,16,128]{2,1,0:T(8,128)S(1)}, f32[16,16,128]{2,1,0:T(8,128)}, u32[]{:S(2)}) copy-start(f32[16,16,128]{2,1,0:T(8,128)} %get-tuple-element.87) | copy-start | bytes 393220
  339.8 26.3 %copy-start.35 = (f32[1,256,128]{2,0,1:T(1,128)S(1)}, f32[1,256,128]{2,0,1:T(1,128)}, u32[]{:S(2)}) copy-start(f32[1,256,128]{2,0,1:T(1,128)} %copy-done.34) | copy-start | bytes 393220
  341.3 7.9 %collective-permute-start.8 = (f32[16,16,1]{2,1,0:T(8,128)S(1)}, f32[16,16,1]{2,1,0:T(8,128)S(1)}, u32[]{:S(2)}, u32[]{:S(2)}) collective-permute-start(f32[16,16,1]{2,1,0:T(8,128)S(1)} %get-tuple-element.125), channel_id=1, source_target_pairs={{0,16},{16,32},{32,48},{48,64},{64,80},{80,96},{96,112},{1,17},{17... | collective-permute-start | bytes 3080 | tf_op jit(solution)/shard_map/ppermute | solution.py:19
  346.8 8.4 %collective-permute-start.9 = (f32[16,16,1]{2,1,0:T(8,128)S(1)}, f32[16,16,1]{2,1,0:T(8,128)S(1)}, u32[]{:S(2)}, u32[]{:S(2)}) collective-permute-start(f32[16,16,1]{2,1,0:T(8,128)S(1)} %get-tuple-element.126), channel_id=1, source_target_pairs={{16,0},{32,16},{48,32},{64,48},{80,64},{96,80},{112,96},{17,1},{33... | collective-permute-start | bytes 3080 | tf_op jit(solution)/shard_map/ppermute | solution.py:20
  356.7 9.3 %all-to-all-start.10 = ((f32[16,16,128]{2,1,0:T(8,128)}), f32[16,16,128]{2,1,0:T(8,128)S(1)}, u32[]{:S(2)}, u32[]{:S(2)}) async-start(f32[16,16,128]{2,1,0:T(8,128)} %fusion.34), calls=%async_computation.10 | async-start | bytes 262144 | tf_op jit(solution)/shard_map/all_to_all | solution.py:140
  366.0 4.3 copy-start.28
  366.0 4.3 copy-start.30
  367.3 3.5 copy-start.33
  367.3 3.5 copy-start.67
  368.7 2.5 copy-start.24
  368.7 2.5 copy-start.65
  371.1 7.7 %copy-start.92 = (f32[8,8,64]{2,1,0:T(8,128)S(1)}, f32[8,8,64]{2,1,0:T(8,128)}, u32[]{:S(2)}) copy-start(f32[8,8,64]{2,1,0:T(8,128)} %reduce_sum.46) | copy-start | bytes 49156
  371.1 7.7 %copy-start.94 = (f32[8,8,64]{2,1,0:T(8,128)S(1)}, f32[8,8,64]{2,1,0:T(8,128)}, u32[]{:S(2)}) copy-start(f32[8,8,64]{2,1,0:T(8,128)} %broadcast_multiply_fusion) | copy-start | bytes 49156
  373.2 54.0 %all-to-all-start.11 = ((f32[1,256,128]{2,0,1:T(1,128)}), f32[1,256,128]{2,0,1:T(1,128)S(1)}, u32[]{:S(2)}, u32[]{:S(2)}) async-start(f32[1,256,128]{2,0,1:T(1,128)} %add_divide_fusion), calls=%async_computation.11 | async-start | bytes 262144 | tf_op jit(solution)/shard_map/all_to_all | solution.py:96
  427.8 58.1 %collective-permute-start.10 = (f32[16,1,128]{2,1,0:T(1,128)}, f32[16,1,128]{2,1,0:T(1,128)}, u32[]{:S(2)}, u32[]{:S(2)}) collective-permute-start(f32[16,1,128]{2,1,0:T(1,128)} %get-tuple-element.105), channel_id=1, source_target_pairs={{0,1},{1,2},{2,3},{3,4},{4,5},{5,6},{6,7},{7,8},{8,9},{9,10},{10,1... | collective-permute-start | bytes 24584 | tf_op jit(solution)/shard_map/ppermute | solution.py:19
  429.7 56.2 %collective-permute-start.11 = (f32[16,1,128]{2,1,0:T(1,128)}, f32[16,1,128]{2,1,0:T(1,128)}, u32[]{:S(2)}, u32[]{:S(2)}) collective-permute-start(f32[16,1,128]{2,1,0:T(1,128)} %get-tuple-element.106), channel_id=1, source_target_pairs={{1,0},{2,1},{3,2},{4,3},{5,4},{6,5},{7,6},{8,7},{9,8},{10,9},{11,1... | collective-permute-start | bytes 24584 | tf_op jit(solution)/shard_map/ppermute | solution.py:20
  480.8 3.0 copy-start.91
  481.5 3.0 copy-start.2
  486.8 5.2 collective-permute-start.12
  488.9 9.1 %collective-permute-start.13 = (f32[16,18,1]{2,1,0:T(8,128)S(1)}, f32[16,18,1]{2,1,0:T(8,128)S(1)}, u32[]{:S(2)}, u32[]{:S(2)}) collective-permute-start(f32[16,18,1]{2,1,0:T(8,128)S(1)} %get-tuple-element.90), channel_id=1, source_target_pairs={{16,0},{32,16},{48,32},{64,48},{80,64},{96,80},{112,96},{17,1},{33... | collective-permute-start | bytes 3464 | tf_op jit(solution)/shard_map/ppermute | solution.py:20
  512.9 46.8 %copy-start.93 = (f32[8,8,64]{2,1,0:T(8,128)}, f32[8,8,64]{2,1,0:T(8,128)S(1)}, u32[]{:S(2)}) copy-start(f32[8,8,64]{2,1,0:T(8,128)S(1)} %broadcast_multiply_fusion.4) | copy-start | bytes 49156
  513.1 46.6 %copy-start.50 = (f32[7,8,512]{2,1,0:T(8,128)S(1)}, f32[7,8,512]{2,1,0:T(8,128)}, u32[]{:S(2)}) copy-start(f32[7,8,512]{2,1,0:T(8,128)} %slice.1284) | copy-start | bytes 344068
  513.1 46.6 %copy-start.96 = (pred[8]{0:T(512)(128)(4,1)S(1)}, pred[8]{0:T(512)(128)(4,1)}, u32[]{:S(2)}) copy-start(pred[8]{0:T(512)(128)(4,1)} %iota_compare_fusion) | copy-start | bytes 28
  560.0 4.4 collective-permute-start.16
  561.9 6.0 %collective-permute-start.15 = (f32[8,1,512]{2,0,1:T(8,128)S(1)}, f32[8,1,512]{2,0,1:T(8,128)S(1)}, u32[]{:S(2)}, u32[]{:S(2)}) collective-permute-start(f32[8,1,512]{2,0,1:T(8,128)S(1)} %copy.207), channel_id=1, source_target_pairs={{0,1},{1,2},{2,3},{3,4},{4,5},{5,6},{6,7},{7,8},{8,9},{9,10},{10,1... | collective-permute-start | bytes 49160 | tf_op jit(solution)/shard_map/ppermute | solution.py:19
  568.3 4.4 collective-permute-start.18
  570.3 6.0 %collective-permute-start.17 = (f32[8,1,512]{2,0,1:T(8,128)S(1)}, f32[8,1,512]{2,0,1:T(8,128)S(1)}, u32[]{:S(2)}, u32[]{:S(2)}) collective-permute-start(f32[8,1,512]{2,0,1:T(8,128)S(1)} %copy.214), channel_id=1, source_target_pairs={{0,1},{1,2},{2,3},{3,4},{4,5},{5,6},{6,7},{7,8},{8,9},{9,10},{10,1... | collective-permute-start | bytes 49160 | tf_op jit(solution)/shard_map/ppermute | solution.py:19
  (64 other events, 67.2 us)
where the time goes:
time: 585 us; the launch traced here: 578 us
  blocking collectives  239 us (41%)
  starting transfers between devices  122 us (21%)
  local copies, waits for them, and re-layouts  103 us (18%)
  other arithmetic  63.3 us (11%)
  waiting for transfers between devices  46.7 us (8%)
    all_gather x1, blocking collectives, body(): lax.all_gather(coarse_z, 'gx', axis=2, tiled=True)  50.2 us
    all_gather x1, blocking collectives, body(): lax.all_gather(coarse_y, 'gx', axis=2, tiled=True)  49.1 us
    reshape x5, local copies, waits for them, and re-layouts, restrict(): blocks = field.reshape(levels // 2, 2, rows // 2, 2, columns // 2, 2)  48.4 us
    all_gather x1, blocking collectives, body(): lax.all_gather(coarse_damp, 'gx', axis=2, tiled=True)  47.4 us
    all_gather x1, blocking collectives, body(): lax.all_gather(coarse_x, 'gx', axis=2, tiled=True)  46.5 us
    all_gather x1, blocking collectives, body(): lax.all_gather(coarse_residual, 'gx', axis=2, tiled=True)  45.9 us
    reduce_sum x5, other arithmetic, restrict(): return jnp.sum(blocks, axis=(1, 3, 5)) * 0.125  21.9 us
    ppermute x8, starting transfers between devices, extended(): after = lax.ppermute(leading, axis, down)  21.2 us
  transfers between devices with their start and end apart: 31, of which 14 were waited for; matrix products, arithmetic and copies ran while one was open for 24% of the time, Pallas kernels for 0%

commit v1 on v0

v1 whole, which is shorter than its diff:
```python
import functools

import jax
import jax.numpy as jnp
from jax import lax
from jax.experimental import pallas as pl
from jax.experimental.pallas import tpu as pltpu
from jax.sharding import PartitionSpec as P

RELAX = 0.8
NK, NJ, NI = 16, 16, 128
ROWS = NK * NJ
GX, GY = 8, 16
STEPS = (1, 2, 4, 8, 16, 32, 64)
F32 = jnp.float32


def sds(*shape):
    return jax.ShapeDtypeStruct(shape, F32)


def call(kernel, outs, *args, scratch=()):
    spec = pl.BlockSpec(memory_space=pltpu.VMEM)
    return pl.pallas_call(
        kernel,
        out_shape=outs,
        in_specs=[spec] * len(args),
        out_specs=[spec] * len(outs),
        scratch_shapes=[pltpu.VMEM(s, F32) for s in scratch],
        compiler_params=pltpu.CompilerParams(vmem_limit_bytes=16 * 1024 * 1024),
    )(*args)


def lanes(rows, width=NI):
    return lax.broadcasted_iota(jnp.int32, (rows, width), 1)


def rolled(value, amount, axis):
    return pltpu.roll(value, amount % value.shape[axis], axis)


def level(ref, k):
    return ref[pl.ds(k * NJ, NJ), :]


def across(ref, j, count=NK, stride=NJ):
    return ref[pl.ds(j, count, stride=stride), :]


def column(value, k):
    return jnp.broadcast_to(value[:, k : k + 1], (value.shape[0], NI))


def z_pair(zc, k):
    return (level(zc, k - 1) if k > 0 else None, level(zc, k) if k < NK - 1 else None)


def z_sum(zc, k, base):
    low, top = z_pair(zc, k)
    if low is not None:
        base = base + low
    if top is not None:
        base = base + top
    return base


def z_terms(zc, field, k, base):
    low, top = z_pair(zc, k)
    if low is not None:
        base = base + low * level(field, k - 1)
    if top is not None:
        base = base + top * level(field, k + 1)
    return base


def y_left_of(yc, halo, k):
    row = lax.broadcasted_iota(jnp.int32, (NJ, NI), 0)
    return jnp.where(row == 0, halo[pl.ds(k, 1), :], rolled(level(yc, k), 1, 0))


def squeeze(values, scale=0.125):
    source = lax.broadcasted_iota(jnp.int32, (NI, NI), 0)
    target = lax.broadcasted_iota(jnp.int32, (NI, NI), 1)
    matrix = jnp.where(source // 2 == target, scale, 0.0).astype(F32)
    return jnp.dot(values, matrix, precision=lax.Precision.HIGHEST, preferred_element_type=F32)


def edges(values, scale=0.125):
    source = lax.broadcasted_iota(jnp.int32, (NI, NI), 0)
    target = lax.broadcasted_iota(jnp.int32, (NI, NI), 1)
    hit = ((source == NI - 1) & (target == 64)) | ((source == 0) & (target == NI - 1))
    matrix = jnp.where(hit, scale, 0.0).astype(F32)
    return jnp.dot(values, matrix, precision=lax.Precision.HIGHEST, preferred_element_type=F32)


def parity_shift(values):
    odd = lax.rem(lax.axis_index("gx"), 2) == 1
    return jnp.where(odd, rolled(values, 64, 1), values)


def store_coarse(out, base, tmp):
    for J in range(NJ // 2):
        out[pl.ds(base + J * 8, 8), :] = across(tmp, 2 * J, 8) + across(tmp, 2 * J + 1, 8)


def first_kernel(p, xc, yc, zc, dp, up, down, coarse, tmp):
    up[pl.ds(0, NK), :] = across(yc, NJ - 1)
    up[pl.ds(NK, NK), :] = across(p, NJ - 1)
    down[pl.ds(0, NK), :] = across(p, 0)
    for q, ref in enumerate((xc, yc, zc, dp)):
        pairs = jnp.concatenate([level(ref, 2 * K) + level(ref, 2 * K + 1) for K in range(NK // 2)], axis=0)
        tmp[...] = parity_shift(squeeze(pairs))
        store_coarse(coarse, q * 64, tmp)
        up[pl.ds(2 * NK + q * 24, 24), :] = coarse[pl.ds(q * 64 + 40, 24), :]
        down[pl.ds(NK + q * 16, 16), :] = coarse[pl.ds(q * 64, 16), :]


def x_first_kernel(f, p, xc, yc, zc, dp, below, above, g, a, b, mult, send):
    d = lax.axis_index("gx")
    lane = lanes(NJ)
    row = lax.broadcasted_iota(jnp.int32, (NJ, NI), 0)
    inner = jnp.logical_or(lane < NI - 1, d == GX - 1)
    packed = jnp.zeros((NJ, NI), F32)
    group = 2
    for k0 in range(0, NK, group):
        diag, off, rhs = [], [], []
        for k in range(k0, k0 + group):
            x, y, v = level(xc, k), level(yc, k), level(p, k)
            y_left = y_left_of(yc, below, k)
            before = jnp.where(row == 0, below[pl.ds(NK + k, 1), :], rolled(v, 1, 0))
            after = jnp.where(row == NJ - 1, above[pl.ds(k, 1), :], rolled(v, -1, 0))
            rest = z_sum(zc, k, y_left + y + level(dp, k))
            x_left = jnp.where(lane == 0, 0.0, rolled(x, 1, 1))
            diag.append(x_left + jnp.where(inner, x, 0.0) + rest)
            off.append(jnp.where(lane == NI - 1, 0.0, -x))
            rhs.append(z_terms(zc, p, k, level(f, k) + y_left * before + y * after))
        diag, off, rhs = (jnp.concatenate(v, axis=0) for v in (diag, off, rhs))
        wide = lanes(group * NJ)
        left = jnp.where(wide == 0, 1.0, 0.0).astype(F32)
        right = jnp.where(wide == NI - 1, 1.0, 0.0).astype(F32)
        place = pl.ds(k0 * NJ, group * NJ)
        for n, s in enumerate(STEPS):
            inv = 1.0 / diag
            low = rolled(off, s, 1)
            alpha = -low * rolled(inv, s, 1)
            beta = -off * rolled(inv, -s, 1)
            mult[2 * n, place, :] = alpha
            mult[2 * n + 1, place, :] = beta
            diag = diag + alpha * low + beta * off
            off = beta * rolled(off, -s, 1)
            rhs = rhs + alpha * rolled(rhs, s, 1) + beta * rolled(rhs, -s, 1)
            left = left + alpha * rolled(left, s, 1) + beta * rolled(left, -s, 1)
            right = right + alpha * rolled(right, s, 1) + beta * rolled(right, -s, 1)
        inv = 1.0 / diag
        mult[2 * len(STEPS), place, :] = inv
        rhs, left, right = rhs * inv, left * inv, right * inv
        g[place, :], a[place, :], b[place, :] = rhs, left, right
        for k in range(k0, k0 + group):
            part = slice((k - k0) * NJ, (k - k0 + 1) * NJ)
            picks = (
                column(rhs[part], 0),
                column(rhs[part], NI - 1),
                column(left[part], 0),
                column(right[part], 0),
                column(right[part], NI - 1),
                column(level(xc, k), NI - 1),
            )
            for q, pick in enumerate(picks):
                packed = jnp.where(lane == q * NK + k, pick, packed)
    send[...] = packed


def x_second_solve(rhs, mult, place):
    for n, s in enumerate(STEPS):
        rhs = rhs + mult[2 * n, place, :] * rolled(rhs, s, 1) + mult[2 * n + 1, place, :] * rolled(rhs, -s, 1)
    return rhs * mult[2 * len(STEPS), place, :]


def x_fluxes(fs, source, low, inv, up):
    zero = jnp.zeros((NJ, NI), F32)
    fs[0], fs[GX] = zero, zero
    forward = [source(0)]
    for d in range(1, GX - 1):
        forward.append(source(d) + low[d] * forward[-1])
    value = forward[-1] * inv[GX - 2]
    fs[GX - 1] = value
    for d in range(GX - 3, -1, -1):
        value = forward[d] * inv[d] + up[d] * value
        fs[1 + d] = value


def x_finish(fs, g, a, b, field):
    d = lax.axis_index("gx")
    flux_left, flux_right = fs[d], fs[d + 1]
    for k in range(NK):
        field[pl.ds(k * NJ, NJ), :] = (
            level(g, k) - level(a, k) * column(flux_left, k) + level(b, k) * column(flux_right, k)
        )
    return flux_left, flux_right


def y_source(f, xc, zc, field, fluxes, c_left, k):
    d = lax.axis_index("gx")
    lane = lanes(NJ)
    flux_left, flux_right = fluxes
    v, x = level(field, k), level(xc, k)
    before = jnp.where(lane == 0, column(c_left, k) * v - column(flux_left, k), rolled(x * v, 1, 1))
    last = jnp.where(d == GX - 1, 0.0, x * v + column(flux_right, k))
    after = jnp.where(lane == NI - 1, last, x * rolled(v, -1, 1))
    return z_terms(zc, field, k, level(f, k) + before + after)


def y_first_kernel(f, xc, yc, zc, dp, below, got, g, a, b, yg, ya, yb, yw, yinv, xred, cl, send, fs, cs, field, src, base):
    d = lax.axis_index("gx")
    e = lax.axis_index("gy")
    lane = lanes(NJ)
    part = lambda n, q: rolled(got[n], -NK * q, 1)
    m = [part(n, 3) for n in range(GX)]
    low, inv, up = [None], [], []
    for n in range(GX - 1):
        dd = part(n, 4) + 1.0 / part(n, 5) + part(n + 1, 2)
        if n:
            low.append(m[n] * inv[-1])
            dd = dd - low[n] * m[n]
        inv.append(1.0 / dd)
        up.append(m[n + 1] * inv[n])
        xred[n], xred[GX + n], xred[2 * GX + n] = (low[n] if n else jnp.zeros_like(dd)), inv[n], up[n]
    x_fluxes(fs, lambda n: part(n + 1, 0) - part(n, 1), low, inv, up)
    cs[0] = jnp.zeros((NJ, NI), F32)
    for n in range(GX):
        cs[n + 1] = part(n, 5)
    c_left = cs[d]
    cl[...] = c_left
    fluxes = x_finish(fs, g, a, b, field)
    for k in range(NK):
        src[pl.ds(k * NJ, NJ), :] = y_source(f, xc, zc, field, fluxes, c_left, k)
        x = level(xc, k)
        x_left = jnp.where(lane == 0, column(c_left, k), rolled(x, 1, 1))
        base[pl.ds(k * NJ, NJ), :] = z_sum(zc, k, x_left + x + level(dp, k))
    ys, ws, invs, spike = [], [None], [], []
    for j in range(NJ):
        y = across(yc, j)
        diag = across(base, j)
        if j < NJ - 1:
            diag = diag + y
        else:
            diag = diag + jnp.where(e == GY - 1, y, 0.0)
        rhs = across(src, j)
        if j:
            y_before = across(yc, j - 1)
            w = y_before * invs[-1]
            ws.append(w)
            diag = diag + y_before - w * y_before
            rhs = rhs + w * ys[-1]
            spike.append(w * spike[-1])
            yw[pl.ds(j * NK, NK), :] = w
        else:
            spike.append(jnp.ones((NK, NI), F32))
            yw[pl.ds(0, NK), :] = jnp.zeros((NK, NI), F32)
        ys.append(rhs)
        invs.append(1.0 / diag)
        yinv[pl.ds(j * NK, NK), :] = invs[-1]
    for j in range(NJ - 1, -1, -1):
        if j == NJ - 1:
            gv, av, bv = ys[j] * invs[j], spike[j] * invs[j], invs[j]
            send[pl.ds(NK, NK), :] = gv
            send[pl.ds(4 * NK, NK), :] = bv + 1.0 / across(yc, j)
        else:
            w = ws[j + 1]
            gv, av, bv = ys[j] * invs[j] + w * gv, spike[j] * invs[j] + w * av, w * bv
        place = pl.ds(j * NK, NK)
        yg[place, :], ya[place, :], yb[place, :] = gv, av, bv
    send[pl.ds(0, NK), :] = gv
    send[pl.ds(2 * NK, NK), :] = av
    send[pl.ds(3 * NK, NK), :] = bv


def y_fluxes(fs, source, low, inv, up):
    zero = jnp.zeros((NK, NI), F32)
    fs[0], fs[GY] = zero, zero
    forward = [source(0)]
    for n in range(1, GY - 1):
        forward.append(source(n) + low(n) * forward[-1])
    value = forward[-1] * inv(GY - 2)
    fs[GY - 1] = value
    for n in range(GY - 3, -1, -1):
        value = forward[n] * inv(n) + up(n) * value
        fs[1 + n] = value


def y_finish(fs, yc, below, yg, ya, yb, field, terms):
    e = lax.axis_index("gy")
    flux_left, flux_right = fs[e], fs[e + 1]
    block = lambda ref, j: ref[pl.ds(j * NK, NK), :]
    p = [block(yg, j) - block(ya, j) * flux_left + block(yb, j) * flux_right for j in range(NJ)]
    for j in range(NJ):
        y = across(yc, j)
        if j:
            before = across(yc, j - 1) * p[j - 1]
        else:
            before = below[pl.ds(0, NK), :] * p[0] - flux_left
        if j < NJ - 1:
            after = y * p[j + 1]
        else:
            after = jnp.where(e == GY - 1, 0.0, y * p[j] + flux_right)
        field[pl.ds(j, NK, stride=NJ), :] = p[j]
        terms[pl.ds(j, NK, stride=NJ), :] = before + after


def x_again_kernel(f, yc, zc, below, got, yg, ya, yb, mult, g, yred, send, fs, field, terms):
    part = lambda n, q: got[n, pl.ds(q * NK, NK), :]
    prev = None
    for n in range(GY - 1):
        dd = part(n, 4) + part(n + 1, 2)
        if n:
            m = part(n, 3)
            low = m * prev
            dd = dd - low * m
            yred[n] = low
        else:
            yred[n] = jnp.zeros_like(dd)
        prev = 1.0 / dd
        yred[GY + n] = prev
        yred[2 * GY + n] = part(n + 1, 3) * prev
    yred[GY - 1] = jnp.zeros((NK, NI), F32)
    yred[2 * GY - 1] = jnp.zeros((NK, NI), F32)
    yred[3 * GY - 1] = jnp.zeros((NK, NI), F32)
    y_fluxes(
        fs,
        lambda n: part(n + 1, 0) - part(n, 1),
        lambda n: yred[n],
        lambda n: yred[GY + n],
        lambda n: yred[2 * GY + n],
    )
    y_finish(fs, yc, below, yg, ya, yb, field, terms)
    lane = lanes(NJ)
    packed = jnp.zeros((NJ, NI), F32)
    group = 2
    for k0 in range(0, NK, group):
        rhs = jnp.concatenate(
            [z_terms(zc, field, k, level(f, k) + level(terms, k)) for k in range(k0, k0 + group)], axis=0
        )
        place = pl.ds(k0 * NJ, group * NJ)
        rhs = x_second_solve(rhs, mult, place)
        g[place, :] = rhs
        for k in range(k0, k0 + group):
            mine = rhs[(k - k0) * NJ : (k - k0 + 1) * NJ]
            packed = jnp.where(lane == k, column(mine, 0), packed)
            packed = jnp.where(lane == NK + k, column(mine, NI - 1), packed)
    send[...] = packed


def y_again_kernel(f, xc, zc, got, g, a, b, xred, cl, yw, yinv, yg, send, fs, field, src):
    part = lambda n, q: rolled(got[n], -NK * q, 1)
    x_fluxes(
        fs,
        lambda n: part(n + 1, 0) - part(n, 1),
        [xred[n] for n in range(GX - 1)],
        [xred[GX + n] for n in range(GX - 1)],
        [xred[2 * GX + n] for n in range(GX - 1)],
    )
    fluxes = x_finish(fs, g, a, b, field)
    c_left = cl[...]
    for k in range(NK):
        src[pl.ds(k * NJ, NJ), :] = y_source(f, xc, zc, field, fluxes, c_left, k)
    block = lambda ref, j: ref[pl.ds(j * NK, NK), :]
    ys = []
    for j in range(NJ):
        rhs = across(src, j)
        if j:
            rhs = rhs + block(yw, j) * ys[-1]
        ys.append(rhs)
    value = None
    for j in range(NJ - 1, -1, -1):
        new = ys[j] * block(yinv, j)
        value = new if value is None else new + block(yw, j + 1) * value
        yg[pl.ds(j * NK, NK), :] = value
        if j == NJ - 1:
            send[pl.ds(NK, NK), :] = value
    send[pl.ds(0, NK), :] = value


def residual_kernel(f, xc, yc, zc, dp, below, got, yg, ya, yb, yred, cl, field, coarse, fs, terms, tmp):
    d = lax.axis_index("gx")
    lane = lanes(NJ)
    part = lambda n, q: got[n, pl.ds(q * NK, NK), :]
    y_fluxes(
        fs,
        lambda n: part(n + 1, 0) - part(n, 1),
        lambda n: yred[n],
        lambda n: yred[GY + n],
        lambda n: yred[2 * GY + n],
    )
    y_finish(fs, yc, below, yg, ya, yb, field, terms)
    c_left = cl[...]
    main, rim = [], []
    for k in range(NK):
        v, x = level(field, k), level(xc, k)
        left = column(c_left, k)
        x_left = jnp.where(lane == 0, left, rolled(x, 1, 1))
        diag = z_sum(zc, k, x_left + x + y_left_of(yc, below, k) + level(yc, k) + level(dp, k))
        around = jnp.where(lane == 0, 0.0, x_left * rolled(v, 1, 1)) + jnp.where(lane == NI - 1, 0.0, x * rolled(v, -1, 1))
        main.append(level(f, k) - (diag * v - around - level(terms, k) - z_terms(zc, field, k, jnp.zeros((NJ, NI), F32))))
        last = jnp.where(d == GX - 1, 0.0, x * v)
        rim.append(jnp.where(lane == 0, left * v, jnp.where(lane == NI - 1, last, 0.0)))
    pairs = jnp.concatenate([main[2 * K] + main[2 * K + 1] for K in range(NK // 2)], axis=0)
    outer = jnp.concatenate([rim[2 * K] + rim[2 * K + 1] for K in range(NK // 2)], axis=0)
    tmp[...] = parity_shift(squeeze(pairs) + edges(outer))
    store_coarse(coarse, 0, tmp)


def coarse_kernel(got, coef, res_out, cor_out, tmp, cor_tmp):
    d = lax.axis_index("gx")
    e = lax.axis_index("gy")
    lane = lanes(8)
    wide = lanes(8, 4 * NI)
    level_k = lax.broadcasted_iota(jnp.int32, (8, 4 * NI), 0)

    def whole_res(J):
        rows = pl.ds(J * 8, 8)
        outs = []
        for m in range(4):
            value = jnp.where(lane <= 64, got[2 * m, rows, :], 0.0) + jnp.where(lane >= 63, got[2 * m + 1, rows, :], 0.0)
            if m > 0:
                value = value + jnp.where(lane == 0, got[2 * m - 1, rows, :], 0.0)
            if m < 3:
                value = value + jnp.where(lane == NI - 1, got[2 * m + 2, rows, :], 0.0)
            outs.append(value)
        return outs

    def whole_coef(q, J):
        rows = pl.ds(q * 104 + J * 8, 8)
        return jnp.concatenate([coef[2 * m, rows, :] + coef[2 * m + 1, rows, :] for m in range(4)], axis=1)

    res, diag, weight, cxl, cxi, cyl, cyr, czl, czt = ([] for _ in range(9))
    for J in range(12):
        outs = whole_res(J)
        if 2 <= J < 10:
            mine = outs[0]
            for m in range(1, 4):
                mine = jnp.where(d // 2 == m, outs[m], mine)
            mine = jnp.where(lax.rem(d, 2) == 1, rolled(mine, 64, 1), mine)
            tmp[pl.ds(J - 2, 8, stride=8), :] = mine
        res.append(jnp.concatenate(outs, axis=1))
        x, y, z, damp = (whole_coef(q, J + 1) for q in range(4))
        y_before = whole_coef(1, J)
        x_left = jnp.where(wide == 0, 0.0, rolled(x, 1, 1))
        z_top = jnp.where(level_k == 7, 0.0, z)
        z_low = rolled(z_top, 1, 0)
        total = x_left + x + y_before + y + z_low + z_top + damp
        at = e * 8 + J - 2
        valid = jnp.logical_and(at >= 0, at < 8 * GY)
        total = jnp.where(valid, total, 1.0)
        diag.append(total)
        weight.append(jnp.where(valid, RELAX / total, 0.0))
        cxl.append(x_left)
        cxi.append(jnp.where(wide == 4 * NI - 1, 0.0, x))
        cyl.append(y_before)
        cyr.append(y)
        czl.append(z_low)
        czt.append(z_top)
    cor = {J: weight[J] * res[J] for J in range(12)}
    for low, high in ((1, 11), (2, 10)):
        new = {}
        for J in range(low, high):
            v = cor[J]
            applied = (
                diag[J] * v
                - cxl[J] * rolled(v, 1, 1)
                - cxi[J] * rolled(v, -1, 1)
                - cyl[J] * cor[J - 1]
                - cyr[J] * cor[J + 1]
                - (czl[J] * rolled(v, 1, 0) + czt[J] * rolled(v, -1, 0))
            )
            new[J] = v + weight[J] * (res[J] - applied)
        cor = new
    for J in range(8):
        for m in range(4):
            cor_tmp[m, pl.ds(J, 8, stride=8), :] = cor[J + 2][:, m * NI : (m + 1) * NI]
    for m in range(4):
        cor_out[:, pl.ds(m * NI, NI)] = cor_tmp[m]
    res_out[...] = tmp[:, :64]


def spread(value, axis, count):
    many = jnp.broadcast_to(value[None], (count,) + value.shape)
    return lax.all_to_all(many, axis, split_axis=0, concat_axis=0, tiled=True)


def body(forcing, pressure_in, x_coupling, y_coupling, z_coupling, damping):
    f, p, xc, yc, zc, dp = (
        v.reshape(ROWS, NI) for v in (forcing, pressure_in, x_coupling, y_coupling, z_coupling, damping)
    )
    forth = [(n, n + 1) for n in range(GY - 1)]
    back = [(n + 1, n) for n in range(GY - 1)]
    whole = sds(ROWS, NI)
    up, down, coef = call(first_kernel, [sds(128, NI), sds(80, NI), sds(256, NI)], p, xc, yc, zc, dp, scratch=[(128, NI)])
    below = lax.ppermute(up, "gy", forth)
    above = lax.ppermute(down, "gy", back)
    g, a, b, mult, send = call(
        x_first_kernel,
        [whole, whole, whole, sds(2 * len(STEPS) + 1, ROWS, NI), sds(NJ, NI)],
        f, p, xc, yc, zc, dp, below, above,
    )
    got = spread(send, "gx", GX)
    coef_rows = jnp.concatenate(
        [below[32:].reshape(4, 24, NI), coef.reshape(4, 64, NI), above[16:].reshape(4, 16, NI)], axis=1
    ).reshape(416, NI)
    coef_all = lax.all_gather(coef_rows, "gx", axis=0, tiled=False)
    yg, ya, yb, yw, yinv, xred, cl, send = call(
        y_first_kernel,
        [whole] * 5 + [sds(3 * GX, NJ, NI), sds(NJ, NI), sds(5 * NK, NI)],
        f, xc, yc, zc, dp, below, got, g, a, b,
        scratch=[(GX + 1, NJ, NI), (GX + 1, NJ, NI), (ROWS, NI), (ROWS, NI), (ROWS, NI)],
    )
    got = spread(send, "gy", GY)
    g, yred, send = call(
        x_again_kernel,
        [whole, sds(3 * GY, NK, NI), sds(NJ, NI)],
        f, yc, zc, below, got, yg, ya, yb, mult,
        scratch=[(GY + 1, NK, NI), (ROWS, NI), (ROWS, NI)],
    )
    got = spread(send, "gx", GX)
    yg, send = call(
        y_again_kernel,
        [whole, sds(2 * NK, NI)],
        f, xc, zc, got, g, a, b, xred, cl, yw, yinv,
        scratch=[(GX + 1, NJ, NI), (ROWS, NI), (ROWS, NI)],
    )
    got = spread(send, "gy", GY)
    field, coarse = call(
        residual_kernel,
        [whole, sds(64, NI)],
        f, xc, yc, zc, dp, below, got, yg, ya, yb, yred, cl,
        scratch=[(GY + 1, NK, NI), (ROWS, NI), (128, NI)],
    )
    lower = lax.ppermute(coarse[48:], "gy", forth)
    upper = lax.ppermute(coarse[:16], "gy", back)
    got = spread(jnp.concatenate([lower, coarse, upper], axis=0), "gx", GX)
    res, cor = call(
        coarse_kernel, [sds(64, 64), sds(64, 512)], got, coef_all, scratch=[(64, NI), (4, 64, NI)]
    )
    return field.reshape(NK, NJ, NI), res.reshape(8, 8, 64), cor.reshape(8, 8, 512)


def solution(mesh):
    spec = P(None, "gy", "gx")
    return jax.shard_map(
        body, mesh=mesh, in_specs=(spec,) * 6, out_specs=(spec, spec, P(None, "gy", None)), check_vma=False
    )
```

time: 585 us -> 119 us (0.20)
  the two profiles are of different devices: /device:TPU:4 before, /device:TPU:1 now
where the time goes in v1:
time: 119 us
  blocking collectives  65.2 us (55%)
  between operations  14.2 us (12%)
  local copies, waits for them, and re-layouts  11.5 us (10%)
  starting transfers between devices  11.1 us (9%)
  Pallas kernels  9.63 us (8%)
  waiting for transfers between devices  6.45 us (5%)
    all_to_all x5, blocking collectives, spread(): return lax.all_to_all(many, axis, split_axis=0, concat_axis=0, tiled=True)  65.2 us
    unnamed x32, local copies, waits for them, and re-layouts  11.4 us
    pallas_call x7, Pallas kernels, call(): pl.pallas_call(kernel, out_shape=outs, in_specs=[spec] * len(args), out_s...  9.63 us
    ppermute x1, starting transfers between devices, body(): below = lax.ppermute(up, 'gy', forth)  4.59 us
    ppermute x1, waiting for transfers between devices, body(): above = lax.ppermute(down, 'gy', back)  3.39 us
    ppermute x1, waiting for transfers between devices, body(): upper = lax.ppermute(coarse[:16], 'gy', back)  3.03 us
    ppermute x1, starting transfers between devices, body(): lower = lax.ppermute(coarse[48:], 'gy', forth)  2.62 us
  transfers between devices with their start and end apart: 5, of which 2 were waited for; matrix products, arithmetic and copies ran while one was open for 0% of the time, Pallas kernels for 7%

profile of v1, /device:TPU:1, one launch (start us, length us, event | category | flops | bytes accessed | tf_op | source)
XLA Modules:
  0.0 118.7 jit_solution(1765022654889494169)
XLA Ops:
  7.2 0.0 all-gather.2.cloned.1.call-start
  7.2 0.0 copy-start
  7.2 0.9 copy-done
  8.1 0.0 copy-start.3
  8.1 0.9 copy-done.3
  9.0 0.0 copy-start.8
  9.0 0.9 copy-done.8
  9.9 0.0 copy-start.10
  9.9 0.9 copy-done.10
  10.8 0.0 copy-start.14
  10.8 0.9 copy-done.14
  11.7 0.0 copy-start.2
  11.7 0.0 copy-start.5
  11.7 0.0 copy-start.7
  11.7 0.5 shard_map.85
  12.3 4.6 %collective-permute-start = (f32[128,128]{1,0:T(8,128)S(1)}, f32[128,128]{1,0:T(8,128)S(1)}, u32[]{:S(2)}, u32[]{:S(2)}) collective-permute-start(f32[128,128]{1,0:T(8,128)S(1)} %get-tuple-element.28), channel_id=1, source_target_pairs={{0,1},{1,2},{2,3},{3,4},{4,5},{5,6},{6,7},{7,8},{8,9},{9,10},{10,1... | collective-permute-start | bytes 196616 | tf_op jit(solution)/shard_map/ppermute | solution.py:498
  16.9 1.9 %collective-permute-start.1 = (f32[80,128]{1,0:T(8,128)S(1)}, f32[80,128]{1,0:T(8,128)S(1)}, u32[]{:S(2)}, u32[]{:S(2)}) collective-permute-start(f32[80,128]{1,0:T(8,128)S(1)} %get-tuple-element.29), channel_id=1, source_target_pairs={{1,0},{2,1},{3,2},{4,3},{5,4},{6,5},{7,6},{8,7},{9,8},{10,9},{11,1... | collective-permute-start | bytes 122888 | tf_op jit(solution)/shard_map/ppermute | solution.py:499
  18.8 3.4 %collective-permute-done.1.above = f32[80,128]{1,0:T(8,128)S(1)} collective-permute-done((f32[80,128]{1,0:T(8,128)S(1)}, f32[80,128]{1,0:T(8,128)S(1)}, u32[]{:S(2)}, u32[]{:S(2)}) %collective-permute-start.1) | collective-permute-done | bytes 40992 | tf_op jit(solution)/shard_map/ppermute | solution.py:499
  22.2 0.0 collective-permute-done.below
  22.2 0.7 pad_maximum_fusion
  22.9 0.0 all-gather.2.cloned.1.call-update
  22.9 0.0 copy-start.1
  22.9 0.9 copy-done.1
  23.8 0.0 copy-start.4
  23.8 0.9 copy-done.4
  24.7 0.0 copy-start.6
  24.7 0.9 copy-done.6
  25.6 0.0 copy-start.9
  25.6 0.9 copy-done.9
  26.5 0.0 copy-start.11
  26.5 0.9 copy-done.11
  27.4 0.0 copy-start.15
  27.5 0.9 copy-done.15
  28.4 5.0 %shard_map.86 = (f32[256,128]{1,0:T(8,128)S(1)}, f32[256,128]{1,0:T(8,128)S(1)}, f32[256,128]{1,0:T(8,128)S(1)}, f32[15,256,128]{2,1,0:T(8,128)S(1)}, f32[16,128]{1,0:T(8,128)S(1)}) custom-call(f32[256,128]{1,0:T(8,128)S(1)} %bitcast.24, f32[256,128]{1,0:T(8,128)S(1)} %bitcast.39, f32[256,128]{1,0:T(8,128)S(1)} %bitcast.20, f32[256,128]{1,0:T(8,128)S(1)} %bitcast.30, ...), custom_call_target="tpu_custom_call" | custom-call | tf_op jit(solution)/shard_map/pallas_call | solution.py:24
  33.3 13.9 %all_to_all.25.got = f32[8,16,128]{2,1,0:T(8,128)S(1)} all-to-all(f32[8,16,128]{2,1,0:T(8,128)S(1)} %broadcast_in_dim.10), channel_id=1, replica_groups=mesh['gx'=8,'gy'=16] {'gx'}, dimensions={0} | all-to-all | bytes 131072 | tf_op jit(solution)/shard_map/all_to_all | solution.py:487
  47.3 0.0 copy-done.2
  47.3 0.0 copy-done.5
  47.3 0.0 copy-done.7
  47.3 0.6 shard_map.87
  48.0 17.3 %all_to_all.26.got = f32[16,80,128]{2,1,0:T(8,128)S(1)} all-to-all(f32[16,80,128]{2,1,0:T(8,128)S(1)} %broadcast_in_dim.11), channel_id=1, replica_groups=mesh['gx'=8,'gy'=16] {'gy'}, dimensions={0} | all-to-all | bytes 1310720 | tf_op jit(solution)/shard_map/all_to_all | solution.py:487
  65.3 1.0 shard_map.88
  66.3 0.0 copy-start.12
  66.3 9.4 %all_to_all.27.got = f32[8,16,128]{2,1,0:T(8,128)S(1)} all-to-all(f32[8,16,128]{2,1,0:T(8,128)S(1)} %broadcast_in_dim.12), channel_id=1, replica_groups=mesh['gx'=8,'gy'=16] {'gx'}, dimensions={0} | all-to-all | bytes 131072 | tf_op jit(solution)/shard_map/all_to_all | solution.py:487
  75.7 0.5 shard_map.89
  76.2 12.1 %all_to_all.28.got = f32[16,32,128]{2,1,0:T(8,128)S(1)} all-to-all(f32[16,32,128]{2,1,0:T(8,128)S(1)} %broadcast_in_dim.13), channel_id=1, replica_groups=mesh['gx'=8,'gy'=16] {'gy'}, dimensions={0} | all-to-all | bytes 524288 | tf_op jit(solution)/shard_map/all_to_all | solution.py:487
  88.3 0.0 copy-done.12
  88.3 1.0 shard_map.90
  89.3 2.6 %collective-permute-start.2 = (f32[16,128]{1,0:T(8,128)S(1)}, f32[16,128]{1,0:T(8,128)S(1)}, u32[]{:S(2)}, u32[]{:S(2)}) collective-permute-start(f32[16,128]{1,0:T(8,128)S(1)} %get-tuple-element.53), channel_id=1, source_target_pairs={{0,1},{1,2},{2,3},{3,4},{4,5},{5,6},{6,7},{7,8},{8,9},{9,10},{10,1... | collective-permute-start | bytes 24584 | tf_op jit(solution)/shard_map/ppermute | solution.py:537
  91.9 1.9 %collective-permute-start.3 = (f32[16,128]{1,0:T(8,128)S(1)}, f32[16,128]{1,0:T(8,128)S(1)}, u32[]{:S(2)}, u32[]{:S(2)}) collective-permute-start(f32[16,128]{1,0:T(8,128)S(1)} %get-tuple-element.54), channel_id=1, source_target_pairs={{1,0},{2,1},{3,2},{4,3},{5,4},{6,5},{7,6},{8,7},{9,8},{10,9},{11,1... | collective-permute-start | bytes 24584 | tf_op jit(solution)/shard_map/ppermute | solution.py:538
  93.8 0.0 collective-permute-done.2
  93.8 3.0 %collective-permute-done.3 = f32[16,128]{1,0:T(8,128)S(1)} collective-permute-done((f32[16,128]{1,0:T(8,128)S(1)}, f32[16,128]{1,0:T(8,128)S(1)}, u32[]{:S(2)}, u32[]{:S(2)}) %collective-permute-start.3) | collective-permute-done | bytes 8224 | tf_op jit(solution)/shard_map/ppermute | solution.py:538
  96.9 12.4 %all_to_all.29.got = f32[8,96,128]{2,1,0:T(8,128)S(1)} all-to-all(f32[8,96,128]{2,1,0:T(8,128)S(1)} %broadcast_in_dim.14), channel_id=1, replica_groups=mesh['gx'=8,'gy'=16] {'gx'}, dimensions={0} | all-to-all | bytes 786432 | tf_op jit(solution)/shard_map/all_to_all | solution.py:487
  109.3 0.0 all-gather.2.cloned.1.call-done.coef
  109.3 0.0 copy-start.13
  109.3 1.5 %copy-done.13 = f32[8,416,128]{2,1,0:T(8,128)S(1)} copy-done((f32[8,416,128]{2,1,0:T(8,128)S(1)}, f32[8,416,128]{2,1,0:T(8,128)}, u32[]{:S(2)}) %copy-start.13) | copy-done | bytes 1703960
  110.8 1.1 shard_map.91
  (9 shorter events, 0.1 us)
Async XLA Ops:
  7.2 102.2 %all-gather.2.cloned.1.call-start = ((), (), s32[]{:S(2)}) async-start(), calls=%async_computation.5 | async-start | bytes 1916928 | tf_op jit(solution)/shard_map/all_gather | solution.py:509
  7.2 0.9 copy-start
  8.1 0.9 copy-start.3
  9.0 0.9 copy-start.8
  9.9 0.9 copy-start.10
  10.8 0.9 copy-start.14
  11.7 35.5 %copy-start.2 = (f32[16,16,128]{2,1,0:T(8,128)S(1)}, f32[16,16,128]{2,1,0:T(8,128)}, u32[]{:S(2)}) copy-start(f32[16,16,128]{2,1,0:T(8,128)} %param.10) | copy-start | bytes 393220
  11.7 35.5 %copy-start.5 = (f32[16,16,128]{2,1,0:T(8,128)S(1)}, f32[16,16,128]{2,1,0:T(8,128)}, u32[]{:S(2)}) copy-start(f32[16,16,128]{2,1,0:T(8,128)} %param.8) | copy-start | bytes 393220
  11.7 35.5 %copy-start.7 = (f32[16,16,128]{2,1,0:T(8,128)S(1)}, f32[16,16,128]{2,1,0:T(8,128)}, u32[]{:S(2)}) copy-start(f32[16,16,128]{2,1,0:T(8,128)} %param.6) | copy-start | bytes 393220
  12.3 9.9 %collective-permute-start = (f32[128,128]{1,0:T(8,128)S(1)}, f32[128,128]{1,0:T(8,128)S(1)}, u32[]{:S(2)}, u32[]{:S(2)}) collective-permute-start(f32[128,128]{1,0:T(8,128)S(1)} %get-tuple-element.28), channel_id=1, source_target_pairs={{0,1},{1,2},{2,3},{3,4},{4,5},{5,6},{6,7},{7,8},{8,9},{9,10},{10,1... | collective-permute-start | bytes 196616 | tf_op jit(solution)/shard_map/ppermute | solution.py:498
  16.9 5.3 %collective-permute-start.1 = (f32[80,128]{1,0:T(8,128)S(1)}, f32[80,128]{1,0:T(8,128)S(1)}, u32[]{:S(2)}, u32[]{:S(2)}) collective-permute-start(f32[80,128]{1,0:T(8,128)S(1)} %get-tuple-element.29), channel_id=1, source_target_pairs={{1,0},{2,1},{3,2},{4,3},{5,4},{6,5},{7,6},{8,7},{9,8},{10,9},{11,1... | collective-permute-start | bytes 122888 | tf_op jit(solution)/shard_map/ppermute | solution.py:499
  22.9 0.9 copy-start.1
  23.8 0.9 copy-start.4
  24.7 0.9 copy-start.6
  25.6 0.9 copy-start.9
  26.5 0.9 copy-start.11
  27.4 0.9 copy-start.15
  66.3 22.0 %copy-start.12 = (f32[16,16,128]{2,1,0:T(8,128)S(1)}, f32[16,16,128]{2,1,0:T(8,128)}, u32[]{:S(2)}) copy-start(f32[16,16,128]{2,1,0:T(8,128)} %param.11) | copy-start | bytes 393220
  89.3 4.6 %collective-permute-start.2 = (f32[16,128]{1,0:T(8,128)S(1)}, f32[16,128]{1,0:T(8,128)S(1)}, u32[]{:S(2)}, u32[]{:S(2)}) collective-permute-start(f32[16,128]{1,0:T(8,128)S(1)} %get-tuple-element.53), channel_id=1, source_target_pairs={{0,1},{1,2},{2,3},{3,4},{4,5},{5,6},{6,7},{7,8},{8,9},{9,10},{10,1... | collective-permute-start | bytes 24584 | tf_op jit(solution)/shard_map/ppermute | solution.py:537
  91.9 5.0 %collective-permute-start.3 = (f32[16,128]{1,0:T(8,128)S(1)}, f32[16,128]{1,0:T(8,128)S(1)}, u32[]{:S(2)}, u32[]{:S(2)}) collective-permute-start(f32[16,128]{1,0:T(8,128)S(1)} %get-tuple-element.54), channel_id=1, source_target_pairs={{1,0},{2,1},{3,2},{4,3},{5,4},{6,5},{7,6},{8,7},{9,8},{10,9},{11,1... | collective-permute-start | bytes 24584 | tf_op jit(solution)/shard_map/ppermute | solution.py:538
  109.3 1.5 %copy-start.13 = (f32[8,416,128]{2,1,0:T(8,128)S(1)}, f32[8,416,128]{2,1,0:T(8,128)}, u32[]{:S(2)}) copy-start(f32[8,416,128]{2,1,0:T(8,128)} %all-gather.2.cloned.1.call-done.coef) | copy-start | bytes 5111812
Sparse Core Ops, SparseCore 0:
  23.0 55.7 all-gather.1

commit v2 on v1

--- a/solution.py
+++ b/solution.py
@@ -19,16 +19,27 @@
     return jax.ShapeDtypeStruct(shape, F32)
 
 
-def call(kernel, outs, *args, scratch=()):
+def call(kernel, outs, *args, scratch=(), hbm=False, aliases={}, sems=0, flops=None):
     spec = pl.BlockSpec(memory_space=pltpu.VMEM)
+    inside = pl.BlockSpec(memory_space=pltpu.HBM) if hbm else spec
+    shapes = [pltpu.VMEM(v, F32) for v in scratch]
+    if sems:
+        shapes.append(pltpu.SemaphoreType.DMA((sems,)))
+    cost = None if flops is None else pl.CostEstimate(flops=flops, bytes_accessed=1 << 20, transcendentals=0)
     return pl.pallas_call(
         kernel,
         out_shape=outs,
-        in_specs=[spec] * len(args),
+        in_specs=[inside] * len(args),
         out_specs=[spec] * len(outs),
-        scratch_shapes=[pltpu.VMEM(s, F32) for s in scratch],
-        compiler_params=pltpu.CompilerParams(vmem_limit_bytes=16 * 1024 * 1024),
+        scratch_shapes=shapes,
+        input_output_aliases=aliases,
+        cost_estimate=cost,
+        compiler_params=pltpu.CompilerParams(vmem_limit_bytes=(58 if hbm else 16) * 1024 * 1024),
     )(*args)
+
+
+def parts(xs):
+    return [xs.at[pl.ds(n * ROWS, ROWS), :] for n in range(6)]
 
 
 def lanes(rows, width=NI):
@@ -78,10 +89,10 @@
     return jnp.where(row == 0, halo[pl.ds(k, 1), :], rolled(level(yc, k), 1, 0))
 
 
-def squeeze(values, scale=0.125):
+def squeeze(values, scale=0.125, start=0):
     source = lax.broadcasted_iota(jnp.int32, (NI, NI), 0)
     target = lax.broadcasted_iota(jnp.int32, (NI, NI), 1)
-    matrix = jnp.where(source // 2 == target, scale, 0.0).astype(F32)
+    matrix = jnp.where(source // 2 + start == target, scale, 0.0).astype(F32)
     return jnp.dot(values, matrix, precision=lax.Precision.HIGHEST, preferred_element_type=F32)
 
 
@@ -103,77 +114,144 @@
         out[pl.ds(base + J * 8, 8), :] = across(tmp, 2 * J, 8) + across(tmp, 2 * J + 1, 8)
 
 
-def first_kernel(p, xc, yc, zc, dp, up, down, coarse, tmp):
+def first_kernel(fh, ph, xh, yh, zh, dh, xs, up, down, coarse, tmp, sems):
+    order = (3, 1, 2, 4, 5, 0)
+    copies = {
+        n: pltpu.make_async_copy(ref, xs.at[pl.ds(n * ROWS, ROWS), :], sems.at[n])
+        for n, ref in enumerate((fh, ph, xh, yh, zh, dh))
+    }
+    for n in order:
+        copies[n].start()
+    f, p, xc, yc, zc, dp = parts(xs)
+    for n in order:
+        copies[n].wait()
     up[pl.ds(0, NK), :] = across(yc, NJ - 1)
     up[pl.ds(NK, NK), :] = across(p, NJ - 1)
     down[pl.ds(0, NK), :] = across(p, 0)
-    for q, ref in enumerate((xc, yc, zc, dp)):
-        pairs = jnp.concatenate([level(ref, 2 * K) + level(ref, 2 * K + 1) for K in range(NK // 2)], axis=0)
-        tmp[...] = parity_shift(squeeze(pairs))
+    for q, two in enumerate(((xc, yc), (zc, dp))):
+        total = jnp.zeros((128, NI), F32)
+        for half, ref in enumerate(two):
+            pairs = jnp.concatenate([level(ref, 2 * K) + level(ref, 2 * K + 1) for K in range(NK // 2)], axis=0)
+            total = total + squeeze(pairs, start=64 * half)
+        tmp[...] = total
         store_coarse(coarse, q * 64, tmp)
         up[pl.ds(2 * NK + q * 24, 24), :] = coarse[pl.ds(q * 64 + 40, 24), :]
         down[pl.ds(NK + q * 16, 16), :] = coarse[pl.ds(q * 64, 16), :]
 
 
-def x_first_kernel(f, p, xc, yc, zc, dp, below, above, g, a, b, mult, send):
+def x_matrix(x, rest):
     d = lax.axis_index("gx")
+    lane = lanes(x.shape[0])
+    inner = jnp.logical_or(lane < NI - 1, d == GX - 1)
+    diag = jnp.where(lane == 0, 0.0, rolled(x, 1, 1)) + jnp.where(inner, x, 0.0) + rest
+    return diag, jnp.where(lane == NI - 1, 0.0, -x)
+
+
+def x_eliminate(diag, off, rhs, keep):
+    wide = lanes(diag.shape[0])
+    left = jnp.where(wide == 0, 1.0, 0.0).astype(F32)
+    right = jnp.where(wide == NI - 1, 1.0, 0.0).astype(F32)
+    for n, s in enumerate(STEPS):
+        inv = 1.0 / diag
+        low = rolled(off, s, 1)
+        alpha = -low * rolled(inv, s, 1)
+        beta = -off * rolled(inv, -s, 1)
+        keep(2 * n, alpha)
+        keep(2 * n + 1, beta)
+        diag = diag + alpha * low + beta * off
+        off = beta * rolled(off, -s, 1)
+        rhs = rhs + alpha * rolled(rhs, s, 1) + beta * rolled(rhs, -s, 1)
+        left = left + alpha * rolled(left, s, 1) + beta * rolled(left, -s, 1)
+        right = right + alpha * rolled(right, s, 1) + beta * rolled(right, -s, 1)
+    inv = 1.0 / diag
+    keep(2 * len(STEPS), inv)
+    return rhs * inv, left * inv, right * inv
+
+
+def x_picks(g, a, b, x):
+    return column(g, 0), column(g, NI - 1), column(a, 0), column(b, 0), column(b, NI - 1), column(x, NI - 1)
+
+
+def x_first_kernel(xs, g, a, b, mult, packed_out):
+    f, p, xc, yc, zc, dp = parts(xs)
     lane = lanes(NJ)
     row = lax.broadcasted_iota(jnp.int32, (NJ, NI), 0)
-    inner = jnp.logical_or(lane < NI - 1, d == GX - 1)
     packed = jnp.zeros((NJ, NI), F32)
     group = 2
     for k0 in range(0, NK, group):
         diag, off, rhs = [], [], []
         for k in range(k0, k0 + group):
-            x, y, v = level(xc, k), level(yc, k), level(p, k)
-            y_left = y_left_of(yc, below, k)
-            before = jnp.where(row == 0, below[pl.ds(NK + k, 1), :], rolled(v, 1, 0))
-            after = jnp.where(row == NJ - 1, above[pl.ds(k, 1), :], rolled(v, -1, 0))
-            rest = z_sum(zc, k, y_left + y + level(dp, k))
-            x_left = jnp.where(lane == 0, 0.0, rolled(x, 1, 1))
-            diag.append(x_left + jnp.where(inner, x, 0.0) + rest)
-            off.append(jnp.where(lane == NI - 1, 0.0, -x))
-            rhs.append(z_terms(zc, p, k, level(f, k) + y_left * before + y * after))
+            y, v = level(yc, k), level(p, k)
+            y_left = jnp.where(row == 0, 0.0, rolled(y, 1, 0))
+            matrix = x_matrix(level(xc, k), z_sum(zc, k, y_left + y + level(dp, k)))
+            diag.append(matrix[0])
+            off.append(matrix[1])
+            after = jnp.where(row == NJ - 1, 0.0, rolled(v, -1, 0))
+            rhs.append(z_terms(zc, p, k, level(f, k) + y_left * rolled(v, 1, 0) + y * after))
         diag, off, rhs = (jnp.concatenate(v, axis=0) for v in (diag, off, rhs))
-        wide = lanes(group * NJ)
-        left = jnp.where(wide == 0, 1.0, 0.0).astype(F32)
-        right = jnp.where(wide == NI - 1, 1.0, 0.0).astype(F32)
         place = pl.ds(k0 * NJ, group * NJ)
-        for n, s in enumerate(STEPS):
-            inv = 1.0 / diag
-            low = rolled(off, s, 1)
-            alpha = -low * rolled(inv, s, 1)
-            beta = -off * rolled(inv, -s, 1)
-            mult[2 * n, place, :] = alpha
-            mult[2 * n + 1, place, :] = beta
-            diag = diag + alpha * low + beta * off
-            off = beta * rolled(off, -s, 1)
-            rhs = rhs + alpha * rolled(rhs, s, 1) + beta * rolled(rhs, -s, 1)
-            left = left + alpha * rolled(left, s, 1) + beta * rolled(left, -s, 1)
-            right = right + alpha * rolled(right, s, 1) + beta * rolled(right, -s, 1)
-        inv = 1.0 / diag
-        mult[2 * len(STEPS), place, :] = inv
-        rhs, left, right = rhs * inv, left * inv, right * inv
+
+        def keep(n, value):
+            mult[pl.ds(n * ROWS + k0 * NJ, group * NJ), :] = value
+
+        rhs, left, right = x_eliminate(diag, off, rhs, keep)
         g[place, :], a[place, :], b[place, :] = rhs, left, right
         for k in range(k0, k0 + group):
             part = slice((k - k0) * NJ, (k - k0 + 1) * NJ)
-            picks = (
-                column(rhs[part], 0),
-                column(rhs[part], NI - 1),
-                column(left[part], 0),
-                column(right[part], 0),
-                column(right[part], NI - 1),
-                column(level(xc, k), NI - 1),
-            )
-            for q, pick in enumerate(picks):
+            for q, pick in enumerate(x_picks(rhs[part], left[part], right[part], level(xc, k))):
                 packed = jnp.where(lane == q * NK + k, pick, packed)
-    send[...] = packed
-
-
-def x_second_solve(rhs, mult, place):
+    packed_out[...] = packed
+
+
+def x_rim_kernel(xs, below, above, coarse, packed, g_in, a_in, b_in, mult_in, g, a, b, mult, send):
+    f, p, xc, yc, zc, dp = parts(xs)
+    lane = lanes(NK)
+    row = lax.broadcasted_iota(jnp.int32, (NK, NI), 0)
+
+    def lifted(j):
+        z, v = across(zc, j), across(p, j)
+        top = jnp.where(row == NK - 1, 0.0, z)
+        low = rolled(top, 1, 0)
+        return low, top, low * rolled(v, 1, 0) + top * rolled(v, -1, 0)
+
+    low, top, z_part = lifted(0)
+    y, y_left = across(yc, 0), below[pl.ds(0, NK), :]
+    diag, off = x_matrix(across(xc, 0), low + top + y + y_left + across(dp, 0))
+    rhs = across(f, 0) + y_left * below[pl.ds(NK, NK), :] + y * across(p, 1) + z_part
+
+    def keep(n, value):
+        mult[pl.ds(n * ROWS, NK, stride=NJ), :] = value
+
+    rhs, left, right = x_eliminate(diag, off, rhs, keep)
+    first = pl.ds(0, NK, stride=NJ)
+    g[first, :], a[first, :], b[first, :] = rhs, left, right
+    line = jnp.zeros((NK, NI), F32)
+    for q, pick in enumerate(x_picks(rhs, left, right, across(xc, 0))):
+        line = line + jnp.where(lane == q * NK + row, pick, 0.0)
+    line = jnp.sum(line, axis=0, keepdims=True)
+
+    j = NJ - 1
+    _, _, z_part = lifted(j)
+    y = across(yc, j)
+    rhs = across(f, j) + across(yc, j - 1) * across(p, j - 1) + y * above[pl.ds(0, NK), :] + z_part
+    rhs = x_second_solve(rhs, lambda n: mult_in[pl.ds(n * ROWS + j, NK, stride=NJ), :])
+    g[pl.ds(j, NK, stride=NJ), :] = rhs
+    last = jnp.where(lane == row, column(rhs, 0), 0.0) + jnp.where(lane == NK + row, column(rhs, NI - 1), 0.0)
+    last = jnp.sum(last, axis=0, keepdims=True)
+    was = packed[...]
+    was = jnp.where(row == 0, line, was)
+    send[pl.ds(0, NJ), :] = jnp.where(jnp.logical_and(row == NJ - 1, lane < 2 * NK), last, was)
+    for q in range(2):
+        at = NJ + q * 104
+        send[pl.ds(at, 24), :] = below[pl.ds(2 * NK + q * 24, 24), :]
+        send[pl.ds(at + 24, 64), :] = coarse[pl.ds(q * 64, 64), :]
+        send[pl.ds(at + 88, 16), :] = above[pl.ds(NK + q * 16, 16), :]
+
+
+def x_second_solve(rhs, kept):
     for n, s in enumerate(STEPS):
-        rhs = rhs + mult[2 * n, place, :] * rolled(rhs, s, 1) + mult[2 * n + 1, place, :] * rolled(rhs, -s, 1)
-    return rhs * mult[2 * len(STEPS), place, :]
+        rhs = rhs + kept(2 * n) * rolled(rhs, s, 1) + kept(2 * n + 1) * rolled(rhs, -s, 1)
+    return rhs * kept(2 * len(STEPS))
 
 
 def x_fluxes(fs, source, low, inv, up):
@@ -210,11 +288,12 @@
     return z_terms(zc, field, k, level(f, k) + before + after)
 
 
-def y_first_kernel(f, xc, yc, zc, dp, below, got, g, a, b, yg, ya, yb, yw, yinv, xred, cl, send, fs, cs, field, src, base):
+def y_first_kernel(xs, got, g, a, b, yg, ya, yb, yw, yinv, xred, cl, send, fs, cs, field, src, base):
+    f, p, xc, yc, zc, dp = parts(xs)
     d = lax.axis_index("gx")
     e = lax.axis_index("gy")
     lane = lanes(NJ)
-    part = lambda n, q: rolled(got[n], -NK * q, 1)
+    part = lambda n, q: rolled(got[n, pl.ds(0, NJ), :], -NK * q, 1)
     m = [part(n, 3) for n in range(GX)]
     low, inv, up = [None], [], []
     for n in range(GX - 1):
@@ -307,7 +386,8 @@
         terms[pl.ds(j, NK, stride=NJ), :] = before + after
 
 
-def x_again_kernel(f, yc, zc, below, got, yg, ya, yb, mult, g, yred, send, fs, field, terms):
+def x_again_kernel(xs, below, got, yg, ya, yb, mult, g, yred, send, fs, field, terms):
+    f, p, xc, yc, zc, dp = parts(xs)
     part = lambda n, q: got[n, pl.ds(q * NK, NK), :]
     prev = None
     for n in range(GY - 1):
@@ -341,7 +421,7 @@
             [z_terms(zc, field, k, level(f, k) + level(terms, k)) for k in range(k0, k0 + group)], axis=0
         )
         place = pl.ds(k0 * NJ, group * NJ)
-        rhs = x_second_solve(rhs, mult, place)
+        rhs = x_second_solve(rhs, lambda n: mult[pl.ds(n * ROWS + k0 * NJ, group * NJ), :])
         g[place, :] = rhs
         for k in range(k0, k0 + group):
             mine = rhs[(k - k0) * NJ : (k - k0 + 1) * NJ]
@@ -350,7 +430,8 @@
     send[...] = packed
 
 
-def y_again_kernel(f, xc, zc, got, g, a, b, xred, cl, yw, yinv, yg, send, fs, field, src):
+def y_again_kernel(xs, got, g, a, b, xred, cl, yw, yinv, yg, send, fs, field, src):
+    f, p, xc, yc, zc, dp = parts(xs)
     part = lambda n, q: rolled(got[n], -NK * q, 1)
     x_fluxes(
         fs,
@@ -380,7 +461,8 @@
     send[pl.ds(0, NK), :] = value
 
 
-def residual_kernel(f, xc, yc, zc, dp, below, got, yg, ya, yb, yred, cl, field, coarse, fs, terms, tmp):
+def residual_kernel(xs, below, got, yg, ya, yb, yred, cl, field, coarse, fs, terms, tmp):
+    f, p, xc, yc, zc, dp = parts(xs)
     d = lax.axis_index("gx")
     lane = lanes(NJ)
     part = lambda n, q: got[n, pl.ds(q * NK, NK), :]
@@ -429,8 +511,16 @@
         return outs
 
     def whole_coef(q, J):
-        rows = pl.ds(q * 104 + J * 8, 8)
-        return jnp.concatenate([coef[2 * m, rows, :] + coef[2 * m + 1, rows, :] for m in range(4)], axis=1)
+        rows = pl.ds(NJ + (q // 2) * 104 + J * 8, 8)
+        outs = []
+        for m in range(4):
+            even, odd = coef[2 * m, rows, :], coef[2 * m + 1, rows, :]
+            if q % 2:
+                even = rolled(even, 64, 1)
+            else:
+                odd = rolled(odd, 64, 1)
+            outs.append(jnp.where(lane < 64, even, odd))
+        return jnp.concatenate(outs, axis=1)
 
     res, diag, weight, cxl, cxi, cyl, cyr, czl, czt = ([] for _ in range(9))
     for J in range(12):
@@ -488,57 +578,61 @@
 
 
 def body(forcing, pressure_in, x_coupling, y_coupling, z_coupling, damping):
-    f, p, xc, yc, zc, dp = (
-        v.reshape(ROWS, NI) for v in (forcing, pressure_in, x_coupling, y_coupling, z_coupling, damping)
-    )
+    args = [v.reshape(ROWS, NI) for v in (forcing, pressure_in, x_coupling, y_coupling, z_coupling, damping)]
     forth = [(n, n + 1) for n in range(GY - 1)]
     back = [(n + 1, n) for n in range(GY - 1)]
     whole = sds(ROWS, NI)
-    up, down, coef = call(first_kernel, [sds(128, NI), sds(80, NI), sds(256, NI)], p, xc, yc, zc, dp, scratch=[(128, NI)])
+    kept = sds((2 * len(STEPS) + 1) * ROWS, NI)
+    xs, up, down, coef = call(
+        first_kernel,
+        [sds(6 * ROWS, NI), sds(80, NI), sds(48, NI), sds(128, NI)],
+        *args,
+        scratch=[(128, NI)],
+        hbm=True,
+        sems=6,
+    )
     below = lax.ppermute(up, "gy", forth)
     above = lax.ppermute(down, "gy", back)
+    g, a, b, mult, packed = call(x_first_kernel, [whole, whole, whole, kept, sds(NJ, NI)], xs, flops=10**8)
     g, a, b, mult, send = call(
-        x_first_kernel,
-        [whole, whole, whole, sds(2 * len(STEPS) + 1, ROWS, NI), sds(NJ, NI)],
-        f, p, xc, yc, zc, dp, below, above,
-    )
-    got = spread(send, "gx", GX)
-    coef_rows = jnp.concatenate(
-        [below[32:].reshape(4, 24, NI), coef.reshape(4, 64, NI), above[16:].reshape(4, 16, NI)], axis=1
-    ).reshape(416, NI)
-    coef_all = lax.all_gather(coef_rows, "gx", axis=0, tiled=False)
+        x_rim_kernel,
+        [whole, whole, whole, kept, sds(NJ + 208, NI)],
+        xs, below, above, coef, packed, g, a, b, mult,
+        aliases={5: 0, 6: 1, 7: 2, 8: 3},
+    )
+    got_coef = got = spread(send, "gx", GX)
     yg, ya, yb, yw, yinv, xred, cl, send = call(
         y_first_kernel,
         [whole] * 5 + [sds(3 * GX, NJ, NI), sds(NJ, NI), sds(5 * NK, NI)],
-        f, xc, yc, zc, dp, below, got, g, a, b,
+        xs, got, g, a, b,
         scratch=[(GX + 1, NJ, NI), (GX + 1, NJ, NI), (ROWS, NI), (ROWS, NI), (ROWS, NI)],
     )
     got = spread(send, "gy", GY)
     g, yred, send = call(
         x_again_kernel,
         [whole, sds(3 * GY, NK, NI), sds(NJ, NI)],
-        f, yc, zc, below, got, yg, ya, yb, mult,
+        xs, below, got, yg, ya, yb, mult,
         scratch=[(GY + 1, NK, NI), (ROWS, NI), (ROWS, NI)],
     )
     got = spread(send, "gx", GX)
     yg, send = call(
         y_again_kernel,
         [whole, sds(2 * NK, NI)],
-        f, xc, zc, got, g, a, b, xred, cl, yw, yinv,
+        xs, got, g, a, b, xred, cl, yw, yinv,
         scratch=[(GX + 1, NJ, NI), (ROWS, NI), (ROWS, NI)],
     )
     got = spread(send, "gy", GY)
     field, coarse = call(
         residual_kernel,
         [whole, sds(64, NI)],
-        f, xc, yc, zc, dp, below, got, yg, ya, yb, yred, cl,
+        xs, below, got, yg, ya, yb, yred, cl,
         scratch=[(GY + 1, NK, NI), (ROWS, NI), (128, NI)],
     )
     lower = lax.ppermute(coarse[48:], "gy", forth)
     upper = lax.ppermute(coarse[:16], "gy", back)
     got = spread(jnp.concatenate([lower, coarse, upper], axis=0), "gx", GX)
     res, cor = call(
-        coarse_kernel, [sds(64, 64), sds(64, 512)], got, coef_all, scratch=[(64, NI), (4, 64, NI)]
+        coarse_kernel, [sds(64, 64), sds(64, 512)], got, got_coef, scratch=[(64, NI), (4, 64, NI)]
     )
     return field.reshape(NK, NJ, NI), res.reshape(8, 8, 64), cor.reshape(8, 8, 512)
 

time: 119 us -> 103 us (0.87)
  between operations: 14.2 us -> 0.76 us
  local copies, waits for them, and re-layouts: 11.5 us -> 2.13 us
  blocking collectives: 65.2 us -> 72.9 us
  waiting for transfers between devices: 6.45 us -> 3.04 us
  Pallas kernels: 9.63 us -> 12.8 us
    unnamed x32 -> x4, local copies, waits for them, and re-layouts: 11.4 us -> 1.96 us
    all_to_all x5, blocking collectives: 65.2 us -> 72.9 us  [spread(): return lax.all_to_all(many, axis, split_axis=0, concat_axis=0, tiled=True)]
    ppermute x1, waiting for transfers between devices: 3.39 us -> 0.01 us  [body(): above = lax.ppermute(down, 'gy', back)]
    pallas_call x7 -> x8, Pallas kernels: 9.63 us -> 12.8 us  [call(): pl.pallas_call(kernel, out_shape=outs, in_specs=[inside] * len(args), out...]
  transfers between devices with their start and end apart: 5 -> 4, of which waited for: 2 -> 1; matrix products, arithmetic and copies ran while one was open for 0% -> 0% of each run, Pallas kernels for 7% -> 5%
where the time goes in v2:
time: 103 us
  blocking collectives  72.9 us (71%)
  Pallas kernels  12.8 us (12%)
  starting transfers between devices  11 us (11%)
  waiting for transfers between devices  3.04 us (3%)
  local copies, waits for them, and re-layouts  2.13 us (2%)
    all_to_all x5, blocking collectives, spread(): return lax.all_to_all(many, axis, split_axis=0, concat_axis=0, tiled=True)  72.9 us
    pallas_call x8, Pallas kernels, call(): pl.pallas_call(kernel, out_shape=outs, in_specs=[inside] * len(args), out...  12.8 us
    ppermute x1, starting transfers between devices, body(): below = lax.ppermute(up, 'gy', forth)  4.59 us
    ppermute x1, waiting for transfers between devices, body(): upper = lax.ppermute(coarse[:16], 'gy', back)  3.03 us
    ppermute x1, starting transfers between devices, body(): lower = lax.ppermute(coarse[48:], 'gy', forth)  2.61 us
  transfers between devices with their start and end apart: 4, of which 1 were waited for; matrix products, arithmetic and copies ran while one was open for 0% of the time, Pallas kernels for 5%

profile of v2, /device:TPU:1, one launch (start us, length us, event | category | flops | bytes accessed | tf_op | source)
XLA Modules:
  0.0 102.6 jit_solution(1756886328848930163)
XLA Ops:
  0.6 2.3 %shard_map.85 = (f32[1536,128]{1,0:T(8,128)}, f32[80,128]{1,0:T(8,128)}, f32[48,128]{1,0:T(8,128)}, f32[128,128]{1,0:T(8,128)}) custom-call(f32[256,128]{1,0:T(8,128)} %bitcast.9, f32[256,128]{1,0:T(8,128)} %bitcast.10, f32[256,128]{1,0:T(8,128)} %bitcast.11, f32[256,128]{1,0:T(8,128)} %bitcast.12, f32[256,128]{1,0:T(8,128)} %bitcast.13, f32[256,128]{1,0:T(8,128)} %bitcast.14), custom_call_target="tpu_custom_call" | custom-call | tf_op jit(solution)/shard_map/pallas_call | solution.py:29
  3.0 4.6 %collective-permute-start = (f32[80,128]{1,0:T(8,128)}, f32[80,128]{1,0:T(8,128)S(1)}, u32[]{:S(2)}, u32[]{:S(2)}) collective-permute-start(f32[80,128]{1,0:T(8,128)} %get-tuple-element.35), channel_id=1, source_target_pairs={{0,1},{1,2},{2,3},{3,4},{4,5},{5,6},{6,7},{7,8},{8,9},{9,10},{10,1... | collective-permute-start | bytes 122888 | tf_op jit(solution)/shard_map/ppermute | solution.py:594
  7.6 1.9 %collective-permute-start.1 = (f32[48,128]{1,0:T(8,128)}, f32[48,128]{1,0:T(8,128)S(1)}, u32[]{:S(2)}, u32[]{:S(2)}) collective-permute-start(f32[48,128]{1,0:T(8,128)} %get-tuple-element.36), channel_id=1, source_target_pairs={{1,0},{2,1},{3,2},{4,3},{5,4},{6,5},{7,6},{8,7},{9,8},{10,9},{11,1... | collective-permute-start | bytes 73736 | tf_op jit(solution)/shard_map/ppermute | solution.py:595
  9.5 0.0 copy-start
  9.5 1.1 %copy-done = f32[1536,128]{1,0:T(8,128)S(1)} copy-done((f32[1536,128]{1,0:T(8,128)S(1)}, f32[1536,128]{1,0:T(8,128)}, u32[]{:S(2)}) %copy-start) | copy-done | bytes 786456
  10.6 5.0 %shard_map.86 = (f32[256,128]{1,0:T(8,128)S(1)}, f32[256,128]{1,0:T(8,128)S(1)}, f32[256,128]{1,0:T(8,128)S(1)}, f32[3840,128]{1,0:T(8,128)S(1)}, f32[16,128]{1,0:T(8,128)S(1)}) custom-call(f32[1536,128]{1,0:T(8,128)S(1)} %copy-done), custom_call_target="tpu_custom_call" | custom-call | flops 100000000 | bytes 1048576 | tf_op jit(solution)/shard_map/pallas_call | solution.py:29
  15.6 0.0 collective-permute-done.1.above
  15.6 0.0 collective-permute-done.below
  15.6 0.0 copy-start.1
  15.6 0.8 copy-done.1
  16.4 0.8 shard_map.87
  17.2 0.1 broadcast_in_dim.10
  17.3 22.4 %all_to_all.25.got.coef = f32[8,224,128]{2,1,0:T(8,128)S(1)} all-to-all(f32[8,224,128]{2,1,0:T(8,128)S(1)} %broadcast_in_dim.10), channel_id=1, replica_groups=mesh['gx'=8,'gy'=16] {'gx'}, dimensions={0} | all-to-all | bytes 1835008 | tf_op jit(solution)/shard_map/all_to_all | solution.py:577
  39.7 0.6 shard_map.88
  40.4 17.7 %all_to_all.26.got = f32[16,80,128]{2,1,0:T(8,128)S(1)} all-to-all(f32[16,80,128]{2,1,0:T(8,128)S(1)} %broadcast_in_dim.11), channel_id=1, replica_groups=mesh['gx'=8,'gy'=16] {'gy'}, dimensions={0} | all-to-all | bytes 1310720 | tf_op jit(solution)/shard_map/all_to_all | solution.py:577
  58.1 1.0 shard_map.89
  59.2 9.4 %all_to_all.27.got = f32[8,16,128]{2,1,0:T(8,128)S(1)} all-to-all(f32[8,16,128]{2,1,0:T(8,128)S(1)} %broadcast_in_dim.12), channel_id=1, replica_groups=mesh['gx'=8,'gy'=16] {'gx'}, dimensions={0} | all-to-all | bytes 131072 | tf_op jit(solution)/shard_map/all_to_all | solution.py:577
  68.6 0.5 shard_map.90
  69.1 11.6 %all_to_all.28.got = f32[16,32,128]{2,1,0:T(8,128)S(1)} all-to-all(f32[16,32,128]{2,1,0:T(8,128)S(1)} %broadcast_in_dim.13), channel_id=1, replica_groups=mesh['gx'=8,'gy'=16] {'gy'}, dimensions={0} | all-to-all | bytes 524288 | tf_op jit(solution)/shard_map/all_to_all | solution.py:577
  80.7 0.9 shard_map.91
  81.6 2.6 %collective-permute-start.2 = (f32[16,128]{1,0:T(8,128)S(1)}, f32[16,128]{1,0:T(8,128)S(1)}, u32[]{:S(2)}, u32[]{:S(2)}) collective-permute-start(f32[16,128]{1,0:T(8,128)S(1)} %get-tuple-element.65), channel_id=1, source_target_pairs={{0,1},{1,2},{2,3},{3,4},{4,5},{5,6},{6,7},{7,8},{8,9},{9,10},{10,1... | collective-permute-start | bytes 24584 | tf_op jit(solution)/shard_map/ppermute | solution.py:631
  84.3 1.9 %collective-permute-start.3 = (f32[16,128]{1,0:T(8,128)S(1)}, f32[16,128]{1,0:T(8,128)S(1)}, u32[]{:S(2)}, u32[]{:S(2)}) collective-permute-start(f32[16,128]{1,0:T(8,128)S(1)} %get-tuple-element.66), channel_id=1, source_target_pairs={{1,0},{2,1},{3,2},{4,3},{5,4},{6,5},{7,6},{8,7},{9,8},{10,9},{11,1... | collective-permute-start | bytes 24584 | tf_op jit(solution)/shard_map/ppermute | solution.py:632
  86.2 0.0 collective-permute-done.2
  86.2 3.0 %collective-permute-done.3 = f32[16,128]{1,0:T(8,128)S(1)} collective-permute-done((f32[16,128]{1,0:T(8,128)S(1)}, f32[16,128]{1,0:T(8,128)S(1)}, u32[]{:S(2)}, u32[]{:S(2)}) %collective-permute-start.3) | collective-permute-done | bytes 8224 | tf_op jit(solution)/shard_map/ppermute | solution.py:632
  89.3 11.6 %all_to_all.29.got = f32[8,96,128]{2,1,0:T(8,128)S(1)} all-to-all(f32[8,96,128]{2,1,0:T(8,128)S(1)} %broadcast_in_dim.14), channel_id=1, replica_groups=mesh['gx'=8,'gy'=16] {'gx'}, dimensions={0} | all-to-all | bytes 786432 | tf_op jit(solution)/shard_map/all_to_all | solution.py:577
  100.9 1.7 %shard_map.92 = (f32[64,64]{1,0:T(8,128)}, f32[64,512]{1,0:T(8,128)}) custom-call(f32[8,96,128]{2,1,0:T(8,128)S(1)} %all_to_all.29.got, f32[8,224,128]{2,1,0:T(8,128)S(1)} %all_to_all.25.got.coef), custom_call_target="tpu_custom_call" | custom-call | tf_op jit(solution)/shard_map/pallas_call | solution.py:29
  (6 shorter events, 0.1 us)
Async XLA Ops:
  3.0 12.6 %collective-permute-start = (f32[80,128]{1,0:T(8,128)}, f32[80,128]{1,0:T(8,128)S(1)}, u32[]{:S(2)}, u32[]{:S(2)}) collective-permute-start(f32[80,128]{1,0:T(8,128)} %get-tuple-element.35), channel_id=1, source_target_pairs={{0,1},{1,2},{2,3},{3,4},{4,5},{5,6},{6,7},{7,8},{8,9},{9,10},{10,1... | collective-permute-start | bytes 122888 | tf_op jit(solution)/shard_map/ppermute | solution.py:594
  7.6 8.0 %collective-permute-start.1 = (f32[48,128]{1,0:T(8,128)}, f32[48,128]{1,0:T(8,128)S(1)}, u32[]{:S(2)}, u32[]{:S(2)}) collective-permute-start(f32[48,128]{1,0:T(8,128)} %get-tuple-element.36), channel_id=1, source_target_pairs={{1,0},{2,1},{3,2},{4,3},{5,4},{6,5},{7,6},{8,7},{9,8},{10,9},{11,1... | collective-permute-start | bytes 73736 | tf_op jit(solution)/shard_map/ppermute | solution.py:595
  9.5 1.1 %copy-start = (f32[1536,128]{1,0:T(8,128)S(1)}, f32[1536,128]{1,0:T(8,128)}, u32[]{:S(2)}) copy-start(f32[1536,128]{1,0:T(8,128)} %get-tuple-element.34.xs) | copy-start | bytes 2359300
  15.6 0.8 copy-start.1
  81.6 4.6 %collective-permute-start.2 = (f32[16,128]{1,0:T(8,128)S(1)}, f32[16,128]{1,0:T(8,128)S(1)}, u32[]{:S(2)}, u32[]{:S(2)}) collective-permute-start(f32[16,128]{1,0:T(8,128)S(1)} %get-tuple-element.65), channel_id=1, source_target_pairs={{0,1},{1,2},{2,3},{3,4},{4,5},{5,6},{6,7},{7,8},{8,9},{9,10},{10,1... | collective-permute-start | bytes 24584 | tf_op jit(solution)/shard_map/ppermute | solution.py:631
  84.3 5.0 %collective-permute-start.3 = (f32[16,128]{1,0:T(8,128)S(1)}, f32[16,128]{1,0:T(8,128)S(1)}, u32[]{:S(2)}, u32[]{:S(2)}) collective-permute-start(f32[16,128]{1,0:T(8,128)S(1)} %get-tuple-element.66), channel_id=1, source_target_pairs={{1,0},{2,1},{3,2},{4,3},{5,4},{6,5},{7,6},{8,7},{9,8},{10,9},{11,1... | collective-permute-start | bytes 24584 | tf_op jit(solution)/shard_map/ppermute | solution.py:632

commit v3 on v2

--- a/solution.py
+++ b/solution.py
@@ -34,7 +34,7 @@
         scratch_shapes=shapes,
         input_output_aliases=aliases,
         cost_estimate=cost,
-        compiler_params=pltpu.CompilerParams(vmem_limit_bytes=(58 if hbm else 16) * 1024 * 1024),
+        compiler_params=pltpu.CompilerParams(vmem_limit_bytes=16 * 1024 * 1024),
     )(*args)
 
 
@@ -114,20 +114,17 @@
         out[pl.ds(base + J * 8, 8), :] = across(tmp, 2 * J, 8) + across(tmp, 2 * J + 1, 8)
 
 
-def first_kernel(fh, ph, xh, yh, zh, dh, xs, up, down, coarse, tmp, sems):
-    order = (3, 1, 2, 4, 5, 0)
-    copies = {
-        n: pltpu.make_async_copy(ref, xs.at[pl.ds(n * ROWS, ROWS), :], sems.at[n])
+def first_kernel(fh, ph, xh, yh, zh, dh, xs, near, far, coarse, tmp, sems):
+    copies = [
+        pltpu.make_async_copy(ref, xs.at[pl.ds(n * ROWS, ROWS), :], sems.at[n])
         for n, ref in enumerate((fh, ph, xh, yh, zh, dh))
-    }
-    for n in order:
-        copies[n].start()
+    ]
+    for copy in copies:
+        copy.start()
+    for copy in copies:
+        copy.wait()
     f, p, xc, yc, zc, dp = parts(xs)
-    for n in order:
-        copies[n].wait()
-    up[pl.ds(0, NK), :] = across(yc, NJ - 1)
-    up[pl.ds(NK, NK), :] = across(p, NJ - 1)
-    down[pl.ds(0, NK), :] = across(p, 0)
+    odd = lax.rem(lax.axis_index("gy"), 2) == 1
     for q, two in enumerate(((xc, yc), (zc, dp))):
         total = jnp.zeros((128, NI), F32)
         for half, ref in enumerate(two):
@@ -135,8 +132,25 @@
             total = total + squeeze(pairs, start=64 * half)
         tmp[...] = total
         store_coarse(coarse, q * 64, tmp)
-        up[pl.ds(2 * NK + q * 24, 24), :] = coarse[pl.ds(q * 64 + 40, 24), :]
-        down[pl.ds(NK + q * 16, 16), :] = coarse[pl.ds(q * 64, 16), :]
+
+    def put(place, up, down):
+        near[place, :] = jnp.where(odd, down, up)
+        far[place, :] = jnp.where(odd, up, down)
+
+    put(pl.ds(0, NK), across(p, NJ - 1), across(p, 0))
+    put(pl.ds(NK, NK), across(yc, NJ - 1), across(yc, 0))
+    for q in range(2):
+        put(pl.ds(2 * NK + q * 24, 24), coarse[pl.ds(q * 64 + 40, 24), :], coarse[pl.ds(q * 64, 24), :])
+
+
+def sorted_out(near, far, place):
+    e = lax.axis_index("gy")
+    odd = lax.rem(e, 2) == 1
+    one, two = near[place, :], far[place, :]
+    return (
+        jnp.where(e == 0, 0.0, jnp.where(odd, one, two)),
+        jnp.where(e == GY - 1, 0.0, jnp.where(odd, two, one)),
+    )
 
 
 def x_matrix(x, rest):
@@ -149,8 +163,7 @@
 
 def x_eliminate(diag, off, rhs, keep):
     wide = lanes(diag.shape[0])
-    left = jnp.where(wide == 0, 1.0, 0.0).astype(F32)
-    right = jnp.where(wide == NI - 1, 1.0, 0.0).astype(F32)
+    ends = jnp.where(jnp.logical_or(wide == 0, wide == NI - 1), 1.0, 0.0).astype(F32)
     for n, s in enumerate(STEPS):
         inv = 1.0 / diag
         low = rolled(off, s, 1)
@@ -159,12 +172,15 @@
         keep(2 * n, alpha)
         keep(2 * n + 1, beta)
         diag = diag + alpha * low + beta * off
-        off = beta * rolled(off, -s, 1)
         rhs = rhs + alpha * rolled(rhs, s, 1) + beta * rolled(rhs, -s, 1)
-        left = left + alpha * rolled(left, s, 1) + beta * rolled(left, -s, 1)
-        right = right + alpha * rolled(right, s, 1) + beta * rolled(right, -s, 1)
+        if s < NI // 2:
+            off = beta * rolled(off, -s, 1)
+            ends = ends + alpha * rolled(ends, s, 1) + beta * rolled(ends, -s, 1)
     inv = 1.0 / diag
     keep(2 * len(STEPS), inv)
+    other = rolled(ends, NI // 2, 1)
+    left = jnp.where(wide < NI // 2, ends, alpha * other)
+    right = jnp.where(wide < NI // 2, beta * other, ends)
     return rhs * inv, left * inv, right * inv
 
 
@@ -172,22 +188,26 @@
     return column(g, 0), column(g, NI - 1), column(a, 0), column(b, 0), column(b, NI - 1), column(x, NI - 1)
 
 
-def x_first_kernel(xs, g, a, b, mult, packed_out):
+def x_first_kernel(xs, near, far, coarse, below, g, a, b, mult, send):
     f, p, xc, yc, zc, dp = parts(xs)
     lane = lanes(NJ)
     row = lax.broadcasted_iota(jnp.int32, (NJ, NI), 0)
     packed = jnp.zeros((NJ, NI), F32)
+    p_below, p_above = sorted_out(near, far, pl.ds(0, NK))
+    y_below, _ = sorted_out(near, far, pl.ds(NK, NK))
+    below[...] = y_below
     group = 2
     for k0 in range(0, NK, group):
         diag, off, rhs = [], [], []
         for k in range(k0, k0 + group):
             y, v = level(yc, k), level(p, k)
-            y_left = jnp.where(row == 0, 0.0, rolled(y, 1, 0))
+            y_left = jnp.where(row == 0, y_below[k : k + 1, :], rolled(y, 1, 0))
             matrix = x_matrix(level(xc, k), z_sum(zc, k, y_left + y + level(dp, k)))
             diag.append(matrix[0])
             off.append(matrix[1])
-            after = jnp.where(row == NJ - 1, 0.0, rolled(v, -1, 0))
-            rhs.append(z_terms(zc, p, k, level(f, k) + y_left * rolled(v, 1, 0) + y * after))
+            before = jnp.where(row == 0, p_below[k : k + 1, :], rolled(v, 1, 0))
+            after = jnp.where(row == NJ - 1, p_above[k : k + 1, :], rolled(v, -1, 0))
+            rhs.append(z_terms(zc, p, k, level(f, k) + y_left * before + y * after))
         diag, off, rhs = (jnp.concatenate(v, axis=0) for v in (diag, off, rhs))
         place = pl.ds(k0 * NJ, group * NJ)
 
@@ -200,52 +220,13 @@
             part = slice((k - k0) * NJ, (k - k0 + 1) * NJ)
             for q, pick in enumerate(x_picks(rhs[part], left[part], right[part], level(xc, k))):
                 packed = jnp.where(lane == q * NK + k, pick, packed)
-    packed_out[...] = packed
-
-
-def x_rim_kernel(xs, below, above, coarse, packed, g_in, a_in, b_in, mult_in, g, a, b, mult, send):
-    f, p, xc, yc, zc, dp = parts(xs)
-    lane = lanes(NK)
-    row = lax.broadcasted_iota(jnp.int32, (NK, NI), 0)
-
-    def lifted(j):
-        z, v = across(zc, j), across(p, j)
-        top = jnp.where(row == NK - 1, 0.0, z)
-        low = rolled(top, 1, 0)
-        return low, top, low * rolled(v, 1, 0) + top * rolled(v, -1, 0)
-
-    low, top, z_part = lifted(0)
-    y, y_left = across(yc, 0), below[pl.ds(0, NK), :]
-    diag, off = x_matrix(across(xc, 0), low + top + y + y_left + across(dp, 0))
-    rhs = across(f, 0) + y_left * below[pl.ds(NK, NK), :] + y * across(p, 1) + z_part
-
-    def keep(n, value):
-        mult[pl.ds(n * ROWS, NK, stride=NJ), :] = value
-
-    rhs, left, right = x_eliminate(diag, off, rhs, keep)
-    first = pl.ds(0, NK, stride=NJ)
-    g[first, :], a[first, :], b[first, :] = rhs, left, right
-    line = jnp.zeros((NK, NI), F32)
-    for q, pick in enumerate(x_picks(rhs, left, right, across(xc, 0))):
-        line = line + jnp.where(lane == q * NK + row, pick, 0.0)
-    line = jnp.sum(line, axis=0, keepdims=True)
-
-    j = NJ - 1
-    _, _, z_part = lifted(j)
-    y = across(yc, j)
-    rhs = across(f, j) + across(yc, j - 1) * across(p, j - 1) + y * above[pl.ds(0, NK), :] + z_part
-    rhs = x_second_solve(rhs, lambda n: mult_in[pl.ds(n * ROWS + j, NK, stride=NJ), :])
-    g[pl.ds(j, NK, stride=NJ), :] = rhs
-    last = jnp.where(lane == row, column(rhs, 0), 0.0) + jnp.where(lane == NK + row, column(rhs, NI - 1), 0.0)
-    last = jnp.sum(last, axis=0, keepdims=True)
-    was = packed[...]
-    was = jnp.where(row == 0, line, was)
-    send[pl.ds(0, NJ), :] = jnp.where(jnp.logical_and(row == NJ - 1, lane < 2 * NK), last, was)
+    send[pl.ds(0, NJ), :] = packed
     for q in range(2):
         at = NJ + q * 104
-        send[pl.ds(at, 24), :] = below[pl.ds(2 * NK + q * 24, 24), :]
+        lower, upper = sorted_out(near, far, pl.ds(2 * NK + q * 24, 24))
+        send[pl.ds(at, 24), :] = lower
         send[pl.ds(at + 24, 64), :] = coarse[pl.ds(q * 64, 64), :]
-        send[pl.ds(at + 88, 16), :] = above[pl.ds(NK + q * 16, 16), :]
+        send[pl.ds(at + 88, 16), :] = upper[:16]
 
 
 def x_second_solve(rhs, kept):
@@ -461,7 +442,7 @@
     send[pl.ds(0, NK), :] = value
 
 
-def residual_kernel(xs, below, got, yg, ya, yb, yred, cl, field, coarse, fs, terms, tmp):
+def residual_kernel(xs, below, got, yg, ya, yb, yred, cl, field, near, far, coarse, fs, terms, tmp):
     f, p, xc, yc, zc, dp = parts(xs)
     d = lax.axis_index("gx")
     lane = lanes(NJ)
@@ -489,14 +470,60 @@
     outer = jnp.concatenate([rim[2 * K] + rim[2 * K + 1] for K in range(NK // 2)], axis=0)
     tmp[...] = parity_shift(squeeze(pairs) + edges(outer))
     store_coarse(coarse, 0, tmp)
-
-
-def coarse_kernel(got, coef, res_out, cor_out, tmp, cor_tmp):
-    d = lax.axis_index("gx")
+    odd = lax.rem(lax.axis_index("gy"), 2) == 1
+    up, down = coarse[pl.ds(48, 16), :], coarse[pl.ds(0, 16), :]
+    near[...] = jnp.where(odd, down, up)
+    far[...] = jnp.where(odd, up, down)
+
+
+def join_kernel(near, far, coarse, send):
+    lower, upper = sorted_out(near, far, pl.ds(0, 16))
+    send[pl.ds(0, 16), :] = lower
+    send[pl.ds(16, 64), :] = coarse[...]
+    send[pl.ds(80, 16), :] = upper
+
+
+def coarse_matrix_kernel(coef, weight_out, x_low_out, x_up_out, y_out, z_out):
     e = lax.axis_index("gy")
     lane = lanes(8)
     wide = lanes(8, 4 * NI)
     level_k = lax.broadcasted_iota(jnp.int32, (8, 4 * NI), 0)
+
+    def whole_coef(q, J):
+        rows = pl.ds(NJ + (q // 2) * 104 + J * 8, 8)
+        outs = []
+        for m in range(4):
+            even, odd = coef[2 * m, rows, :], coef[2 * m + 1, rows, :]
+            if q % 2:
+                even = rolled(even, 64, 1)
+            else:
+                odd = rolled(odd, 64, 1)
+            outs.append(jnp.where(lane < 64, even, odd))
+        return jnp.concatenate(outs, axis=1)
+
+    y_before = whole_coef(1, 0)
+    y_out[pl.ds(0, 8), :] = y_before
+    for J in range(12):
+        rows = pl.ds(J * 8, 8)
+        x, y, z, damp = (whole_coef(q, J + 1) for q in range(4))
+        x_left = jnp.where(wide == 0, 0.0, rolled(x, 1, 1))
+        z_top = jnp.where(level_k == 7, 0.0, z)
+        total = x_left + x + y_before + y + rolled(z_top, 1, 0) + z_top + damp
+        at = e * 8 + J - 2
+        valid = jnp.logical_and(at >= 0, at < 8 * GY)
+        total = jnp.where(valid, total, 1.0)
+        weight_out[0, rows, :] = total
+        weight_out[1, rows, :] = jnp.where(valid, RELAX / total, 0.0)
+        x_low_out[rows, :] = x_left
+        x_up_out[rows, :] = jnp.where(wide == 4 * NI - 1, 0.0, x)
+        y_out[pl.ds(J * 8 + 8, 8), :] = y
+        z_out[rows, :] = z_top
+        y_before = y
+
+
+def coarse_kernel(got, weight, x_low, x_up, y_all, z_all, res_out, cor_out, tmp, cor_tmp):
+    d = lax.axis_index("gx")
+    lane = lanes(8)
 
     def whole_res(J):
         rows = pl.ds(J * 8, 8)
@@ -510,19 +537,10 @@
             outs.append(value)
         return outs
 
-    def whole_coef(q, J):
-        rows = pl.ds(NJ + (q // 2) * 104 + J * 8, 8)
-        outs = []
-        for m in range(4):
-            even, odd = coef[2 * m, rows, :], coef[2 * m + 1, rows, :]
-            if q % 2:
-                even = rolled(even, 64, 1)
-            else:
-                odd = rolled(odd, 64, 1)
-            outs.append(jnp.where(lane < 64, even, odd))
-        return jnp.concatenate(outs, axis=1)
-
-    res, diag, weight, cxl, cxi, cyl, cyr, czl, czt = ([] for _ in range(9))
+    at = lambda ref, J: ref[pl.ds(J * 8, 8), :]
+    diag = lambda J: weight[0, pl.ds(J * 8, 8), :]
+    scale = lambda J: weight[1, pl.ds(J * 8, 8), :]
+    res = []
     for J in range(12):
         outs = whole_res(J)
         if 2 <= J < 10:
@@ -532,37 +550,21 @@
             mine = jnp.where(lax.rem(d, 2) == 1, rolled(mine, 64, 1), mine)
             tmp[pl.ds(J - 2, 8, stride=8), :] = mine
         res.append(jnp.concatenate(outs, axis=1))
-        x, y, z, damp = (whole_coef(q, J + 1) for q in range(4))
-        y_before = whole_coef(1, J)
-        x_left = jnp.where(wide == 0, 0.0, rolled(x, 1, 1))
-        z_top = jnp.where(level_k == 7, 0.0, z)
-        z_low = rolled(z_top, 1, 0)
-        total = x_left + x + y_before + y + z_low + z_top + damp
-        at = e * 8 + J - 2
-        valid = jnp.logical_and(at >= 0, at < 8 * GY)
-        total = jnp.where(valid, total, 1.0)
-        diag.append(total)
-        weight.append(jnp.where(valid, RELAX / total, 0.0))
-        cxl.append(x_left)
-        cxi.append(jnp.where(wide == 4 * NI - 1, 0.0, x))
-        cyl.append(y_before)
-        cyr.append(y)
-        czl.append(z_low)
-        czt.append(z_top)
-    cor = {J: weight[J] * res[J] for J in range(12)}
+    cor = {J: scale(J) * res[J] for J in range(12)}
     for low, high in ((1, 11), (2, 10)):
         new = {}
         for J in range(low, high):
             v = cor[J]
+            z_top = at(z_all, J)
             applied = (
-                diag[J] * v
-                - cxl[J] * rolled(v, 1, 1)
-                - cxi[J] * rolled(v, -1, 1)
-                - cyl[J] * cor[J - 1]
-                - cyr[J] * cor[J + 1]
-                - (czl[J] * rolled(v, 1, 0) + czt[J] * rolled(v, -1, 0))
+                diag(J) * v
+                - at(x_low, J) * rolled(v, 1, 1)
+                - at(x_up, J) * rolled(v, -1, 1)
+                - at(y_all, J) * cor[J - 1]
+                - at(y_all, J + 1) * cor[J + 1]
+                - (rolled(z_top * v, 1, 0) + z_top * rolled(v, -1, 0))
             )
-            new[J] = v + weight[J] * (res[J] - applied)
+            new[J] = v + scale(J) * (res[J] - applied)
         cor = new
     for J in range(8):
         for m in range(4):
@@ -577,28 +579,27 @@
     return lax.all_to_all(many, axis, split_axis=0, concat_axis=0, tiled=True)
 
 
+def swap(near, far):
+    pairs = [(n, n ^ 1) for n in range(GY)]
+    others = [(n, (n + 1) % GY if n % 2 else (n - 1) % GY) for n in range(GY)]
+    return lax.ppermute(near, "gy", pairs), lax.ppermute(far, "gy", others)
+
+
 def body(forcing, pressure_in, x_coupling, y_coupling, z_coupling, damping):
     args = [v.reshape(ROWS, NI) for v in (forcing, pressure_in, x_coupling, y_coupling, z_coupling, damping)]
-    forth = [(n, n + 1) for n in range(GY - 1)]
-    back = [(n + 1, n) for n in range(GY - 1)]
     whole = sds(ROWS, NI)
     kept = sds((2 * len(STEPS) + 1) * ROWS, NI)
-    xs, up, down, coef = call(
+    xs, near, far, coef = call(
         first_kernel,
-        [sds(6 * ROWS, NI), sds(80, NI), sds(48, NI), sds(128, NI)],
-        *args,
+        [sds(6 * ROWS, NI), sds(80, NI), sds(80, NI), sds(128, NI)],
+        *[pltpu.with_memory_space_constraint(v, pltpu.HBM) for v in args],
         scratch=[(128, NI)],
         hbm=True,
         sems=6,
     )
-    below = lax.ppermute(up, "gy", forth)
-    above = lax.ppermute(down, "gy", back)
-    g, a, b, mult, packed = call(x_first_kernel, [whole, whole, whole, kept, sds(NJ, NI)], xs, flops=10**8)
-    g, a, b, mult, send = call(
-        x_rim_kernel,
-        [whole, whole, whole, kept, sds(NJ + 208, NI)],
-        xs, below, above, coef, packed, g, a, b, mult,
-        aliases={5: 0, 6: 1, 7: 2, 8: 3},
+    near, far = swap(near, far)
+    below, g, a, b, mult, send = call(
+        x_first_kernel, [sds(NK, NI), whole, whole, whole, kept, sds(NJ + 208, NI)], xs, near, far, coef
     )
     got_coef = got = spread(send, "gx", GX)
     yg, ya, yb, yw, yinv, xred, cl, send = call(
@@ -622,18 +623,20 @@
         scratch=[(GX + 1, NJ, NI), (ROWS, NI), (ROWS, NI)],
     )
     got = spread(send, "gy", GY)
-    field, coarse = call(
+    field, near, far, coarse = call(
         residual_kernel,
-        [whole, sds(64, NI)],
+        [whole, sds(16, NI), sds(16, NI), sds(64, NI)],
         xs, below, got, yg, ya, yb, yred, cl,
         scratch=[(GY + 1, NK, NI), (ROWS, NI), (128, NI)],
     )
-    lower = lax.ppermute(coarse[48:], "gy", forth)
-    upper = lax.ppermute(coarse[:16], "gy", back)
-    got = spread(jnp.concatenate([lower, coarse, upper], axis=0), "gx", GX)
-    res, cor = call(
-        coarse_kernel, [sds(64, 64), sds(64, 512)], got, got_coef, scratch=[(64, NI), (4, 64, NI)]
-    )
+    near, far = swap(near, far)
+    rows = sds(96, 4 * NI)
+    matrix = call(
+        coarse_matrix_kernel, [sds(2, 96, 4 * NI), rows, rows, sds(104, 4 * NI), rows], got_coef, flops=10**7
+    )
+    (send,) = call(join_kernel, [sds(96, NI)], near, far, coarse)
+    got = spread(send, "gx", GX)
+    res, cor = call(coarse_kernel, [sds(64, 64), sds(64, 512)], got, *matrix, scratch=[(64, NI), (4, 64, NI)])
     return field.reshape(NK, NJ, NI), res.reshape(8, 8, 64), cor.reshape(8, 8, 512)
 
 

time: 103 us -> 97.1 us (0.943)
  the two profiles are of different devices: /device:TPU:1 before, /device:TPU:0 now
where the time goes in v3:
time: 97.1 us; the launch traced here: 96.7 us
  blocking collectives  60.7 us (63%)
  waiting for transfers between devices  14.9 us (15%)
  Pallas kernels  11.3 us (12%)
  starting transfers between devices  8.33 us (9%)
    all_to_all x4, blocking collectives, spread(): return lax.all_to_all(many, axis, split_axis=0, concat_axis=0, tiled=True)  60.7 us
    pallas_call x9, Pallas kernels, call(): pl.pallas_call(kernel, out_shape=outs, in_specs=[inside] * len(args), out...  11.3 us
    all_to_all x1, waiting for transfers between devices, spread(): return lax.all_to_all(many, axis, split_axis=0, concat_axis=0, tiled=True)  8.74 us
    ppermute x4, waiting for transfers between devices, swap(): return (lax.ppermute(near, 'gy', pairs), lax.ppermute(far, 'gy', others))  6.12 us
    ppermute x4, starting transfers between devices, swap(): return (lax.ppermute(near, 'gy', pairs), lax.ppermute(far, 'gy', others))  4.88 us
    all_to_all x1, starting transfers between devices, spread(): return lax.all_to_all(many, axis, split_axis=0, concat_axis=0, tiled=True)  3.45 us
  transfers between devices with their start and end apart: 5, of which 4 were waited for; matrix products, arithmetic and copies ran while one was open for 0% of the time, Pallas kernels for 1%

profile of v3, /device:TPU:0, one launch (start us, length us, event | category | flops | bytes accessed | tf_op | source)
XLA Modules:
  0.0 96.7 jit_solution(8954486134389354459)
XLA Ops:
  0.6 1.7 %shard_map.85 = (f32[1536,128]{1,0:T(8,128)S(1)}, f32[80,128]{1,0:T(8,128)S(1)}, f32[80,128]{1,0:T(8,128)S(1)}, f32[128,128]{1,0:T(8,128)S(1)}) custom-call(f32[256,128]{1,0:T(8,128)} %bitcast.9, f32[256,128]{1,0:T(8,128)} %bitcast.10, f32[256,128]{1,0:T(8,128)} %bitcast.11, f32[256,128]{1,0:T(8,128)} %bitcast.12, f32[256,128]{1,0:T(8,128)} %bitcast.13, ...), custom_call_target="tpu_custom_call" | custom-call | tf_op jit(solution)/shard_map/pallas_call | solution.py:29
  2.3 0.1 collective-permute-start
  2.4 4.0 %collective-permute-start.1 = (f32[80,128]{1,0:T(8,128)S(1)}, f32[80,128]{1,0:T(8,128)S(1)}, u32[]{:S(2)}, u32[]{:S(2)}) collective-permute-start(f32[80,128]{1,0:T(8,128)S(1)} %get-tuple-element.39), channel_id=1, source_target_pairs={{0,15},{1,2},{2,1},{3,4},{4,3},{5,6},{6,5},{7,8},{8,7},{9,10},{10,... | collective-permute-start | bytes 122888 | tf_op jit(solution)/shard_map/ppermute | solution.py:585
  6.4 0.0 collective-permute-done.near
  6.4 1.7 %collective-permute-done.1.far = f32[80,128]{1,0:T(8,128)S(1)} collective-permute-done((f32[80,128]{1,0:T(8,128)S(1)}, f32[80,128]{1,0:T(8,128)S(1)}, u32[]{:S(2)}, u32[]{:S(2)}) %collective-permute-start.1) | collective-permute-done | bytes 40992 | tf_op jit(solution)/shard_map/ppermute | solution.py:585
  8.0 4.9 %shard_map.86 = (f32[16,128]{1,0:T(8,128)S(1)}, f32[256,128]{1,0:T(8,128)S(1)}, f32[256,128]{1,0:T(8,128)S(1)}, f32[256,128]{1,0:T(8,128)S(1)}, f32[3840,128]{1,0:T(8,128)S(1)}, /*index=5*/f32[224,128]{1,0:T(8,128)S(1)}) custom-call(f32[1536,128]{1,0:T(8,128)S(1)} %get-tuple-element.37.xs, f32[80,128]{1,0:T(8,128)S(1)} %collective-permute-done.near, ...), custom_call_target="tpu_custom_call" | custom-call | tf_op jit(solution)/shard_map/pallas_call | solution.py:29
  12.9 0.1 broadcast_in_dim.10
  13.0 22.2 %all_to_all.25.got.coef = f32[8,224,128]{2,1,0:T(8,128)S(1)} all-to-all(f32[8,224,128]{2,1,0:T(8,128)S(1)} %broadcast_in_dim.10), channel_id=1, replica_groups=mesh['gx'=8,'gy'=16] {'gx'}, dimensions={0} | all-to-all | bytes 1835008 | tf_op jit(solution)/shard_map/all_to_all | solution.py:579
  35.2 0.6 shard_map.87
  35.9 17.1 %all_to_all.26.got = f32[16,80,128]{2,1,0:T(8,128)S(1)} all-to-all(f32[16,80,128]{2,1,0:T(8,128)S(1)} %broadcast_in_dim.11), channel_id=1, replica_groups=mesh['gx'=8,'gy'=16] {'gy'}, dimensions={0} | all-to-all | bytes 1310720 | tf_op jit(solution)/shard_map/all_to_all | solution.py:579
  53.0 1.0 %shard_map.88 = (f32[256,128]{1,0:T(8,128)S(1)}, f32[48,16,128]{2,1,0:T(8,128)S(1)}, f32[16,128]{1,0:T(8,128)S(1)}) custom-call(f32[1536,128]{1,0:T(8,128)S(1)} %get-tuple-element.37.xs, f32[16,128]{1,0:T(8,128)S(1)} %get-tuple-element.41.below, f32[16,80,128]{2,1,0:T(8,128)S(1)} %all_to_all.26.got, f32[256,128]{1,0:T(8,128)S(1)} %get-tuple-element.47.yg, ...), custom_call_target="tpu_custom_call" | custom-call | tf_op jit(solution)/shard_map/pallas_call | solution.py:29
  54.0 11.1 %all_to_all.27.got = f32[8,16,128]{2,1,0:T(8,128)S(1)} all-to-all(f32[8,16,128]{2,1,0:T(8,128)S(1)} %broadcast_in_dim.12), channel_id=1, replica_groups=mesh['gx'=8,'gy'=16] {'gx'}, dimensions={0} | all-to-all | bytes 131072 | tf_op jit(solution)/shard_map/all_to_all | solution.py:579
  65.1 0.5 shard_map.89
  65.6 10.3 %all_to_all.28.got = f32[16,32,128]{2,1,0:T(8,128)S(1)} all-to-all(f32[16,32,128]{2,1,0:T(8,128)S(1)} %broadcast_in_dim.13), channel_id=1, replica_groups=mesh['gx'=8,'gy'=16] {'gy'}, dimensions={0} | all-to-all | bytes 524288 | tf_op jit(solution)/shard_map/all_to_all | solution.py:579
  75.9 1.0 shard_map.90
  76.8 0.1 collective-permute-start.2
  76.9 0.7 collective-permute-start.3
  77.7 0.3 collective-permute-done.2.near
  78.0 4.1 %collective-permute-done.3.far = f32[16,128]{1,0:T(8,128)S(1)} collective-permute-done((f32[16,128]{1,0:T(8,128)S(1)}, f32[16,128]{1,0:T(8,128)S(1)}, u32[]{:S(2)}, u32[]{:S(2)}) %collective-permute-start.3) | collective-permute-done | bytes 8224 | tf_op jit(solution)/shard_map/ppermute | solution.py:585
  82.1 0.8 broadcast_in_dim.14
  82.9 3.5 %all-to-all-start.4 = ((f32[8,96,128]{2,1,0:T(8,128)}), f32[8,96,128]{2,1,0:T(8,128)S(1)}, u32[]{:S(2)}, u32[]{:S(2)}) async-start(f32[8,96,128]{2,1,0:T(8,128)} %broadcast_in_dim.14), calls=%async_computation.4 | async-start | bytes 786432 | tf_op jit(solution)/shard_map/all_to_all | solution.py:579
  86.3 0.7 shard_map.92
  87.0 8.7 %all-to-all-done.4.got = f32[8,96,128]{2,1,0:T(8,128)S(1)} async-done(((f32[8,96,128]{2,1,0:T(8,128)}), f32[8,96,128]{2,1,0:T(8,128)S(1)}, u32[]{:S(2)}, u32[]{:S(2)}) %all-to-all-start.4) | async-done | bytes 393248 | tf_op jit(solution)/shard_map/all_to_all | solution.py:579
  95.8 1.0 %shard_map.93 = (f32[64,64]{1,0:T(8,128)}, f32[64,512]{1,0:T(8,128)}) custom-call(f32[8,96,128]{2,1,0:T(8,128)S(1)} %all-to-all-done.4.got, f32[2,96,512]{2,1,0:T(8,128)S(1)} %get-tuple-element.64.weight, f32[96,512]{1,0:T(8,128)S(1)} %get-tuple-element.65.x_low, f32[96,512]{1,0:T(8,128)S(1)} %get-tuple-element.66.x_up, ...), custom_call_target="tpu_custom_call" | custom-call | tf_op jit(solution)/shard_map/pallas_call | solution.py:29
  (4 shorter events, 0.1 us)
Async XLA Ops:
  2.3 4.1 %collective-permute-start = (f32[80,128]{1,0:T(8,128)S(1)}, f32[80,128]{1,0:T(8,128)S(1)}, u32[]{:S(2)}, u32[]{:S(2)}) collective-permute-start(f32[80,128]{1,0:T(8,128)S(1)} %get-tuple-element.38), channel_id=1, source_target_pairs={{0,1},{1,0},{2,3},{3,2},{4,5},{5,4},{6,7},{7,6},{8,9},{9,8},{10,11... | collective-permute-start | bytes 122888 | tf_op jit(solution)/shard_map/ppermute | solution.py:585
  2.4 5.6 %collective-permute-start.1 = (f32[80,128]{1,0:T(8,128)S(1)}, f32[80,128]{1,0:T(8,128)S(1)}, u32[]{:S(2)}, u32[]{:S(2)}) collective-permute-start(f32[80,128]{1,0:T(8,128)S(1)} %get-tuple-element.39), channel_id=1, source_target_pairs={{0,15},{1,2},{2,1},{3,4},{4,3},{5,6},{6,5},{7,8},{8,7},{9,10},{10,... | collective-permute-start | bytes 122888 | tf_op jit(solution)/shard_map/ppermute | solution.py:585
  76.8 1.2 %collective-permute-start.2 = (f32[16,128]{1,0:T(8,128)S(1)}, f32[16,128]{1,0:T(8,128)S(1)}, u32[]{:S(2)}, u32[]{:S(2)}) collective-permute-start(f32[16,128]{1,0:T(8,128)S(1)} %get-tuple-element.61), channel_id=1, source_target_pairs={{0,1},{1,0},{2,3},{3,2},{4,5},{5,4},{6,7},{7,6},{8,9},{9,8},{10,11... | collective-permute-start | bytes 24584 | tf_op jit(solution)/shard_map/ppermute | solution.py:585
  76.9 5.2 %collective-permute-start.3 = (f32[16,128]{1,0:T(8,128)S(1)}, f32[16,128]{1,0:T(8,128)S(1)}, u32[]{:S(2)}, u32[]{:S(2)}) collective-permute-start(f32[16,128]{1,0:T(8,128)S(1)} %get-tuple-element.62), channel_id=1, source_target_pairs={{0,15},{1,2},{2,1},{3,4},{4,3},{5,6},{6,5},{7,8},{8,7},{9,10},{10,... | collective-permute-start | bytes 24584 | tf_op jit(solution)/shard_map/ppermute | solution.py:585
  82.9 12.9 %all-to-all-start.4 = ((f32[8,96,128]{2,1,0:T(8,128)}), f32[8,96,128]{2,1,0:T(8,128)S(1)}, u32[]{:S(2)}, u32[]{:S(2)}) async-start(f32[8,96,128]{2,1,0:T(8,128)} %broadcast_in_dim.14), calls=%async_computation.4 | async-start | bytes 786432 | tf_op jit(solution)/shard_map/all_to_all | solution.py:579

commit v4 on v3

--- a/solution.py
+++ b/solution.py
@@ -188,26 +188,22 @@
     return column(g, 0), column(g, NI - 1), column(a, 0), column(b, 0), column(b, NI - 1), column(x, NI - 1)
 
 
-def x_first_kernel(xs, near, far, coarse, below, g, a, b, mult, send):
+def x_first_kernel(xs, g, a, b, mult, packed_out):
     f, p, xc, yc, zc, dp = parts(xs)
     lane = lanes(NJ)
     row = lax.broadcasted_iota(jnp.int32, (NJ, NI), 0)
     packed = jnp.zeros((NJ, NI), F32)
-    p_below, p_above = sorted_out(near, far, pl.ds(0, NK))
-    y_below, _ = sorted_out(near, far, pl.ds(NK, NK))
-    below[...] = y_below
     group = 2
     for k0 in range(0, NK, group):
         diag, off, rhs = [], [], []
         for k in range(k0, k0 + group):
             y, v = level(yc, k), level(p, k)
-            y_left = jnp.where(row == 0, y_below[k : k + 1, :], rolled(y, 1, 0))
+            y_left = jnp.where(row == 0, 0.0, rolled(y, 1, 0))
             matrix = x_matrix(level(xc, k), z_sum(zc, k, y_left + y + level(dp, k)))
             diag.append(matrix[0])
             off.append(matrix[1])
-            before = jnp.where(row == 0, p_below[k : k + 1, :], rolled(v, 1, 0))
-            after = jnp.where(row == NJ - 1, p_above[k : k + 1, :], rolled(v, -1, 0))
-            rhs.append(z_terms(zc, p, k, level(f, k) + y_left * before + y * after))
+            after = jnp.where(row == NJ - 1, 0.0, rolled(v, -1, 0))
+            rhs.append(z_terms(zc, p, k, level(f, k) + y_left * rolled(v, 1, 0) + y * after))
         diag, off, rhs = (jnp.concatenate(v, axis=0) for v in (diag, off, rhs))
         place = pl.ds(k0 * NJ, group * NJ)
 
@@ -220,7 +216,50 @@
             part = slice((k - k0) * NJ, (k - k0 + 1) * NJ)
             for q, pick in enumerate(x_picks(rhs[part], left[part], right[part], level(xc, k))):
                 packed = jnp.where(lane == q * NK + k, pick, packed)
-    send[pl.ds(0, NJ), :] = packed
+    packed_out[...] = packed
+
+
+def x_rim_kernel(xs, near, far, coarse, packed, g_in, a_in, b_in, mult_in, below, g, a, b, mult, send):
+    f, p, xc, yc, zc, dp = parts(xs)
+    lane = lanes(NK)
+    row = lax.broadcasted_iota(jnp.int32, (NK, NI), 0)
+
+    def lifted(j):
+        z, v = across(zc, j), across(p, j)
+        top = jnp.where(row == NK - 1, 0.0, z)
+        low = rolled(top, 1, 0)
+        return low, top, low * rolled(v, 1, 0) + top * rolled(v, -1, 0)
+
+    p_below, p_above = sorted_out(near, far, pl.ds(0, NK))
+    y_left, _ = sorted_out(near, far, pl.ds(NK, NK))
+    below[...] = y_left
+    low, top, z_part = lifted(0)
+    y = across(yc, 0)
+    diag, off = x_matrix(across(xc, 0), low + top + y + y_left + across(dp, 0))
+    rhs = across(f, 0) + y_left * p_below + y * across(p, 1) + z_part
+
+    def keep(n, value):
+        mult[pl.ds(n * ROWS, NK, stride=NJ), :] = value
+
+    rhs, left, right = x_eliminate(diag, off, rhs, keep)
+    first = pl.ds(0, NK, stride=NJ)
+    g[first, :], a[first, :], b[first, :] = rhs, left, right
+    line = jnp.zeros((NK, NI), F32)
+    for q, pick in enumerate(x_picks(rhs, left, right, across(xc, 0))):
+        line = line + jnp.where(lane == q * NK + row, pick, 0.0)
+    line = jnp.sum(line, axis=0, keepdims=True)
+
+    j = NJ - 1
+    _, _, z_part = lifted(j)
+    y = across(yc, j)
+    rhs = across(f, j) + across(yc, j - 1) * across(p, j - 1) + y * p_above + z_part
+    rhs = x_second_solve(rhs, lambda n: mult_in[pl.ds(n * ROWS + j, NK, stride=NJ), :])
+    g[pl.ds(j, NK, stride=NJ), :] = rhs
+    last = jnp.where(lane == row, column(rhs, 0), 0.0) + jnp.where(lane == NK + row, column(rhs, NI - 1), 0.0)
+    last = jnp.sum(last, axis=0, keepdims=True)
+    was = packed[...]
+    was = jnp.where(row == 0, line, was)
+    send[pl.ds(0, NJ), :] = jnp.where(jnp.logical_and(row == NJ - 1, lane < 2 * NK), last, was)
     for q in range(2):
         at = NJ + q * 104
         lower, upper = sorted_out(near, far, pl.ds(2 * NK + q * 24, 24))
@@ -476,7 +515,7 @@
     far[...] = jnp.where(odd, up, down)
 
 
-def join_kernel(near, far, coarse, send):
+def join_kernel(near, far, coarse, matrix, send):
     lower, upper = sorted_out(near, far, pl.ds(0, 16))
     send[pl.ds(0, 16), :] = lower
     send[pl.ds(16, 64), :] = coarse[...]
@@ -598,8 +637,12 @@
         sems=6,
     )
     near, far = swap(near, far)
+    g, a, b, mult, packed = call(x_first_kernel, [whole, whole, whole, kept, sds(NJ, NI)], xs, flops=10**8)
     below, g, a, b, mult, send = call(
-        x_first_kernel, [sds(NK, NI), whole, whole, whole, kept, sds(NJ + 208, NI)], xs, near, far, coef
+        x_rim_kernel,
+        [sds(NK, NI), whole, whole, whole, kept, sds(NJ + 208, NI)],
+        xs, near, far, coef, packed, g, a, b, mult,
+        aliases={5: 1, 6: 2, 7: 3, 8: 4},
     )
     got_coef = got = spread(send, "gx", GX)
     yg, ya, yb, yw, yinv, xred, cl, send = call(
@@ -634,7 +677,7 @@
     matrix = call(
         coarse_matrix_kernel, [sds(2, 96, 4 * NI), rows, rows, sds(104, 4 * NI), rows], got_coef, flops=10**7
     )
-    (send,) = call(join_kernel, [sds(96, NI)], near, far, coarse)
+    (send,) = call(join_kernel, [sds(96, NI)], near, far, coarse, matrix[-1])
     got = spread(send, "gx", GX)
     res, cor = call(coarse_kernel, [sds(64, 64), sds(64, 512)], got, *matrix, scratch=[(64, NI), (4, 64, NI)])
     return field.reshape(NK, NJ, NI), res.reshape(8, 8, 64), cor.reshape(8, 8, 512)

time: 97.1 us -> 93 us (0.958)
  waiting for transfers between devices: 14.9 us -> 3.76 us
  blocking collectives: 60.7 us -> 71.1 us
  starting transfers between devices: 8.33 us -> 4.88 us
    all_to_all x4 -> x5, blocking collectives: 60.7 us -> 71.1 us  [spread(): return lax.all_to_all(many, axis, split_axis=0, concat_axis=0, tiled=True)]
    all_to_all x1 -> x0, waiting for transfers between devices: 8.74 us -> none  [spread(): return lax.all_to_all(many, axis, split_axis=0, concat_axis=0, tiled=True)]
    all_to_all x1 -> x0, starting transfers between devices: 3.45 us -> none  [spread(): return lax.all_to_all(many, axis, split_axis=0, concat_axis=0, tiled=True)]
    ppermute x4, waiting for transfers between devices: 6.12 us -> 3.76 us  [swap(): return (lax.ppermute(near, 'gy', pairs), lax.ppermute(far, 'gy', others))]
    pallas_call x9 -> x10, Pallas kernels: 11.3 us -> 12 us  [call(): pl.pallas_call(kernel, out_shape=outs, in_specs=[inside] * len(args), out...]
  transfers between devices with their start and end apart: 5 -> 4, of which waited for: 4 -> 1; matrix products, arithmetic and copies ran while one was open for 0% -> 0% of each run, Pallas kernels for 1% -> 6%
where the time goes in v4:
time: 93 us; the launch traced here: 92.7 us
  blocking collectives  71.1 us (76%)
  Pallas kernels  12 us (13%)
  starting transfers between devices  4.88 us (5%)
  waiting for transfers between devices  3.76 us (4%)
    all_to_all x5, blocking collectives, spread(): return lax.all_to_all(many, axis, split_axis=0, concat_axis=0, tiled=True)  71.1 us
    pallas_call x10, Pallas kernels, call(): pl.pallas_call(kernel, out_shape=outs, in_specs=[inside] * len(args), out...  12 us
    ppermute x4, starting transfers between devices, swap(): return (lax.ppermute(near, 'gy', pairs), lax.ppermute(far, 'gy', others))  4.88 us
    ppermute x4, waiting for transfers between devices, swap(): return (lax.ppermute(near, 'gy', pairs), lax.ppermute(far, 'gy', others))  3.76 us
  transfers between devices with their start and end apart: 4, of which 1 were waited for; matrix products, arithmetic and copies ran while one was open for 0% of the time, Pallas kernels for 6%

profile of v4, /device:TPU:0, one launch (start us, length us, event | category | flops | bytes accessed | tf_op | source)
XLA Modules:
  0.0 92.7 jit_solution(17078261483092197217)
XLA Ops:
  0.6 1.7 %shard_map.85 = (f32[1536,128]{1,0:T(8,128)S(1)}, f32[80,128]{1,0:T(8,128)S(1)}, f32[80,128]{1,0:T(8,128)S(1)}, f32[128,128]{1,0:T(8,128)S(1)}) custom-call(f32[256,128]{1,0:T(8,128)} %bitcast.9, f32[256,128]{1,0:T(8,128)} %bitcast.10, f32[256,128]{1,0:T(8,128)} %bitcast.11, f32[256,128]{1,0:T(8,128)} %bitcast.12, f32[256,128]{1,0:T(8,128)} %bitcast.13, ...), custom_call_target="tpu_custom_call" | custom-call | tf_op jit(solution)/shard_map/pallas_call | solution.py:29
  2.3 0.1 collective-permute-start
  2.4 4.0 %collective-permute-start.1 = (f32[80,128]{1,0:T(8,128)S(1)}, f32[80,128]{1,0:T(8,128)S(1)}, u32[]{:S(2)}, u32[]{:S(2)}) collective-permute-start(f32[80,128]{1,0:T(8,128)S(1)} %get-tuple-element.44), channel_id=1, source_target_pairs={{0,15},{1,2},{2,1},{3,4},{4,3},{5,6},{6,5},{7,8},{8,7},{9,10},{10,... | collective-permute-start | bytes 122888 | tf_op jit(solution)/shard_map/ppermute | solution.py:624
  6.4 4.9 %shard_map.86 = (f32[256,128]{1,0:T(8,128)S(1)}, f32[256,128]{1,0:T(8,128)S(1)}, f32[256,128]{1,0:T(8,128)S(1)}, f32[3840,128]{1,0:T(8,128)S(1)}, f32[16,128]{1,0:T(8,128)S(1)}) custom-call(f32[1536,128]{1,0:T(8,128)S(1)} %get-tuple-element.42.xs), custom_call_target="tpu_custom_call" | custom-call | flops 100000000 | bytes 1048576 | tf_op jit(solution)/shard_map/pallas_call | solution.py:29
  11.2 0.0 collective-permute-done.near
  11.3 0.0 collective-permute-done.1.far
  11.3 0.8 shard_map.87
  12.1 0.1 broadcast_in_dim.10
  12.1 21.4 %all_to_all.25.got.coef = f32[8,224,128]{2,1,0:T(8,128)S(1)} all-to-all(f32[8,224,128]{2,1,0:T(8,128)S(1)} %broadcast_in_dim.10), channel_id=1, replica_groups=mesh['gx'=8,'gy'=16] {'gx'}, dimensions={0} | all-to-all | bytes 1835008 | tf_op jit(solution)/shard_map/all_to_all | solution.py:618
  33.6 0.6 shard_map.88
  34.2 16.4 %all_to_all.26.got = f32[16,80,128]{2,1,0:T(8,128)S(1)} all-to-all(f32[16,80,128]{2,1,0:T(8,128)S(1)} %broadcast_in_dim.11), channel_id=1, replica_groups=mesh['gx'=8,'gy'=16] {'gy'}, dimensions={0} | all-to-all | bytes 1310720 | tf_op jit(solution)/shard_map/all_to_all | solution.py:618
  50.7 1.0 %shard_map.89 = (f32[256,128]{1,0:T(8,128)S(1)}, f32[48,16,128]{2,1,0:T(8,128)S(1)}, f32[16,128]{1,0:T(8,128)S(1)}) custom-call(f32[1536,128]{1,0:T(8,128)S(1)} %get-tuple-element.42.xs, f32[16,128]{1,0:T(8,128)S(1)} %get-tuple-element.51.below, f32[16,80,128]{2,1,0:T(8,128)S(1)} %all_to_all.26.got, f32[256,128]{1,0:T(8,128)S(1)} %get-tuple-element.57.yg, ...), custom_call_target="tpu_custom_call" | custom-call | tf_op jit(solution)/shard_map/pallas_call | solution.py:29
  51.7 10.9 %all_to_all.27.got = f32[8,16,128]{2,1,0:T(8,128)S(1)} all-to-all(f32[8,16,128]{2,1,0:T(8,128)S(1)} %broadcast_in_dim.12), channel_id=1, replica_groups=mesh['gx'=8,'gy'=16] {'gx'}, dimensions={0} | all-to-all | bytes 131072 | tf_op jit(solution)/shard_map/all_to_all | solution.py:618
  62.6 0.5 shard_map.90
  63.1 10.3 %all_to_all.28.got = f32[16,32,128]{2,1,0:T(8,128)S(1)} all-to-all(f32[16,32,128]{2,1,0:T(8,128)S(1)} %broadcast_in_dim.13), channel_id=1, replica_groups=mesh['gx'=8,'gy'=16] {'gy'}, dimensions={0} | all-to-all | bytes 524288 | tf_op jit(solution)/shard_map/all_to_all | solution.py:618
  73.4 1.0 %shard_map.91 = (f32[256,128]{1,0:T(8,128)}, f32[16,128]{1,0:T(8,128)S(1)}, f32[16,128]{1,0:T(8,128)S(1)}, f32[64,128]{1,0:T(8,128)S(1)}) custom-call(f32[1536,128]{1,0:T(8,128)S(1)} %get-tuple-element.42.xs, f32[16,128]{1,0:T(8,128)S(1)} %get-tuple-element.51.below, f32[16,32,128]{2,1,0:T(8,128)S(1)} %all_to_all.28.got, ...), custom_call_target="tpu_custom_call" | custom-call | tf_op jit(solution)/shard_map/pallas_call | solution.py:29
  74.3 0.1 collective-permute-start.2
  74.4 0.7 collective-permute-start.3
  75.1 0.7 shard_map.92
  75.8 0.0 collective-permute-done.2.near
  75.8 3.7 %collective-permute-done.3.far = f32[16,128]{1,0:T(8,128)S(1)} collective-permute-done((f32[16,128]{1,0:T(8,128)S(1)}, f32[16,128]{1,0:T(8,128)S(1)}, u32[]{:S(2)}, u32[]{:S(2)}) %collective-permute-start.3) | collective-permute-done | bytes 8224 | tf_op jit(solution)/shard_map/ppermute | solution.py:624
  79.6 12.1 %all_to_all.29.got = f32[8,96,128]{2,1,0:T(8,128)S(1)} all-to-all(f32[8,96,128]{2,1,0:T(8,128)S(1)} %broadcast_in_dim.14), channel_id=1, replica_groups=mesh['gx'=8,'gy'=16] {'gx'}, dimensions={0} | all-to-all | bytes 786432 | tf_op jit(solution)/shard_map/all_to_all | solution.py:618
  91.7 1.0 %shard_map.94 = (f32[64,64]{1,0:T(8,128)}, f32[64,512]{1,0:T(8,128)}) custom-call(f32[8,96,128]{2,1,0:T(8,128)S(1)} %all_to_all.29.got, f32[2,96,512]{2,1,0:T(8,128)S(1)} %get-tuple-element.75.weight, f32[96,512]{1,0:T(8,128)S(1)} %get-tuple-element.76.x_low, f32[96,512]{1,0:T(8,128)S(1)} %get-tuple-element.77.x_up, f32[104,512]{1,0:T(8,128)S(1)} %get-tuple-element.78.y_all, ...), custom_call_target="tpu_custom_call" | custom-call | tf_op jit(solution)/shard_map/pallas_call | solution.py:29
  (5 shorter events, 0.1 us)
Async XLA Ops:
  2.3 8.9 %collective-permute-start = (f32[80,128]{1,0:T(8,128)S(1)}, f32[80,128]{1,0:T(8,128)S(1)}, u32[]{:S(2)}, u32[]{:S(2)}) collective-permute-start(f32[80,128]{1,0:T(8,128)S(1)} %get-tuple-element.43), channel_id=1, source_target_pairs={{0,1},{1,0},{2,3},{3,2},{4,5},{5,4},{6,7},{7,6},{8,9},{9,8},{10,11... | collective-permute-start | bytes 122888 | tf_op jit(solution)/shard_map/ppermute | solution.py:624
  2.4 8.8 %collective-permute-start.1 = (f32[80,128]{1,0:T(8,128)S(1)}, f32[80,128]{1,0:T(8,128)S(1)}, u32[]{:S(2)}, u32[]{:S(2)}) collective-permute-start(f32[80,128]{1,0:T(8,128)S(1)} %get-tuple-element.44), channel_id=1, source_target_pairs={{0,15},{1,2},{2,1},{3,4},{4,3},{5,6},{6,5},{7,8},{8,7},{9,10},{10,... | collective-permute-start | bytes 122888 | tf_op jit(solution)/shard_map/ppermute | solution.py:624
  74.3 1.5 %collective-permute-start.2 = (f32[16,128]{1,0:T(8,128)S(1)}, f32[16,128]{1,0:T(8,128)S(1)}, u32[]{:S(2)}, u32[]{:S(2)}) collective-permute-start(f32[16,128]{1,0:T(8,128)S(1)} %get-tuple-element.71), channel_id=1, source_target_pairs={{0,1},{1,0},{2,3},{3,2},{4,5},{5,4},{6,7},{7,6},{8,9},{9,8},{10,11... | collective-permute-start | bytes 24584 | tf_op jit(solution)/shard_map/ppermute | solution.py:624
  74.4 5.2 %collective-permute-start.3 = (f32[16,128]{1,0:T(8,128)S(1)}, f32[16,128]{1,0:T(8,128)S(1)}, u32[]{:S(2)}, u32[]{:S(2)}) collective-permute-start(f32[16,128]{1,0:T(8,128)S(1)} %get-tuple-element.72), channel_id=1, source_target_pairs={{0,15},{1,2},{2,1},{3,4},{4,3},{5,6},{6,5},{7,8},{8,7},{9,10},{10,... | collective-permute-start | bytes 24584 | tf_op jit(solution)/shard_map/ppermute | solution.py:624

commit v5 on v4

--- a/solution.py
+++ b/solution.py
@@ -114,24 +114,17 @@
         out[pl.ds(base + J * 8, 8), :] = across(tmp, 2 * J, 8) + across(tmp, 2 * J + 1, 8)
 
 
-def first_kernel(fh, ph, xh, yh, zh, dh, xs, near, far, coarse, tmp, sems):
-    copies = [
-        pltpu.make_async_copy(ref, xs.at[pl.ds(n * ROWS, ROWS), :], sems.at[n])
+def first_kernel(fh, ph, xh, yh, zh, dh, xs, near, far, tmp, sems):
+    copies = {
+        n: pltpu.make_async_copy(ref, xs.at[pl.ds(n * ROWS, ROWS), :], sems.at[n])
         for n, ref in enumerate((fh, ph, xh, yh, zh, dh))
-    ]
-    for copy in copies:
-        copy.start()
-    for copy in copies:
-        copy.wait()
+    }
+    for n in (1, 3, 0, 2, 4, 5):
+        copies[n].start()
+    copies[1].wait()
+    copies[3].wait()
     f, p, xc, yc, zc, dp = parts(xs)
     odd = lax.rem(lax.axis_index("gy"), 2) == 1
-    for q, two in enumerate(((xc, yc), (zc, dp))):
-        total = jnp.zeros((128, NI), F32)
-        for half, ref in enumerate(two):
-            pairs = jnp.concatenate([level(ref, 2 * K) + level(ref, 2 * K + 1) for K in range(NK // 2)], axis=0)
-            total = total + squeeze(pairs, start=64 * half)
-        tmp[...] = total
-        store_coarse(coarse, q * 64, tmp)
 
     def put(place, up, down):
         near[place, :] = jnp.where(odd, down, up)
@@ -139,8 +132,11 @@
 
     put(pl.ds(0, NK), across(p, NJ - 1), across(p, 0))
     put(pl.ds(NK, NK), across(yc, NJ - 1), across(yc, 0))
-    for q in range(2):
-        put(pl.ds(2 * NK + q * 24, 24), coarse[pl.ds(q * 64 + 40, 24), :], coarse[pl.ds(q * 64, 24), :])
+    tmp[...] = squeeze(across(yc, NJ - 2) + across(yc, NJ - 1))
+    row = tmp[pl.ds(0, 8, stride=2), :] + tmp[pl.ds(1, 8, stride=2), :]
+    put(pl.ds(2 * NK, 8), row, row)
+    for n in (0, 2, 4, 5):
+        copies[n].wait()
 
 
 def sorted_out(near, far, place):
@@ -188,7 +184,7 @@
     return column(g, 0), column(g, NI - 1), column(a, 0), column(b, 0), column(b, NI - 1), column(x, NI - 1)
 
 
-def x_first_kernel(xs, g, a, b, mult, packed_out):
+def x_first_kernel(xs, g, a, b, mult, packed_out, coarse, tmp):
     f, p, xc, yc, zc, dp = parts(xs)
     lane = lanes(NJ)
     row = lax.broadcasted_iota(jnp.int32, (NJ, NI), 0)
@@ -217,6 +213,13 @@
             for q, pick in enumerate(x_picks(rhs[part], left[part], right[part], level(xc, k))):
                 packed = jnp.where(lane == q * NK + k, pick, packed)
     packed_out[...] = packed
+    for q, two in enumerate(((xc, yc), (zc, dp))):
+        total = jnp.zeros((128, NI), F32)
+        for half, ref in enumerate(two):
+            pairs = jnp.concatenate([level(ref, 2 * K) + level(ref, 2 * K + 1) for K in range(NK // 2)], axis=0)
+            total = total + squeeze(pairs, start=64 * half)
+        tmp[...] = total
+        store_coarse(coarse, q * 64, tmp)
 
 
 def x_rim_kernel(xs, near, far, coarse, packed, g_in, a_in, b_in, mult_in, below, g, a, b, mult, send):
@@ -260,12 +263,8 @@
     was = packed[...]
     was = jnp.where(row == 0, line, was)
     send[pl.ds(0, NJ), :] = jnp.where(jnp.logical_and(row == NJ - 1, lane < 2 * NK), last, was)
-    for q in range(2):
-        at = NJ + q * 104
-        lower, upper = sorted_out(near, far, pl.ds(2 * NK + q * 24, 24))
-        send[pl.ds(at, 24), :] = lower
-        send[pl.ds(at + 24, 64), :] = coarse[pl.ds(q * 64, 64), :]
-        send[pl.ds(at + 88, 16), :] = upper[:16]
+    send[pl.ds(NJ, 128), :] = coarse[...]
+    send[pl.ds(NJ + 128, 8), :] = sorted_out(near, far, pl.ds(2 * NK, 8))[0]
 
 
 def x_second_solve(rhs, kept):
@@ -406,9 +405,14 @@
         terms[pl.ds(j, NK, stride=NJ), :] = before + after
 
 
-def x_again_kernel(xs, below, got, yg, ya, yb, mult, g, yred, send, fs, field, terms):
+def x_again_kernel(xs, below, mine, other, yg, ya, yb, mult, w, g, yred, send, fs, field, terms):
     f, p, xc, yc, zc, dp = parts(xs)
-    part = lambda n, q: got[n, pl.ds(q * NK, NK), :]
+    odd = lax.rem(lax.axis_index("gy"), 2) == 1
+
+    def part(n, q):
+        one, two = mine[n // 2, pl.ds(q * NK, NK), :], other[n // 2, pl.ds(q * NK, NK), :]
+        return jnp.where(odd, one, two) if n % 2 else jnp.where(odd, two, one)
+
     prev = None
     for n in range(GY - 1):
         dd = part(n, 4) + part(n + 1, 2)
@@ -481,7 +485,7 @@
     send[pl.ds(0, NK), :] = value
 
 
-def residual_kernel(xs, below, got, yg, ya, yb, yred, cl, field, near, far, coarse, fs, terms, tmp):
+def residual_kernel(xs, below, got, yg, ya, yb, yred, cl, field, coarse, fs, terms, tmp):
     f, p, xc, yc, zc, dp = parts(xs)
     d = lax.axis_index("gx")
     lane = lanes(NJ)
@@ -509,62 +513,60 @@
     outer = jnp.concatenate([rim[2 * K] + rim[2 * K + 1] for K in range(NK // 2)], axis=0)
     tmp[...] = parity_shift(squeeze(pairs) + edges(outer))
     store_coarse(coarse, 0, tmp)
-    odd = lax.rem(lax.axis_index("gy"), 2) == 1
-    up, down = coarse[pl.ds(48, 16), :], coarse[pl.ds(0, 16), :]
-    near[...] = jnp.where(odd, down, up)
-    far[...] = jnp.where(odd, up, down)
-
-
-def join_kernel(near, far, coarse, matrix, send):
-    lower, upper = sorted_out(near, far, pl.ds(0, 16))
-    send[pl.ds(0, 16), :] = lower
-    send[pl.ds(16, 64), :] = coarse[...]
-    send[pl.ds(80, 16), :] = upper
-
-
-def coarse_matrix_kernel(coef, weight_out, x_low_out, x_up_out, y_out, z_out):
-    e = lax.axis_index("gy")
+
+
+def coarse_matrix_kernel(coef, w, xl, xu, yl, yu, zl, zu):
     lane = lanes(8)
     wide = lanes(8, 4 * NI)
     level_k = lax.broadcasted_iota(jnp.int32, (8, 4 * NI), 0)
 
-    def whole_coef(q, J):
-        rows = pl.ds(NJ + (q // 2) * 104 + J * 8, 8)
+    def whole(at, half):
+        rows = pl.ds(at, 8)
         outs = []
         for m in range(4):
             even, odd = coef[2 * m, rows, :], coef[2 * m + 1, rows, :]
-            if q % 2:
+            if half:
                 even = rolled(even, 64, 1)
             else:
                 odd = rolled(odd, 64, 1)
             outs.append(jnp.where(lane < 64, even, odd))
         return jnp.concatenate(outs, axis=1)
 
-    y_before = whole_coef(1, 0)
-    y_out[pl.ds(0, 8), :] = y_before
-    for J in range(12):
+    y_before = whole(NJ + 128, 0)
+    for J in range(8):
         rows = pl.ds(J * 8, 8)
-        x, y, z, damp = (whole_coef(q, J + 1) for q in range(4))
+        x, y, z, damp = (whole(NJ + (q // 2) * 64 + J * 8, q % 2) for q in range(4))
         x_left = jnp.where(wide == 0, 0.0, rolled(x, 1, 1))
         z_top = jnp.where(level_k == 7, 0.0, z)
-        total = x_left + x + y_before + y + rolled(z_top, 1, 0) + z_top + damp
-        at = e * 8 + J - 2
-        valid = jnp.logical_and(at >= 0, at < 8 * GY)
-        total = jnp.where(valid, total, 1.0)
-        weight_out[0, rows, :] = total
-        weight_out[1, rows, :] = jnp.where(valid, RELAX / total, 0.0)
-        x_low_out[rows, :] = x_left
-        x_up_out[rows, :] = jnp.where(wide == 4 * NI - 1, 0.0, x)
-        y_out[pl.ds(J * 8 + 8, 8), :] = y
-        z_out[rows, :] = z_top
+        z_low = rolled(z_top, 1, 0)
+        weight = RELAX / (x_left + x + y_before + y + z_low + z_top + damp)
+        w[rows, :] = weight
+        xl[rows, :] = weight * x_left
+        xu[rows, :] = jnp.where(wide == 4 * NI - 1, 0.0, weight * x)
+        yl[rows, :] = weight * y_before
+        yu[rows, :] = weight * y
+        zl[rows, :] = weight * z_low
+        zu[rows, :] = weight * z_top
         y_before = y
 
 
-def coarse_kernel(got, weight, x_low, x_up, y_all, z_all, res_out, cor_out, tmp, cor_tmp):
+def eight(ref, J):
+    return ref[pl.ds(J * 8, 8), :]
+
+
+def flat_terms(v, J, xl, xu, zl, zu):
+    return (
+        eight(xl, J) * rolled(v, 1, 1)
+        + eight(xu, J) * rolled(v, -1, 1)
+        + eight(zl, J) * rolled(v, 1, 0)
+        + eight(zu, J) * rolled(v, -1, 0)
+    )
+
+
+def coarse_one_kernel(got, w, xl, xu, yl, yu, zl, zu, res_out, c0, c1, near, far, tmp):
     d = lax.axis_index("gx")
     lane = lanes(8)
-
-    def whole_res(J):
+    for J in range(8):
         rows = pl.ds(J * 8, 8)
         outs = []
         for m in range(4):
@@ -574,48 +576,67 @@
             if m < 3:
                 value = value + jnp.where(lane == NI - 1, got[2 * m + 2, rows, :], 0.0)
             outs.append(value)
-        return outs
-
-    at = lambda ref, J: ref[pl.ds(J * 8, 8), :]
-    diag = lambda J: weight[0, pl.ds(J * 8, 8), :]
-    scale = lambda J: weight[1, pl.ds(J * 8, 8), :]
-    res = []
-    for J in range(12):
-        outs = whole_res(J)
-        if 2 <= J < 10:
-            mine = outs[0]
-            for m in range(1, 4):
-                mine = jnp.where(d // 2 == m, outs[m], mine)
-            mine = jnp.where(lax.rem(d, 2) == 1, rolled(mine, 64, 1), mine)
-            tmp[pl.ds(J - 2, 8, stride=8), :] = mine
-        res.append(jnp.concatenate(outs, axis=1))
-    cor = {J: scale(J) * res[J] for J in range(12)}
-    for low, high in ((1, 11), (2, 10)):
-        new = {}
-        for J in range(low, high):
-            v = cor[J]
-            z_top = at(z_all, J)
-            applied = (
-                diag(J) * v
-                - at(x_low, J) * rolled(v, 1, 1)
-                - at(x_up, J) * rolled(v, -1, 1)
-                - at(y_all, J) * cor[J - 1]
-                - at(y_all, J + 1) * cor[J + 1]
-                - (rolled(z_top * v, 1, 0) + z_top * rolled(v, -1, 0))
-            )
-            new[J] = v + scale(J) * (res[J] - applied)
-        cor = new
+        mine = outs[0]
+        for m in range(1, 4):
+            mine = jnp.where(d // 2 == m, outs[m], mine)
+        mine = jnp.where(lax.rem(d, 2) == 1, rolled(mine, 64, 1), mine)
+        tmp[pl.ds(J, 8, stride=8), :] = mine
+        c0[rows, :] = eight(w, J) * jnp.concatenate(outs, axis=1)
     for J in range(8):
+        v = eight(c0, J)
+        new = (2.0 - RELAX) * v + flat_terms(v, J, xl, xu, zl, zu)
+        if J:
+            new = new + eight(yl, J) * eight(c0, J - 1)
+        if J < 7:
+            new = new + eight(yu, J) * eight(c0, J + 1)
+        c1[pl.ds(J * 8, 8), :] = new
+    odd = lax.rem(lax.axis_index("gy"), 2) == 1
+    for n, (up, down) in enumerate(((eight(c0, 7), eight(c0, 0)), (eight(c1, 7), eight(c1, 0)), (eight(yu, 7), eight(yl, 0)))):
+        near[pl.ds(n * 8, 8), :] = jnp.where(odd, down, up)
+        far[pl.ds(n * 8, 8), :] = jnp.where(odd, up, down)
+    res_out[...] = tmp[:, :64]
+
+
+def coarse_two_kernel(c0, c1, xl, xu, yl, yu, zl, zu, c2):
+    for J in range(8):
+        v = eight(c1, J)
+        new = eight(c0, J) + (1.0 - RELAX) * v + flat_terms(v, J, xl, xu, zl, zu)
+        if J:
+            new = new + eight(yl, J) * eight(c1, J - 1)
+        if J < 7:
+            new = new + eight(yu, J) * eight(c1, J + 1)
+        c2[pl.ds(J * 8, 8), :] = new
+
+
+def coarse_three_kernel(near, far, c0, c2, xl, xu, yl, yu, zl, zu, out, tmp):
+    sides = [sorted_out(near, far, pl.ds(n * 8, 8)) for n in range(3)]
+    extra = {}
+    for side, (J, inward, coupling) in enumerate(((0, 1, yl), (7, 6, yu))):
+        their0, their1, weight = (pair[side] for pair in sides)
+        change = eight(coupling, J) * their0
+        beside = their1 + weight * eight(c0, J)
+        extra[J] = (1.0 - RELAX) * change + flat_terms(change, J, xl, xu, zl, zu) + eight(coupling, J) * beside
+        extra[inward] = eight(coupling, inward) * change
+    for J in range(8):
+        new = eight(c2, J)
+        if J in extra:
+            new = new + extra[J]
         for m in range(4):
-            cor_tmp[m, pl.ds(J, 8, stride=8), :] = cor[J + 2][:, m * NI : (m + 1) * NI]
+            tmp[m, pl.ds(J, 8, stride=8), :] = new[:, m * NI : (m + 1) * NI]
     for m in range(4):
-        cor_out[:, pl.ds(m * NI, NI)] = cor_tmp[m]
-    res_out[...] = tmp[:, :64]
+        out[:, pl.ds(m * NI, NI)] = tmp[m]
 
 
 def spread(value, axis, count):
     many = jnp.broadcast_to(value[None], (count,) + value.shape)
     return lax.all_to_all(many, axis, split_axis=0, concat_axis=0, tiled=True)
+
+
+def spread_by_core(value):
+    groups = [list(range(0, GY, 2)), list(range(1, GY, 2))]
+    many = jnp.broadcast_to(value[None], (GY // 2,) + value.shape)
+    mine = lax.all_to_all(many, "gy", split_axis=0, concat_axis=0, tiled=True, axis_index_groups=groups)
+    return mine, lax.ppermute(mine, "gy", [(n, n ^ 1) for n in range(GY)])
 
 
 def swap(near, far):
@@ -628,19 +649,25 @@
     args = [v.reshape(ROWS, NI) for v in (forcing, pressure_in, x_coupling, y_coupling, z_coupling, damping)]
     whole = sds(ROWS, NI)
     kept = sds((2 * len(STEPS) + 1) * ROWS, NI)
-    xs, near, far, coef = call(
+    xs, near, far = call(
         first_kernel,
-        [sds(6 * ROWS, NI), sds(80, NI), sds(80, NI), sds(128, NI)],
+        [sds(6 * ROWS, NI), sds(40, NI), sds(40, NI)],
         *[pltpu.with_memory_space_constraint(v, pltpu.HBM) for v in args],
-        scratch=[(128, NI)],
+        scratch=[(NK, NI)],
         hbm=True,
         sems=6,
     )
     near, far = swap(near, far)
-    g, a, b, mult, packed = call(x_first_kernel, [whole, whole, whole, kept, sds(NJ, NI)], xs, flops=10**8)
+    g, a, b, mult, packed, coef = call(
+        x_first_kernel,
+        [whole, whole, whole, kept, sds(NJ, NI), sds(128, NI)],
+        xs,
+        scratch=[(128, NI)],
+        flops=10**8,
+    )
     below, g, a, b, mult, send = call(
         x_rim_kernel,
-        [sds(NK, NI), whole, whole, whole, kept, sds(NJ + 208, NI)],
+        [sds(NK, NI), whole, whole, whole, kept, sds(NJ + 136, NI)],
         xs, near, far, coef, packed, g, a, b, mult,
         aliases={5: 1, 6: 2, 7: 3, 8: 4},
     )
@@ -651,11 +678,13 @@
         xs, got, g, a, b,
         scratch=[(GX + 1, NJ, NI), (GX + 1, NJ, NI), (ROWS, NI), (ROWS, NI), (ROWS, NI)],
     )
-    got = spread(send, "gy", GY)
+    got = spread_by_core(send)
+    rows = sds(64, 4 * NI)
+    w, *matrix = call(coarse_matrix_kernel, [rows] * 7, got_coef, flops=10**7)
     g, yred, send = call(
         x_again_kernel,
         [whole, sds(3 * GY, NK, NI), sds(NJ, NI)],
-        xs, below, got, yg, ya, yb, mult,
+        xs, below, *got, yg, ya, yb, mult, w,
         scratch=[(GY + 1, NK, NI), (ROWS, NI), (ROWS, NI)],
     )
     got = spread(send, "gx", GX)
@@ -666,20 +695,22 @@
         scratch=[(GX + 1, NJ, NI), (ROWS, NI), (ROWS, NI)],
     )
     got = spread(send, "gy", GY)
-    field, near, far, coarse = call(
+    field, coarse = call(
         residual_kernel,
-        [whole, sds(16, NI), sds(16, NI), sds(64, NI)],
+        [whole, sds(64, NI)],
         xs, below, got, yg, ya, yb, yred, cl,
         scratch=[(GY + 1, NK, NI), (ROWS, NI), (128, NI)],
     )
+    got = spread(coarse, "gx", GX)
+    res, c0, c1, near, far = call(
+        coarse_one_kernel,
+        [sds(64, 64), rows, rows, sds(24, 4 * NI), sds(24, 4 * NI)],
+        got, w, *matrix,
+        scratch=[(64, NI)],
+    )
     near, far = swap(near, far)
-    rows = sds(96, 4 * NI)
-    matrix = call(
-        coarse_matrix_kernel, [sds(2, 96, 4 * NI), rows, rows, sds(104, 4 * NI), rows], got_coef, flops=10**7
-    )
-    (send,) = call(join_kernel, [sds(96, NI)], near, far, coarse, matrix[-1])
-    got = spread(send, "gx", GX)
-    res, cor = call(coarse_kernel, [sds(64, 64), sds(64, 512)], got, *matrix, scratch=[(64, NI), (4, 64, NI)])
+    (c2,) = call(coarse_two_kernel, [rows], c0, c1, *matrix, flops=10**7)
+    (cor,) = call(coarse_three_kernel, [sds(64, 4 * NI)], near, far, c0, c2, *matrix, scratch=[(4, 64, NI)])
     return field.reshape(NK, NJ, NI), res.reshape(8, 8, 64), cor.reshape(8, 8, 512)
 
 

time: 93 us -> 87.3 us (0.939)
  blocking collectives: 71.1 us -> 63.4 us
  waiting for transfers between devices: 3.76 us -> 5.44 us
    all_to_all x5 -> x4, blocking collectives: 71.1 us -> 51.5 us  [spread(): return lax.all_to_all(many, axis, split_axis=0, concat_axis=0, tiled=True)]
    all_to_all x0 -> x1, blocking collectives: none -> 12 us  [spread_by_core(): lax.all_to_all(many, 'gy', split_axis=0, concat_axis=0, tiled=True, axis_...]
    ppermute x0 -> x1, waiting for transfers between devices: none -> 1.22 us  [spread_by_core(): return (mine, lax.ppermute(mine, 'gy', [(n, n ^ 1) for n in range(GY)]))]
    pallas_call x10 -> x11, Pallas kernels: 12 us -> 12 us  [call(): pl.pallas_call(kernel, out_shape=outs, in_specs=[inside] * len(args), out...]
  transfers between devices with their start and end apart: 4 -> 5, of which waited for: 1 -> 2; matrix products, arithmetic and copies ran while one was open for 0% -> 0% of each run, Pallas kernels for 6% -> 6%
where the time goes in v5:
time: 87.3 us; the launch traced here: 87 us
  blocking collectives  63.4 us (73%)
  Pallas kernels  12 us (14%)
  waiting for transfers between devices  5.44 us (6%)
  starting transfers between devices  5.3 us (6%)
    all_to_all x4, blocking collectives, spread(): return lax.all_to_all(many, axis, split_axis=0, concat_axis=0, tiled=True)  51.5 us
    pallas_call x11, Pallas kernels, call(): pl.pallas_call(kernel, out_shape=outs, in_specs=[inside] * len(args), out...  12 us
    all_to_all x1, blocking collectives, spread_by_core(): lax.all_to_all(many, 'gy', split_axis=0, concat_axis=0, tiled=True, axis_...  12 us
    ppermute x4, starting transfers between devices, swap(): return (lax.ppermute(near, 'gy', pairs), lax.ppermute(far, 'gy', others))  5.3 us
    ppermute x4, waiting for transfers between devices, swap(): return (lax.ppermute(near, 'gy', pairs), lax.ppermute(far, 'gy', others))  4.22 us
  transfers between devices with their start and end apart: 5, of which 2 were waited for; matrix products, arithmetic and copies ran while one was open for 0% of the time, Pallas kernels for 6%

profile of v5, /device:TPU:0, one launch (start us, length us, event | category | flops | bytes accessed | tf_op | source)
XLA Modules:
  0.0 87.0 jit_solution(8606953863899195214)
XLA Ops:
  0.6 1.3 %shard_map.85 = (f32[1536,128]{1,0:T(8,128)S(1)}, f32[40,128]{1,0:T(8,128)S(1)}, f32[40,128]{1,0:T(8,128)S(1)}) custom-call(f32[256,128]{1,0:T(8,128)} %bitcast.10, f32[256,128]{1,0:T(8,128)} %bitcast.11, f32[256,128]{1,0:T(8,128)} %bitcast.12, f32[256,128]{1,0:T(8,128)} %bitcast.13, f32[256,128]{1,0:T(8,128)} %bitcast.14, f32[256,128]{1,0:T(8,128)} %bitcast.15), custom_call_target="tpu_custom_call" | custom-call | tf_op jit(solution)/shard_map/pallas_call | solution.py:29
  1.9 0.1 collective-permute-start
  2.0 4.0 %collective-permute-start.1 = (f32[40,128]{1,0:T(8,128)S(1)}, f32[40,128]{1,0:T(8,128)S(1)}, u32[]{:S(2)}, u32[]{:S(2)}) collective-permute-start(f32[40,128]{1,0:T(8,128)S(1)} %get-tuple-element.47), channel_id=1, source_target_pairs={{0,15},{1,2},{2,1},{3,4},{4,3},{5,6},{6,5},{7,8},{8,7},{9,10},{10,... | collective-permute-start | bytes 61448 | tf_op jit(solution)/shard_map/ppermute | solution.py:645
  5.9 4.9 %shard_map.86 = (f32[256,128]{1,0:T(8,128)S(1)}, f32[256,128]{1,0:T(8,128)S(1)}, f32[256,128]{1,0:T(8,128)S(1)}, f32[3840,128]{1,0:T(8,128)S(1)}, f32[16,128]{1,0:T(8,128)S(1)}, /*index=5*/f32[128,128]{1,0:T(8,128)S(1)}) custom-call(f32[1536,128]{1,0:T(8,128)S(1)} %get-tuple-element.45.xs), custom_call_target="tpu_custom_call" | custom-call | flops 100000000 | bytes 1048576 | tf_op jit(solution)/shard_map/pallas_call | solution.py:29
  10.8 0.0 collective-permute-done.near
  10.8 0.0 collective-permute-done.1.far
  10.9 0.8 shard_map.87
  11.7 18.3 %all_to_all.25.got.coef = f32[8,152,128]{2,1,0:T(8,128)S(1)} all-to-all(f32[8,152,128]{2,1,0:T(8,128)S(1)} %broadcast_in_dim.10), channel_id=1, replica_groups=mesh['gx'=8,'gy'=16] {'gx'}, dimensions={0} | all-to-all | bytes 1245184 | tf_op jit(solution)/shard_map/all_to_all | solution.py:632
  30.0 0.6 shard_map.88
  30.7 12.0 %all_to_all.26.mine = f32[8,80,128]{2,1,0:T(8,128)S(1)} all-to-all(f32[8,80,128]{2,1,0:T(8,128)S(1)} %broadcast_in_dim.11), channel_id=1, replica_groups={{0,2,4,6,8,10,12,14},{1,3,5,7,9,11,13,15},{16,18,20,22,24,26,28,30},{17..., dimensions={0} | all-to-all | bytes 655360 | tf_op jit(solution)/shard_map/all_to_all | solution.py:638
  42.6 0.0 collective-permute-start.2
  42.6 0.4 shard_map.89
  43.0 1.2 %collective-permute-done.2.other = f32[8,80,128]{2,1,0:T(8,128)S(1)} collective-permute-done((f32[8,80,128]{2,1,0:T(8,128)S(1)}, f32[8,80,128]{2,1,0:T(8,128)S(1)}, u32[]{:S(2)}, u32[]{:S(2)}) %collective-permute-start.2) | collective-permute-done | bytes 327712 | tf_op jit(solution)/shard_map/ppermute | solution.py:639
  44.3 1.0 %shard_map.90 = (f32[256,128]{1,0:T(8,128)S(1)}, f32[48,16,128]{2,1,0:T(8,128)S(1)}, f32[16,128]{1,0:T(8,128)S(1)}) custom-call(f32[1536,128]{1,0:T(8,128)S(1)} %get-tuple-element.45.xs, f32[16,128]{1,0:T(8,128)S(1)} %get-tuple-element.54.below, f32[8,80,128]{2,1,0:T(8,128)S(1)} %all_to_all.26.mine, f32[8,80,128]{2,1,0:T(8,128)S(1)} %collective-permute-done.2.other, ...), custom_call_target="tpu_custom_call" | custom-call | tf_op jit(solution)/shard_map/pallas_call | solution.py:29
  45.3 11.2 %all_to_all.27.got = f32[8,16,128]{2,1,0:T(8,128)S(1)} all-to-all(f32[8,16,128]{2,1,0:T(8,128)S(1)} %broadcast_in_dim.12), channel_id=1, replica_groups=mesh['gx'=8,'gy'=16] {'gx'}, dimensions={0} | all-to-all | bytes 131072 | tf_op jit(solution)/shard_map/all_to_all | solution.py:632
  56.4 0.5 shard_map.91
  56.9 10.3 %all_to_all.28.got = f32[16,32,128]{2,1,0:T(8,128)S(1)} all-to-all(f32[16,32,128]{2,1,0:T(8,128)S(1)} %broadcast_in_dim.13), channel_id=1, replica_groups=mesh['gx'=8,'gy'=16] {'gy'}, dimensions={0} | all-to-all | bytes 524288 | tf_op jit(solution)/shard_map/all_to_all | solution.py:632
  67.2 0.9 %shard_map.92 = (f32[256,128]{1,0:T(8,128)}, f32[64,128]{1,0:T(8,128)S(1)}) custom-call(f32[1536,128]{1,0:T(8,128)S(1)} %get-tuple-element.45.xs, f32[16,128]{1,0:T(8,128)S(1)} %get-tuple-element.54.below, f32[16,32,128]{2,1,0:T(8,128)S(1)} %all_to_all.28.got, f32[256,128]{1,0:T(8,128)S(1)} %get-tuple-element.72.yg, f32[256,128]{1,0:T(8,128)S(1)} %get-tuple-element.61.ya, ...), custom_call_target="tpu_custom_call" | custom-call | tf_op jit(solution)/shard_map/pallas_call | solution.py:29
  68.2 11.7 %all_to_all.29.got = f32[8,64,128]{2,1,0:T(8,128)S(1)} all-to-all(f32[8,64,128]{2,1,0:T(8,128)S(1)} %broadcast_in_dim.14), channel_id=1, replica_groups=mesh['gx'=8,'gy'=16] {'gx'}, dimensions={0} | all-to-all | bytes 524288 | tf_op jit(solution)/shard_map/all_to_all | solution.py:632
  79.9 0.7 shard_map.93
  80.6 0.0 collective-permute-start.3
  80.6 1.3 %collective-permute-start.4 = (f32[24,512]{1,0:T(8,128)S(1)}, f32[24,512]{1,0:T(8,128)S(1)}, u32[]{:S(2)}, u32[]{:S(2)}) collective-permute-start(f32[24,512]{1,0:T(8,128)S(1)} %get-tuple-element.84), channel_id=1, source_target_pairs={{0,15},{1,2},{2,1},{3,4},{4,3},{5,6},{6,5},{7,8},{8,7},{9,10},{10,... | collective-permute-start | bytes 147464 | tf_op jit(solution)/shard_map/ppermute | solution.py:645
  81.9 0.1 shard_map.94.c2
  82.0 0.0 collective-permute-done.3.near
  82.0 4.2 %collective-permute-done.4.far = f32[24,512]{1,0:T(8,128)S(1)} collective-permute-done((f32[24,512]{1,0:T(8,128)S(1)}, f32[24,512]{1,0:T(8,128)S(1)}, u32[]{:S(2)}, u32[]{:S(2)}) %collective-permute-start.4) | collective-permute-done | bytes 49184 | tf_op jit(solution)/shard_map/ppermute | solution.py:645
  86.2 0.8 shard_map.95
  (5 shorter events, 0.1 us)
Async XLA Ops:
  1.9 8.9 %collective-permute-start = (f32[40,128]{1,0:T(8,128)S(1)}, f32[40,128]{1,0:T(8,128)S(1)}, u32[]{:S(2)}, u32[]{:S(2)}) collective-permute-start(f32[40,128]{1,0:T(8,128)S(1)} %get-tuple-element.46), channel_id=1, source_target_pairs={{0,1},{1,0},{2,3},{3,2},{4,5},{5,4},{6,7},{7,6},{8,9},{9,8},{10,11... | collective-permute-start | bytes 61448 | tf_op jit(solution)/shard_map/ppermute | solution.py:645
  2.0 8.9 %collective-permute-start.1 = (f32[40,128]{1,0:T(8,128)S(1)}, f32[40,128]{1,0:T(8,128)S(1)}, u32[]{:S(2)}, u32[]{:S(2)}) collective-permute-start(f32[40,128]{1,0:T(8,128)S(1)} %get-tuple-element.47), channel_id=1, source_target_pairs={{0,15},{1,2},{2,1},{3,4},{4,3},{5,6},{6,5},{7,8},{8,7},{9,10},{10,... | collective-permute-start | bytes 61448 | tf_op jit(solution)/shard_map/ppermute | solution.py:645
  42.6 1.6 %collective-permute-start.2 = (f32[8,80,128]{2,1,0:T(8,128)S(1)}, f32[8,80,128]{2,1,0:T(8,128)S(1)}, u32[]{:S(2)}, u32[]{:S(2)}) collective-permute-start(f32[8,80,128]{2,1,0:T(8,128)S(1)} %all_to_all.26.mine), channel_id=1, source_target_pairs={{0,1},{1,0},{2,3},{3,2},{4,5},{5,4},{6,7},{7,6},{8,9},{9,8},{10,11... | collective-permute-start | bytes 983048 | tf_op jit(solution)/shard_map/ppermute | solution.py:639
  80.6 1.4 %collective-permute-start.3 = (f32[24,512]{1,0:T(8,128)S(1)}, f32[24,512]{1,0:T(8,128)S(1)}, u32[]{:S(2)}, u32[]{:S(2)}) collective-permute-start(f32[24,512]{1,0:T(8,128)S(1)} %get-tuple-element.83), channel_id=1, source_target_pairs={{0,1},{1,0},{2,3},{3,2},{4,5},{5,4},{6,7},{7,6},{8,9},{9,8},{10,11... | collective-permute-start | bytes 147464 | tf_op jit(solution)/shard_map/ppermute | solution.py:645
  80.6 5.6 %collective-permute-start.4 = (f32[24,512]{1,0:T(8,128)S(1)}, f32[24,512]{1,0:T(8,128)S(1)}, u32[]{:S(2)}, u32[]{:S(2)}) collective-permute-start(f32[24,512]{1,0:T(8,128)S(1)} %get-tuple-element.84), channel_id=1, source_target_pairs={{0,15},{1,2},{2,1},{3,4},{4,3},{5,6},{6,5},{7,8},{8,7},{9,10},{10,... | collective-permute-start | bytes 147464 | tf_op jit(solution)/shard_map/ppermute | solution.py:645

commit v6 on v5

--- a/solution.py
+++ b/solution.py
@@ -19,9 +19,10 @@
     return jax.ShapeDtypeStruct(shape, F32)
 
 
-def call(kernel, outs, *args, scratch=(), hbm=False, aliases={}, sems=0, flops=None):
+def call(kernel, outs, *args, scratch=(), hbm=0, aliases={}, sems=0, flops=None):
     spec = pl.BlockSpec(memory_space=pltpu.VMEM)
-    inside = pl.BlockSpec(memory_space=pltpu.HBM) if hbm else spec
+    outside = pl.BlockSpec(memory_space=pltpu.HBM)
+    args = [pltpu.with_memory_space_constraint(v, pltpu.HBM) for v in args[:hbm]] + list(args[hbm:])
     shapes = [pltpu.VMEM(v, F32) for v in scratch]
     if sems:
         shapes.append(pltpu.SemaphoreType.DMA((sems,)))
@@ -29,7 +30,7 @@
     return pl.pallas_call(
         kernel,
         out_shape=outs,
-        in_specs=[inside] * len(args),
+        in_specs=[outside] * hbm + [spec] * (len(args) - hbm),
         out_specs=[spec] * len(outs),
         scratch_shapes=shapes,
         input_output_aliases=aliases,
@@ -114,29 +115,24 @@
         out[pl.ds(base + J * 8, 8), :] = across(tmp, 2 * J, 8) + across(tmp, 2 * J + 1, 8)
 
 
-def first_kernel(fh, ph, xh, yh, zh, dh, xs, near, far, tmp, sems):
-    copies = {
-        n: pltpu.make_async_copy(ref, xs.at[pl.ds(n * ROWS, ROWS), :], sems.at[n])
-        for n, ref in enumerate((fh, ph, xh, yh, zh, dh))
-    }
-    for n in (1, 3, 0, 2, 4, 5):
-        copies[n].start()
-    copies[1].wait()
-    copies[3].wait()
-    f, p, xc, yc, zc, dp = parts(xs)
+def first_kernel(ph, yh, near, far, rows, tmp, sems):
+    picks = ((ph, NJ - 1), (ph, 0), (yh, NJ - 1), (yh, NJ - 2))
+    copies = [pltpu.make_async_copy(ref.at[:, j, :], rows.at[n], sems.at[n]) for n, (ref, j) in enumerate(picks)]
+    for copy in copies:
+        copy.start()
+    for copy in copies:
+        copy.wait()
     odd = lax.rem(lax.axis_index("gy"), 2) == 1
 
     def put(place, up, down):
         near[place, :] = jnp.where(odd, down, up)
         far[place, :] = jnp.where(odd, up, down)
 
-    put(pl.ds(0, NK), across(p, NJ - 1), across(p, 0))
-    put(pl.ds(NK, NK), across(yc, NJ - 1), across(yc, 0))
-    tmp[...] = squeeze(across(yc, NJ - 2) + across(yc, NJ - 1))
+    put(pl.ds(0, NK), rows[0], rows[1])
+    put(pl.ds(NK, NK), rows[2], rows[2])
+    tmp[...] = squeeze(rows[2] + rows[3])
     row = tmp[pl.ds(0, 8, stride=2), :] + tmp[pl.ds(1, 8, stride=2), :]
     put(pl.ds(2 * NK, 8), row, row)
-    for n in (0, 2, 4, 5):
-        copies[n].wait()
 
 
 def sorted_out(near, far, place):
@@ -184,12 +180,20 @@
     return column(g, 0), column(g, NI - 1), column(a, 0), column(b, 0), column(b, NI - 1), column(x, NI - 1)
 
 
-def x_first_kernel(xs, g, a, b, mult, packed_out, coarse, tmp):
+def x_first_kernel(fh, ph, xh, yh, zh, dh, order, xs, g, a, b, mult, packed_out, coarse, tmp, sems):
+    copies = [
+        pltpu.make_async_copy(ref, xs.at[pl.ds(n * ROWS, ROWS), :], sems.at[n])
+        for n, ref in enumerate((fh, ph, xh, yh, zh, dh))
+    ]
+    for copy in copies:
+        copy.start()
+    for copy in copies:
+        copy.wait()
     f, p, xc, yc, zc, dp = parts(xs)
     lane = lanes(NJ)
     row = lax.broadcasted_iota(jnp.int32, (NJ, NI), 0)
     packed = jnp.zeros((NJ, NI), F32)
-    group = 2
+    group = 8
     for k0 in range(0, NK, group):
         diag, off, rhs = [], [], []
         for k in range(k0, k0 + group):
@@ -485,7 +489,7 @@
     send[pl.ds(0, NK), :] = value
 
 
-def residual_kernel(xs, below, got, yg, ya, yb, yred, cl, field, coarse, fs, terms, tmp):
+def residual_kernel(xs, below, got, yg, ya, yb, yred, cl, fluxes, coarse, fs, terms, tmp, field):
     f, p, xc, yc, zc, dp = parts(xs)
     d = lax.axis_index("gx")
     lane = lanes(NJ)
@@ -497,6 +501,8 @@
         lambda n: yred[GY + n],
         lambda n: yred[2 * GY + n],
     )
+    e = lax.axis_index("gy")
+    fluxes[0], fluxes[1] = fs[e], fs[e + 1]
     y_finish(fs, yc, below, yg, ya, yb, field, terms)
     c_left = cl[...]
     main, rim = [], []
@@ -563,7 +569,7 @@
     )
 
 
-def coarse_one_kernel(got, w, xl, xu, yl, yu, zl, zu, res_out, c0, c1, near, far, tmp):
+def coarse_one_kernel(got, w, xl, xu, yl, yu, zl, zu, tmp, c0, c1, near, far):
     d = lax.axis_index("gx")
     lane = lanes(8)
     for J in range(8):
@@ -594,10 +600,13 @@
     for n, (up, down) in enumerate(((eight(c0, 7), eight(c0, 0)), (eight(c1, 7), eight(c1, 0)), (eight(yu, 7), eight(yl, 0)))):
         near[pl.ds(n * 8, 8), :] = jnp.where(odd, down, up)
         far[pl.ds(n * 8, 8), :] = jnp.where(odd, up, down)
-    res_out[...] = tmp[:, :64]
-
-
-def coarse_two_kernel(c0, c1, xl, xu, yl, yu, zl, zu, c2):
+
+
+def coarse_two_kernel(c0, c1, xl, xu, yl, yu, zl, zu, res, fluxes, yg, ya, yb, c2, res_out, field):
+    res_out[...] = res[:, :64]
+    for j in range(NJ):
+        place = pl.ds(j * NK, NK)
+        field[pl.ds(j, NK, stride=NJ), :] = yg[place, :] - ya[place, :] * fluxes[0] + yb[place, :] * fluxes[1]
     for J in range(8):
         v = eight(c1, J)
         new = eight(c0, J) + (1.0 - RELAX) * v + flat_terms(v, J, xl, xu, zl, zu)
@@ -646,23 +655,25 @@
 
 
 def body(forcing, pressure_in, x_coupling, y_coupling, z_coupling, damping):
-    args = [v.reshape(ROWS, NI) for v in (forcing, pressure_in, x_coupling, y_coupling, z_coupling, damping)]
+    args = (forcing, pressure_in, x_coupling, y_coupling, z_coupling, damping)
     whole = sds(ROWS, NI)
     kept = sds((2 * len(STEPS) + 1) * ROWS, NI)
-    xs, near, far = call(
+    mine = call(
         first_kernel,
-        [sds(6 * ROWS, NI), sds(40, NI), sds(40, NI)],
-        *[pltpu.with_memory_space_constraint(v, pltpu.HBM) for v in args],
-        scratch=[(NK, NI)],
-        hbm=True,
+        [sds(40, NI), sds(40, NI)],
+        pressure_in, y_coupling,
+        scratch=[(4, NK, NI), (NK, NI)],
+        hbm=2,
+        sems=4,
+    )
+    near, far = swap(*mine)
+    xs, g, a, b, mult, packed, coef = call(
+        x_first_kernel,
+        [sds(6 * ROWS, NI), whole, whole, whole, kept, sds(NJ, NI), sds(128, NI)],
+        *[v.reshape(ROWS, NI) for v in args], mine[0],
+        scratch=[(128, NI)],
+        hbm=6,
         sems=6,
-    )
-    near, far = swap(near, far)
-    g, a, b, mult, packed, coef = call(
-        x_first_kernel,
-        [whole, whole, whole, kept, sds(NJ, NI), sds(128, NI)],
-        xs,
-        scratch=[(128, NI)],
         flops=10**8,
     )
     below, g, a, b, mult, send = call(
@@ -695,21 +706,25 @@
         scratch=[(GX + 1, NJ, NI), (ROWS, NI), (ROWS, NI)],
     )
     got = spread(send, "gy", GY)
-    field, coarse = call(
+    fluxes, coarse = call(
         residual_kernel,
-        [whole, sds(64, NI)],
+        [sds(2, NK, NI), sds(64, NI)],
         xs, below, got, yg, ya, yb, yred, cl,
-        scratch=[(GY + 1, NK, NI), (ROWS, NI), (128, NI)],
+        scratch=[(GY + 1, NK, NI), (ROWS, NI), (128, NI), (ROWS, NI)],
     )
     got = spread(coarse, "gx", GX)
     res, c0, c1, near, far = call(
         coarse_one_kernel,
-        [sds(64, 64), rows, rows, sds(24, 4 * NI), sds(24, 4 * NI)],
+        [sds(64, NI), rows, rows, sds(24, 4 * NI), sds(24, 4 * NI)],
         got, w, *matrix,
-        scratch=[(64, NI)],
     )
     near, far = swap(near, far)
-    (c2,) = call(coarse_two_kernel, [rows], c0, c1, *matrix, flops=10**7)
+    c2, res, field = call(
+        coarse_two_kernel,
+        [rows, sds(64, 64), whole],
+        c0, c1, *matrix, res, fluxes, yg, ya, yb,
+        flops=10**7,
+    )
     (cor,) = call(coarse_three_kernel, [sds(64, 4 * NI)], near, far, c0, c2, *matrix, scratch=[(4, 64, NI)])
     return field.reshape(NK, NJ, NI), res.reshape(8, 8, 64), cor.reshape(8, 8, 512)
 

time: 87.3 us -> 85 us (0.974)
  Pallas kernels: 12 us -> 10.4 us
    all_to_all x4, blocking collectives: 51.5 us -> 53.6 us  [spread(): return lax.all_to_all(many, axis, split_axis=0, concat_axis=0, tiled=True)]
    all_to_all x1, blocking collectives: 12 us -> 10.1 us  [spread_by_core(): lax.all_to_all(many, 'gy', split_axis=0, concat_axis=0, tiled=True, axis_...]
    pallas_call x11, Pallas kernels: 12 us -> 10.4 us  [call(): pl.pallas_call(kernel, out_shape=outs, in_specs=[outside] * hbm + [spec]...]
where the time goes in v6:
time: 85 us; the launch traced here: 84.6 us
  blocking collectives  63.7 us (75%)
  Pallas kernels  10.4 us (12%)
  waiting for transfers between devices  4.89 us (6%)
  starting transfers between devices  4.7 us (6%)
    all_to_all x4, blocking collectives, spread(): return lax.all_to_all(many, axis, split_axis=0, concat_axis=0, tiled=True)  53.6 us
    pallas_call x11, Pallas kernels, call(): pl.pallas_call(kernel, out_shape=outs, in_specs=[outside] * hbm + [spec]...  10.4 us
    all_to_all x1, blocking collectives, spread_by_core(): lax.all_to_all(many, 'gy', split_axis=0, concat_axis=0, tiled=True, axis_...  10.1 us
    ppermute x4, starting transfers between devices, swap(): return (lax.ppermute(near, 'gy', pairs), lax.ppermute(far, 'gy', others))  4.7 us
    ppermute x4, waiting for transfers between devices, swap(): return (lax.ppermute(near, 'gy', pairs), lax.ppermute(far, 'gy', others))  3.66 us
  transfers between devices with their start and end apart: 5, of which 2 were waited for; matrix products, arithmetic and copies ran while one was open for 0% of the time, Pallas kernels for 6%

profile of v6, /device:TPU:0, one launch (start us, length us, event | category | flops | bytes accessed | tf_op | source)
XLA Modules:
  0.0 84.6 jit_solution(13470068493816915384)
XLA Ops:
  0.6 1.0 %shard_map.85 = (f32[40,128]{1,0:T(8,128)S(1)}, f32[40,128]{1,0:T(8,128)S(1)}) custom-call(f32[16,16,128]{2,1,0:T(8,128)} %ph.1, f32[16,16,128]{2,1,0:T(8,128)} %yh.1), custom_call_target="tpu_custom_call" | custom-call | tf_op jit(solution)/shard_map/pallas_call | solution.py:30
  1.6 3.4 %collective-permute-start.1 = (f32[40,128]{1,0:T(8,128)S(1)}, f32[40,128]{1,0:T(8,128)S(1)}, u32[]{:S(2)}, u32[]{:S(2)}) collective-permute-start(f32[40,128]{1,0:T(8,128)S(1)} %get-tuple-element.50), channel_id=1, source_target_pairs={{0,15},{1,2},{2,1},{3,4},{4,3},{5,6},{6,5},{7,8},{8,7},{9,10},{10,... | collective-permute-start | bytes 61448 | tf_op jit(solution)/shard_map/ppermute | solution.py:654
  5.0 0.0 collective-permute-start
  5.0 3.8 %shard_map.86 = (f32[1536,128]{1,0:T(8,128)S(1)}, f32[256,128]{1,0:T(8,128)S(1)}, f32[256,128]{1,0:T(8,128)S(1)}, f32[256,128]{1,0:T(8,128)S(1)}, f32[3840,128]{...) custom-call(f32[256,128]{1,0:T(8,128)} %bitcast.11, f32[256,128]{1,0:T(8,128)} %bitcast.9, ...), custom_call_target="tpu_custom_call" | custom-call | flops 100000000 | bytes 1048576 | tf_op jit(solution)/shard_map/pallas_call | solution.py:30
  8.8 0.0 collective-permute-done.1.far
  8.8 0.0 collective-permute-done.near
  8.8 0.8 shard_map.87
  9.7 20.9 %all_to_all.25.got.coef = f32[8,152,128]{2,1,0:T(8,128)S(1)} all-to-all(f32[8,152,128]{2,1,0:T(8,128)S(1)} %broadcast_in_dim.10), channel_id=1, replica_groups=mesh['gx'=8,'gy'=16] {'gx'}, dimensions={0} | all-to-all | bytes 1245184 | tf_op jit(solution)/shard_map/all_to_all | solution.py:641
  30.6 0.6 shard_map.88
  31.2 10.1 %all_to_all.26.mine = f32[8,80,128]{2,1,0:T(8,128)S(1)} all-to-all(f32[8,80,128]{2,1,0:T(8,128)S(1)} %broadcast_in_dim.11), channel_id=1, replica_groups={{0,2,4,6,8,10,12,14},{1,3,5,7,9,11,13,15},{16,18,20,22,24,26,28,30},{17..., dimensions={0} | all-to-all | bytes 655360 | tf_op jit(solution)/shard_map/all_to_all | solution.py:647
  41.3 0.0 collective-permute-start.2
  41.3 0.4 shard_map.89
  41.7 1.2 %collective-permute-done.2.other = f32[8,80,128]{2,1,0:T(8,128)S(1)} collective-permute-done((f32[8,80,128]{2,1,0:T(8,128)S(1)}, f32[8,80,128]{2,1,0:T(8,128)S(1)}, u32[]{:S(2)}, u32[]{:S(2)}) %collective-permute-start.2) | collective-permute-done | bytes 327712 | tf_op jit(solution)/shard_map/ppermute | solution.py:648
  43.0 1.0 %shard_map.90 = (f32[256,128]{1,0:T(8,128)S(1)}, f32[48,16,128]{2,1,0:T(8,128)S(1)}, f32[16,128]{1,0:T(8,128)S(1)}) custom-call(f32[1536,128]{1,0:T(8,128)S(1)} %get-tuple-element.49.xs, f32[16,128]{1,0:T(8,128)S(1)} %get-tuple-element.57.below, f32[8,80,128]{2,1,0:T(8,128)S(1)} %all_to_all.26.mine, f32[8,80,128]{2,1,0:T(8,128)S(1)} %collective-permute-done.2.other, ...), custom_call_target="tpu_custom_call" | custom-call | tf_op jit(solution)/shard_map/pallas_call | solution.py:30
  44.0 10.7 %all_to_all.27.got = f32[8,16,128]{2,1,0:T(8,128)S(1)} all-to-all(f32[8,16,128]{2,1,0:T(8,128)S(1)} %broadcast_in_dim.12), channel_id=1, replica_groups=mesh['gx'=8,'gy'=16] {'gx'}, dimensions={0} | all-to-all | bytes 131072 | tf_op jit(solution)/shard_map/all_to_all | solution.py:641
  54.7 0.5 shard_map.91
  55.2 10.3 %all_to_all.28.got = f32[16,32,128]{2,1,0:T(8,128)S(1)} all-to-all(f32[16,32,128]{2,1,0:T(8,128)S(1)} %broadcast_in_dim.13), channel_id=1, replica_groups=mesh['gx'=8,'gy'=16] {'gy'}, dimensions={0} | all-to-all | bytes 524288 | tf_op jit(solution)/shard_map/all_to_all | solution.py:641
  65.5 0.6 shard_map.92
  66.2 11.7 %all_to_all.29.got = f32[8,64,128]{2,1,0:T(8,128)S(1)} all-to-all(f32[8,64,128]{2,1,0:T(8,128)S(1)} %broadcast_in_dim.14), channel_id=1, replica_groups=mesh['gx'=8,'gy'=16] {'gx'}, dimensions={0} | all-to-all | bytes 524288 | tf_op jit(solution)/shard_map/all_to_all | solution.py:641
  77.9 0.2 shard_map.93
  78.0 0.1 collective-permute-start.3
  78.1 1.2 %collective-permute-start.4 = (f32[24,512]{1,0:T(8,128)S(1)}, f32[24,512]{1,0:T(8,128)S(1)}, u32[]{:S(2)}, u32[]{:S(2)}) collective-permute-start(f32[24,512]{1,0:T(8,128)S(1)} %get-tuple-element.91), channel_id=1, source_target_pairs={{0,15},{1,2},{2,1},{3,4},{4,3},{5,6},{6,5},{7,8},{8,7},{9,10},{10,... | collective-permute-start | bytes 147464 | tf_op jit(solution)/shard_map/ppermute | solution.py:654
  79.4 0.8 shard_map.94
  80.2 0.0 collective-permute-done.3.near
  80.2 3.7 %collective-permute-done.4.far = f32[24,512]{1,0:T(8,128)S(1)} collective-permute-done((f32[24,512]{1,0:T(8,128)S(1)}, f32[24,512]{1,0:T(8,128)S(1)}, u32[]{:S(2)}, u32[]{:S(2)}) %collective-permute-start.4) | collective-permute-done | bytes 49184 | tf_op jit(solution)/shard_map/ppermute | solution.py:654
  83.8 0.8 shard_map.95
  (5 shorter events, 0.1 us)
Async XLA Ops:
  1.6 7.2 %collective-permute-start.1 = (f32[40,128]{1,0:T(8,128)S(1)}, f32[40,128]{1,0:T(8,128)S(1)}, u32[]{:S(2)}, u32[]{:S(2)}) collective-permute-start(f32[40,128]{1,0:T(8,128)S(1)} %get-tuple-element.50), channel_id=1, source_target_pairs={{0,15},{1,2},{2,1},{3,4},{4,3},{5,6},{6,5},{7,8},{8,7},{9,10},{10,... | collective-permute-start | bytes 61448 | tf_op jit(solution)/shard_map/ppermute | solution.py:654
  5.0 3.8 %collective-permute-start = (f32[40,128]{1,0:T(8,128)S(1)}, f32[40,128]{1,0:T(8,128)S(1)}, u32[]{:S(2)}, u32[]{:S(2)}) collective-permute-start(f32[40,128]{1,0:T(8,128)S(1)} %get-tuple-element.48.order), channel_id=1, source_target_pairs={{0,1},{1,0},{2,3},{3,2},{4,5},{5,4},{6,7},{7,6},{8,9},{9,8},{10,11... | collective-permute-start | bytes 61448 | tf_op jit(solution)/shard_map/ppermute | solution.py:654
  41.3 1.6 %collective-permute-start.2 = (f32[8,80,128]{2,1,0:T(8,128)S(1)}, f32[8,80,128]{2,1,0:T(8,128)S(1)}, u32[]{:S(2)}, u32[]{:S(2)}) collective-permute-start(f32[8,80,128]{2,1,0:T(8,128)S(1)} %all_to_all.26.mine), channel_id=1, source_target_pairs={{0,1},{1,0},{2,3},{3,2},{4,5},{5,4},{6,7},{7,6},{8,9},{9,8},{10,11... | collective-permute-start | bytes 983048 | tf_op jit(solution)/shard_map/ppermute | solution.py:648
  78.0 2.1 %collective-permute-start.3 = (f32[24,512]{1,0:T(8,128)S(1)}, f32[24,512]{1,0:T(8,128)S(1)}, u32[]{:S(2)}, u32[]{:S(2)}) collective-permute-start(f32[24,512]{1,0:T(8,128)S(1)} %get-tuple-element.90), channel_id=1, source_target_pairs={{0,1},{1,0},{2,3},{3,2},{4,5},{5,4},{6,7},{7,6},{8,9},{9,8},{10,11... | collective-permute-start | bytes 147464 | tf_op jit(solution)/shard_map/ppermute | solution.py:654
  78.1 5.7 %collective-permute-start.4 = (f32[24,512]{1,0:T(8,128)S(1)}, f32[24,512]{1,0:T(8,128)S(1)}, u32[]{:S(2)}, u32[]{:S(2)}) collective-permute-start(f32[24,512]{1,0:T(8,128)S(1)} %get-tuple-element.91), channel_id=1, source_target_pairs={{0,15},{1,2},{2,1},{3,4},{4,3},{5,6},{6,5},{7,8},{8,7},{9,10},{10,... | collective-permute-start | bytes 147464 | tf_op jit(solution)/shard_map/ppermute | solution.py:654

commit v7 on v4

--- a/solution.py
+++ b/solution.py
@@ -19,9 +19,10 @@
     return jax.ShapeDtypeStruct(shape, F32)
 
 
-def call(kernel, outs, *args, scratch=(), hbm=False, aliases={}, sems=0, flops=None):
+def call(kernel, outs, *args, scratch=(), hbm=0, aliases={}, sems=0, flops=None):
     spec = pl.BlockSpec(memory_space=pltpu.VMEM)
-    inside = pl.BlockSpec(memory_space=pltpu.HBM) if hbm else spec
+    outside = pl.BlockSpec(memory_space=pltpu.HBM)
+    args = [pltpu.with_memory_space_constraint(v, pltpu.HBM) for v in args[:hbm]] + list(args[hbm:])
     shapes = [pltpu.VMEM(v, F32) for v in scratch]
     if sems:
         shapes.append(pltpu.SemaphoreType.DMA((sems,)))
@@ -29,7 +30,7 @@
     return pl.pallas_call(
         kernel,
         out_shape=outs,
-        in_specs=[inside] * len(args),
+        in_specs=[outside] * hbm + [spec] * (len(args) - hbm),
         out_specs=[spec] * len(outs),
         scratch_shapes=shapes,
         input_output_aliases=aliases,
@@ -104,11 +105,6 @@
     return jnp.dot(values, matrix, precision=lax.Precision.HIGHEST, preferred_element_type=F32)
 
 
-def parity_shift(values):
-    odd = lax.rem(lax.axis_index("gx"), 2) == 1
-    return jnp.where(odd, rolled(values, 64, 1), values)
-
-
 def store_coarse(out, base, tmp):
     for J in range(NJ // 2):
         out[pl.ds(base + J * 8, 8), :] = across(tmp, 2 * J, 8) + across(tmp, 2 * J + 1, 8)
@@ -121,7 +117,7 @@
     ]
     for copy in copies:
         copy.start()
-    for copy in copies:
+    for copy in copies[1:]:
         copy.wait()
     f, p, xc, yc, zc, dp = parts(xs)
     odd = lax.rem(lax.axis_index("gy"), 2) == 1
@@ -141,6 +137,7 @@
     put(pl.ds(NK, NK), across(yc, NJ - 1), across(yc, 0))
     for q in range(2):
         put(pl.ds(2 * NK + q * 24, 24), coarse[pl.ds(q * 64 + 40, 24), :], coarse[pl.ds(q * 64, 24), :])
+    copies[0].wait()
 
 
 def sorted_out(near, far, place):
@@ -193,7 +190,7 @@
     lane = lanes(NJ)
     row = lax.broadcasted_iota(jnp.int32, (NJ, NI), 0)
     packed = jnp.zeros((NJ, NI), F32)
-    group = 2
+    group = 8
     for k0 in range(0, NK, group):
         diag, off, rhs = [], [], []
         for k in range(k0, k0 + group):
@@ -219,7 +216,7 @@
     packed_out[...] = packed
 
 
-def x_rim_kernel(xs, near, far, coarse, packed, g_in, a_in, b_in, mult_in, below, g, a, b, mult, send):
+def x_rim_kernel(xs, near, far, coarse, packed, g_in, a_in, b_in, mult_in, below, g, a, b, mult, send, ext):
     f, p, xc, yc, zc, dp = parts(xs)
     lane = lanes(NK)
     row = lax.broadcasted_iota(jnp.int32, (NK, NI), 0)
@@ -260,12 +257,34 @@
     was = packed[...]
     was = jnp.where(row == 0, line, was)
     send[pl.ds(0, NJ), :] = jnp.where(jnp.logical_and(row == NJ - 1, lane < 2 * NK), last, was)
+    coarse_share(near, far, coarse, send, ext)
+
+
+def coarse_share(near, far, coarse, send, ext):
+    wide = lanes(8)
+    level_k = lax.broadcasted_iota(jnp.int32, (8, NI), 0)
+    fields = [[], [], [], []]
     for q in range(2):
-        at = NJ + q * 104
         lower, upper = sorted_out(near, far, pl.ds(2 * NK + q * 24, 24))
-        send[pl.ds(at, 24), :] = lower
-        send[pl.ds(at + 24, 64), :] = coarse[pl.ds(q * 64, 64), :]
-        send[pl.ds(at + 88, 16), :] = upper[:16]
+        rows = [lower[n * 8 : n * 8 + 8] for n in range(3)]
+        rows += [coarse[pl.ds(q * 64 + n * 8, 8), :] for n in range(8)]
+        rows += [upper[n * 8 : n * 8 + 8] for n in range(2)]
+        for row in rows:
+            fields[2 * q].append(jnp.where(wide < 64, row, 0.0))
+            fields[2 * q + 1].append(jnp.where(wide < 64, rolled(row, 64, 1), 0.0))
+    xs_, ys_, zs_, damps = fields
+    shares = [jnp.zeros((8, NI), F32)] * 4
+    for J in range(12):
+        top = jnp.where(level_k == 7, 0.0, zs_[J + 1])
+        rest = damps[J + 1] + ys_[J + 1] + ys_[J] + top + rolled(top, 1, 0) + xs_[J + 1] + rolled(xs_[J + 1], 1, 1)
+        for n, value in enumerate((xs_[J + 1], ys_[J + 1], top, rest)):
+            ext[pl.ds(n * 96 + J * 8, 8), :] = value
+            at = 10 * J
+            first, last = rolled(value, at, 1), rolled(value, at + 5 - 59, 1)
+            share = jnp.where(jnp.logical_and(wide >= at, wide < at + 5), first, shares[n])
+            shares[n] = jnp.where(jnp.logical_and(wide >= at + 5, wide < at + 10), last, share)
+    for n in range(4):
+        send[pl.ds(NJ + n * 8, 8), :] = shares[n]
 
 
 def x_second_solve(rhs, kept):
@@ -406,9 +425,14 @@
         terms[pl.ds(j, NK, stride=NJ), :] = before + after
 
 
-def x_again_kernel(xs, below, got, yg, ya, yb, mult, g, yred, send, fs, field, terms):
+def x_again_kernel(xs, below, mine, other, yg, ya, yb, mult, order, g, yred, send, fs, field, terms):
     f, p, xc, yc, zc, dp = parts(xs)
-    part = lambda n, q: got[n, pl.ds(q * NK, NK), :]
+    odd = lax.rem(lax.axis_index("gy"), 2) == 1
+
+    def part(n, q):
+        one, two = mine[n // 2, pl.ds(q * NK, NK), :], other[n // 2, pl.ds(q * NK, NK), :]
+        return jnp.where(odd, one, two) if n % 2 else jnp.where(odd, two, one)
+
     prev = None
     for n in range(GY - 1):
         dd = part(n, 4) + part(n + 1, 2)
@@ -481,7 +505,7 @@
     send[pl.ds(0, NK), :] = value
 
 
-def residual_kernel(xs, below, got, yg, ya, yb, yred, cl, field, near, far, coarse, fs, terms, tmp):
+def residual_kernel(xs, below, got, yg, ya, yb, yred, cl, fluxes, coarse, near, far, fs, terms, tmp, field):
     f, p, xc, yc, zc, dp = parts(xs)
     d = lax.axis_index("gx")
     lane = lanes(NJ)
@@ -493,6 +517,8 @@
         lambda n: yred[GY + n],
         lambda n: yred[2 * GY + n],
     )
+    e = lax.axis_index("gy")
+    fluxes[0], fluxes[1] = fs[e], fs[e + 1]
     y_finish(fs, yc, below, yg, ya, yb, field, terms)
     c_left = cl[...]
     main, rim = [], []
@@ -507,115 +533,136 @@
         rim.append(jnp.where(lane == 0, left * v, jnp.where(lane == NI - 1, last, 0.0)))
     pairs = jnp.concatenate([main[2 * K] + main[2 * K + 1] for K in range(NK // 2)], axis=0)
     outer = jnp.concatenate([rim[2 * K] + rim[2 * K + 1] for K in range(NK // 2)], axis=0)
-    tmp[...] = parity_shift(squeeze(pairs) + edges(outer))
+    tmp[...] = squeeze(pairs) + edges(outer)
     store_coarse(coarse, 0, tmp)
-    odd = lax.rem(lax.axis_index("gy"), 2) == 1
+    odd = lax.rem(e, 2) == 1
     up, down = coarse[pl.ds(48, 16), :], coarse[pl.ds(0, 16), :]
     near[...] = jnp.where(odd, down, up)
     far[...] = jnp.where(odd, up, down)
 
 
-def join_kernel(near, far, coarse, matrix, send):
-    lower, upper = sorted_out(near, far, pl.ds(0, 16))
-    send[pl.ds(0, 16), :] = lower
-    send[pl.ds(16, 64), :] = coarse[...]
-    send[pl.ds(80, 16), :] = upper
-
-
-def coarse_matrix_kernel(coef, weight_out, x_low_out, x_up_out, y_out, z_out):
+def eight(ref, J):
+    return ref[pl.ds(J * 8, 8), :]
+
+
+def coarse_matrix_kernel(ext, got, *outs):
     e = lax.axis_index("gy")
     lane = lanes(8)
-    wide = lanes(8, 4 * NI)
-    level_k = lax.broadcasted_iota(jnp.int32, (8, 4 * NI), 0)
-
-    def whole_coef(q, J):
-        rows = pl.ds(NJ + (q // 2) * 104 + J * 8, 8)
-        outs = []
+
+    def joint(n, J):
+        value = jnp.zeros((8, NI), F32)
+        for d in range(GX):
+            moved = rolled(got[d, pl.ds(NJ + n * 8, 8), :], 10 * (d - J), 1)
+            value = jnp.where(jnp.logical_and(lane >= 10 * d, lane < 10 * d + 10), moved, value)
+        return value
+
+    own = lambda n, J: ext[pl.ds(n * 96 + J * 8, 8), :]
+    first = jnp.logical_and(lax.rem(lane, 10) == 0, lane > 0)
+    for out, source, width in ((outs[0], own, 64), (outs[1], joint, 10 * GX)):
+        y_before = jnp.zeros((8, NI), F32)
+        for J in range(12):
+            x, y, z_top, rest = (source(n, J) for n in range(4))
+            x_left = rolled(x, 1, 1)
+            at = e * 8 + J - 2
+            valid = jnp.logical_and(jnp.logical_and(at >= 0, at < 8 * GY), lane < width)
+            if width != 64:
+                rest = rest + jnp.where(first, x_left, 0.0)
+            weight = jnp.where(valid, RELAX / jnp.where(valid, rest, 1.0), 0.0)
+            couplings = (x_left, x, y_before, y, rolled(z_top, 1, 0), z_top)
+            for n, value in enumerate((weight, *(weight * c for c in couplings))):
+                out[n, pl.ds(J * 8, 8), :] = value
+            y_before = y
+
+
+def relaxed(res, matrix):
+    at = lambda n, J: matrix[n, pl.ds(J * 8, 8), :]
+
+    def around(v, J):
+        return (
+            at(1, J) * rolled(v[J], 1, 1)
+            + at(2, J) * rolled(v[J], -1, 1)
+            + at(3, J) * v[J - 1]
+            + at(4, J) * v[J + 1]
+            + at(5, J) * rolled(v[J], 1, 0)
+            + at(6, J) * rolled(v[J], -1, 0)
+        )
+
+    first = {J: at(0, J) * res[J] for J in range(12)}
+    second = {J: (2.0 - RELAX) * first[J] + around(first, J) for J in range(1, 11)}
+    return [first[J] + (1.0 - RELAX) * second[J] + around(second, J) for J in range(2, 10)]
+
+
+def coarse_own_kernel(order, near, far, coarse, matrix, send):
+    lane = lanes(8)
+    lower, upper = sorted_out(near, far, pl.ds(0, 16))
+    res = [lower[:8], lower[8:], *(eight(coarse, J) for J in range(8)), upper[:8], upper[8:]]
+    done = relaxed(res, matrix)
+    for t in range(4):
+        send[pl.ds(t * 8, 8), :] = jnp.where(lane < 64, done[t], rolled(done[t + 4], 64, 1))
+    strips = [jnp.zeros((8, NI), F32)] * 2
+    for J in range(12):
+        at = 16 * (J % 8)
+        strip = jnp.where(jnp.logical_and(lane >= at, lane < at + 6), rolled(res[J], at + 1, 1), strips[J // 8])
+        strips[J // 8] = jnp.where(jnp.logical_and(lane >= at + 6, lane < at + 12), rolled(res[J], at + 6 - 59, 1), strip)
+    send[pl.ds(32, 8), :] = strips[0]
+    send[pl.ds(40, 8), :] = strips[1]
+
+
+def coarse_last_kernel(got, coarse, matrix, res_out, cor_out, tmp, res_tmp):
+    d_own = lax.axis_index("gx")
+    lane = lanes(8)
+    joint = []
+    for J in range(12):
+        value = jnp.zeros((8, NI), F32)
+        for d in range(GX):
+            low = 10 * d - 1
+            moved = rolled(got[d, pl.ds(32 + 8 * (J // 8), 8), :], low - 16 * (J % 8), 1)
+            value = value + jnp.where(jnp.logical_and(lane >= low, lane < low + 12), moved, 0.0)
+        joint.append(value)
+    done = relaxed(joint, matrix)
+    for J in range(8):
+        ends = joint[J + 2]
+        mine = rolled(ends, 0, 1)
+        for d in range(1, GX):
+            mine = jnp.where(d_own == d, rolled(ends, -10 * d, 1), mine)
+        mine = jnp.where(lane == 0, mine, jnp.where(lane == 63, rolled(mine, 54, 1), eight(coarse, J)))
+        res_tmp[pl.ds(J, 8, stride=8), :] = mine
+        rows = pl.ds((J % 4) * 8, 8)
         for m in range(4):
-            even, odd = coef[2 * m, rows, :], coef[2 * m + 1, rows, :]
-            if q % 2:
+            even, odd = got[2 * m, rows, :], got[2 * m + 1, rows, :]
+            if J < 4:
+                odd = rolled(odd, 64, 1)
+            else:
                 even = rolled(even, 64, 1)
-            else:
-                odd = rolled(odd, 64, 1)
-            outs.append(jnp.where(lane < 64, even, odd))
-        return jnp.concatenate(outs, axis=1)
-
-    y_before = whole_coef(1, 0)
-    y_out[pl.ds(0, 8), :] = y_before
-    for J in range(12):
-        rows = pl.ds(J * 8, 8)
-        x, y, z, damp = (whole_coef(q, J + 1) for q in range(4))
-        x_left = jnp.where(wide == 0, 0.0, rolled(x, 1, 1))
-        z_top = jnp.where(level_k == 7, 0.0, z)
-        total = x_left + x + y_before + y + rolled(z_top, 1, 0) + z_top + damp
-        at = e * 8 + J - 2
-        valid = jnp.logical_and(at >= 0, at < 8 * GY)
-        total = jnp.where(valid, total, 1.0)
-        weight_out[0, rows, :] = total
-        weight_out[1, rows, :] = jnp.where(valid, RELAX / total, 0.0)
-        x_low_out[rows, :] = x_left
-        x_up_out[rows, :] = jnp.where(wide == 4 * NI - 1, 0.0, x)
-        y_out[pl.ds(J * 8 + 8, 8), :] = y
-        z_out[rows, :] = z_top
-        y_before = y
-
-
-def coarse_kernel(got, weight, x_low, x_up, y_all, z_all, res_out, cor_out, tmp, cor_tmp):
-    d = lax.axis_index("gx")
-    lane = lanes(8)
-
-    def whole_res(J):
-        rows = pl.ds(J * 8, 8)
-        outs = []
-        for m in range(4):
-            value = jnp.where(lane <= 64, got[2 * m, rows, :], 0.0) + jnp.where(lane >= 63, got[2 * m + 1, rows, :], 0.0)
-            if m > 0:
-                value = value + jnp.where(lane == 0, got[2 * m - 1, rows, :], 0.0)
-            if m < 3:
-                value = value + jnp.where(lane == NI - 1, got[2 * m + 2, rows, :], 0.0)
-            outs.append(value)
-        return outs
-
-    at = lambda ref, J: ref[pl.ds(J * 8, 8), :]
-    diag = lambda J: weight[0, pl.ds(J * 8, 8), :]
-    scale = lambda J: weight[1, pl.ds(J * 8, 8), :]
-    res = []
-    for J in range(12):
-        outs = whole_res(J)
-        if 2 <= J < 10:
-            mine = outs[0]
-            for m in range(1, 4):
-                mine = jnp.where(d // 2 == m, outs[m], mine)
-            mine = jnp.where(lax.rem(d, 2) == 1, rolled(mine, 64, 1), mine)
-            tmp[pl.ds(J - 2, 8, stride=8), :] = mine
-        res.append(jnp.concatenate(outs, axis=1))
-    cor = {J: scale(J) * res[J] for J in range(12)}
-    for low, high in ((1, 11), (2, 10)):
-        new = {}
-        for J in range(low, high):
-            v = cor[J]
-            z_top = at(z_all, J)
-            applied = (
-                diag(J) * v
-                - at(x_low, J) * rolled(v, 1, 1)
-                - at(x_up, J) * rolled(v, -1, 1)
-                - at(y_all, J) * cor[J - 1]
-                - at(y_all, J + 1) * cor[J + 1]
-                - (rolled(z_top * v, 1, 0) + z_top * rolled(v, -1, 0))
-            )
-            new[J] = v + scale(J) * (res[J] - applied)
-        cor = new
-    for J in range(8):
-        for m in range(4):
-            cor_tmp[m, pl.ds(J, 8, stride=8), :] = cor[J + 2][:, m * NI : (m + 1) * NI]
+            value = jnp.where(lane < 64, even, odd)
+            for d in (2 * m, 2 * m + 1):
+                start = 64 * (d % 2)
+                left = jnp.logical_and(lane >= start, lane < start + 3)
+                right = jnp.logical_and(lane >= start + 61, lane < start + 64)
+                value = jnp.where(left, rolled(done[J], start - 10 * d, 1), value)
+                value = jnp.where(right, rolled(done[J], start + 54 - 10 * d, 1), value)
+            tmp[m, pl.ds(J, 8, stride=8), :] = value
     for m in range(4):
-        cor_out[:, pl.ds(m * NI, NI)] = cor_tmp[m]
-    res_out[...] = tmp[:, :64]
+        cor_out[:, pl.ds(m * NI, NI)] = tmp[m]
+    res_out[...] = res_tmp[:, :64]
+
+
+def field_kernel(fluxes, yg, ya, yb, field):
+    for j in range(NJ):
+        place = pl.ds(j * NK, NK)
+        field[pl.ds(j, NK, stride=NJ), :] = yg[place, :] - ya[place, :] * fluxes[0] + yb[place, :] * fluxes[1]
 
 
 def spread(value, axis, count):
     many = jnp.broadcast_to(value[None], (count,) + value.shape)
     return lax.all_to_all(many, axis, split_axis=0, concat_axis=0, tiled=True)
+
+
+def spread_by_core(value):
+    groups = [list(range(0, GY, 2)), list(range(1, GY, 2))]
+    many = jnp.broadcast_to(value[None], (GY // 2,) + value.shape)
+    mine = lax.all_to_all(many, "gy", split_axis=0, concat_axis=0, tiled=True, axis_index_groups=groups)
+    return mine, lax.ppermute(mine, "gy", [(n, n ^ 1) for n in range(GY)])
 
 
 def swap(near, far):
@@ -625,22 +672,22 @@
 
 
 def body(forcing, pressure_in, x_coupling, y_coupling, z_coupling, damping):
-    args = [v.reshape(ROWS, NI) for v in (forcing, pressure_in, x_coupling, y_coupling, z_coupling, damping)]
+    args = (forcing, pressure_in, x_coupling, y_coupling, z_coupling, damping)
     whole = sds(ROWS, NI)
     kept = sds((2 * len(STEPS) + 1) * ROWS, NI)
     xs, near, far, coef = call(
         first_kernel,
         [sds(6 * ROWS, NI), sds(80, NI), sds(80, NI), sds(128, NI)],
-        *[pltpu.with_memory_space_constraint(v, pltpu.HBM) for v in args],
+        *[v.reshape(ROWS, NI) for v in args],
         scratch=[(128, NI)],
-        hbm=True,
+        hbm=6,
         sems=6,
     )
     near, far = swap(near, far)
     g, a, b, mult, packed = call(x_first_kernel, [whole, whole, whole, kept, sds(NJ, NI)], xs, flops=10**8)
-    below, g, a, b, mult, send = call(
+    below, g, a, b, mult, send, ext = call(
         x_rim_kernel,
-        [sds(NK, NI), whole, whole, whole, kept, sds(NJ + 208, NI)],
+        [sds(NK, NI), whole, whole, whole, kept, sds(NJ + 32, NI), sds(4 * 96, NI)],
         xs, near, far, coef, packed, g, a, b, mult,
         aliases={5: 1, 6: 2, 7: 3, 8: 4},
     )
@@ -651,11 +698,12 @@
         xs, got, g, a, b,
         scratch=[(GX + 1, NJ, NI), (GX + 1, NJ, NI), (ROWS, NI), (ROWS, NI), (ROWS, NI)],
     )
-    got = spread(send, "gy", GY)
+    got = spread_by_core(send)
+    own, joint = call(coarse_matrix_kernel, [sds(7, 96, NI)] * 2, ext, got_coef, flops=10**7)
     g, yred, send = call(
         x_again_kernel,
         [whole, sds(3 * GY, NK, NI), sds(NJ, NI)],
-        xs, below, got, yg, ya, yb, mult,
+        xs, below, *got, yg, ya, yb, mult, joint,
         scratch=[(GY + 1, NK, NI), (ROWS, NI), (ROWS, NI)],
     )
     got = spread(send, "gx", GX)
@@ -666,20 +714,19 @@
         scratch=[(GX + 1, NJ, NI), (ROWS, NI), (ROWS, NI)],
     )
     got = spread(send, "gy", GY)
-    field, near, far, coarse = call(
+    fluxes, coarse, near, far = call(
         residual_kernel,
-        [whole, sds(16, NI), sds(16, NI), sds(64, NI)],
+        [sds(2, NK, NI), sds(64, NI), sds(16, NI), sds(16, NI)],
         xs, below, got, yg, ya, yb, yred, cl,
-        scratch=[(GY + 1, NK, NI), (ROWS, NI), (128, NI)],
+        scratch=[(GY + 1, NK, NI), (ROWS, NI), (128, NI), (ROWS, NI)],
     )
     near, far = swap(near, far)
-    rows = sds(96, 4 * NI)
-    matrix = call(
-        coarse_matrix_kernel, [sds(2, 96, 4 * NI), rows, rows, sds(104, 4 * NI), rows], got_coef, flops=10**7
-    )
-    (send,) = call(join_kernel, [sds(96, NI)], near, far, coarse, matrix[-1])
+    (field,) = call(field_kernel, [whole], fluxes, yg, ya, yb, flops=10**7)
+    (send,) = call(coarse_own_kernel, [sds(48, NI)], field, near, far, coarse, own, hbm=1)
     got = spread(send, "gx", GX)
-    res, cor = call(coarse_kernel, [sds(64, 64), sds(64, 512)], got, *matrix, scratch=[(64, NI), (4, 64, NI)])
+    res, cor = call(
+        coarse_last_kernel, [sds(64, 64), sds(64, 4 * NI)], got, coarse, joint, scratch=[(4, 64, NI), (64, NI)]
+    )
     return field.reshape(NK, NJ, NI), res.reshape(8, 8, 64), cor.reshape(8, 8, 512)
 
 

time: 93 us -> 80.7 us (0.87)
  blocking collectives: 71.1 us -> 59 us
    all_to_all x5 -> x4, blocking collectives: 71.1 us -> 48.2 us  [spread(): return lax.all_to_all(many, axis, split_axis=0, concat_axis=0, tiled=True)]
    all_to_all x0 -> x1, blocking collectives: none -> 10.8 us  [spread_by_core(): lax.all_to_all(many, 'gy', split_axis=0, concat_axis=0, tiled=True, axis_...]
    pallas_call x10 -> x11, Pallas kernels: 12 us -> 11.1 us  [call(): pl.pallas_call(kernel, out_shape=outs, in_specs=[outside] * hbm + [spec]...]
  transfers between devices with their start and end apart: 4 -> 5, of which waited for: 1 -> 2; matrix products, arithmetic and copies ran while one was open for 0% -> 0% of each run, Pallas kernels for 6% -> 5%
where the time goes in v7:
time: 80.7 us; the launch traced here: 80.4 us
  blocking collectives  59 us (73%)
  Pallas kernels  11.1 us (14%)
  starting transfers between devices  5.05 us (6%)
  waiting for transfers between devices  4.43 us (5%)
    all_to_all x4, blocking collectives, spread(): return lax.all_to_all(many, axis, split_axis=0, concat_axis=0, tiled=True)  48.2 us
    pallas_call x11, Pallas kernels, call(): pl.pallas_call(kernel, out_shape=outs, in_specs=[outside] * hbm + [spec]...  11.1 us
    all_to_all x1, blocking collectives, spread_by_core(): lax.all_to_all(many, 'gy', split_axis=0, concat_axis=0, tiled=True, axis_...  10.8 us
    ppermute x4, starting transfers between devices, swap(): return (lax.ppermute(near, 'gy', pairs), lax.ppermute(far, 'gy', others))  5.05 us
    ppermute x4, waiting for transfers between devices, swap(): return (lax.ppermute(near, 'gy', pairs), lax.ppermute(far, 'gy', others))  3.65 us
  transfers between devices with their start and end apart: 5, of which 2 were waited for; matrix products, arithmetic and copies ran while one was open for 0% of the time, Pallas kernels for 5%

profile of v7, /device:TPU:0, one launch (start us, length us, event | category | flops | bytes accessed | tf_op | source)
XLA Modules:
  0.0 80.4 jit_solution(5307145212491481942)
XLA Ops:
  0.6 1.7 %shard_map.85 = (f32[1536,128]{1,0:T(8,128)S(1)}, f32[80,128]{1,0:T(8,128)S(1)}, f32[80,128]{1,0:T(8,128)S(1)}, f32[128,128]{1,0:T(8,128)S(1)}) custom-call(f32[256,128]{1,0:T(8,128)} %bitcast.10, f32[256,128]{1,0:T(8,128)} %bitcast.11, f32[256,128]{1,0:T(8,128)} %bitcast.12, f32[256,128]{1,0:T(8,128)} %bitcast.13, f32[256,128]{1,0:T(8,128)} %bitcast.14, ...), custom_call_target="tpu_custom_call" | custom-call | tf_op jit(solution)/shard_map/pallas_call | solution.py:30
  2.3 0.1 collective-permute-start
  2.4 4.0 %collective-permute-start.1 = (f32[80,128]{1,0:T(8,128)S(1)}, f32[80,128]{1,0:T(8,128)S(1)}, u32[]{:S(2)}, u32[]{:S(2)}) collective-permute-start(f32[80,128]{1,0:T(8,128)S(1)} %get-tuple-element.42), channel_id=1, source_target_pairs={{0,15},{1,2},{2,1},{3,4},{4,3},{5,6},{6,5},{7,8},{8,7},{9,10},{10,... | collective-permute-start | bytes 122888 | tf_op jit(solution)/shard_map/ppermute | solution.py:671
  6.4 2.5 %shard_map.86 = (f32[256,128]{1,0:T(8,128)S(1)}, f32[256,128]{1,0:T(8,128)S(1)}, f32[256,128]{1,0:T(8,128)S(1)}, f32[3840,128]{1,0:T(8,128)S(1)}, f32[16,128]{1,0:T(8,128)S(1)}) custom-call(f32[1536,128]{1,0:T(8,128)S(1)} %get-tuple-element.40.xs), custom_call_target="tpu_custom_call" | custom-call | flops 100000000 | bytes 1048576 | tf_op jit(solution)/shard_map/pallas_call | solution.py:30
  8.9 0.0 collective-permute-done.near
  8.9 0.0 collective-permute-done.1.far
  8.9 1.0 %shard_map.87 = (f32[16,128]{1,0:T(8,128)S(1)}, f32[256,128]{1,0:T(8,128)S(1)}, f32[256,128]{1,0:T(8,128)S(1)}, f32[256,128]{1,0:T(8,128)S(1)}, f32[3840,128]{1,...) custom-call(f32[1536,128]{1,0:T(8,128)S(1)} %get-tuple-element.40.xs, ...), custom_call_target="tpu_custom_call", output_to_operand_aliasing={{1}: (5, {}), {2}: (6, {}), {3}: (7, {}), {4}: (8, {})} | custom-call | tf_op jit(solution)/shard_map/pallas_call | solution.py:30
  9.9 15.9 %all_to_all.25.got = f32[8,48,128]{2,1,0:T(8,128)S(1)} all-to-all(f32[8,48,128]{2,1,0:T(8,128)S(1)} %broadcast_in_dim.10), channel_id=1, replica_groups=mesh['gx'=8,'gy'=16] {'gx'}, dimensions={0} | all-to-all | bytes 393216 | tf_op jit(solution)/shard_map/all_to_all | solution.py:658
  25.9 0.6 shard_map.88
  26.5 10.8 %all_to_all.26.mine = f32[8,80,128]{2,1,0:T(8,128)S(1)} all-to-all(f32[8,80,128]{2,1,0:T(8,128)S(1)} %broadcast_in_dim.11), channel_id=1, replica_groups={{0,2,4,6,8,10,12,14},{1,3,5,7,9,11,13,15},{16,18,20,22,24,26,28,30},{17..., dimensions={0} | all-to-all | bytes 655360 | tf_op jit(solution)/shard_map/all_to_all | solution.py:664
  37.3 0.0 collective-permute-start.2
  37.3 0.8 %shard_map.89 = (f32[7,96,128]{2,1,0:T(8,128)S(1)}, f32[7,96,128]{2,1,0:T(8,128)S(1)}) custom-call(f32[384,128]{1,0:T(8,128)S(1)} %get-tuple-element.59.ext, f32[8,48,128]{2,1,0:T(8,128)S(1)} %all_to_all.25.got), custom_call_target="tpu_custom_call" | custom-call | flops 10000000 | bytes 1048576 | tf_op jit(solution)/shard_map/pallas_call | solution.py:30
  38.2 0.8 collective-permute-done.2.other
  39.0 1.0 %shard_map.90 = (f32[256,128]{1,0:T(8,128)S(1)}, f32[48,16,128]{2,1,0:T(8,128)S(1)}, f32[16,128]{1,0:T(8,128)S(1)}) custom-call(f32[1536,128]{1,0:T(8,128)S(1)} %get-tuple-element.40.xs, f32[16,128]{1,0:T(8,128)S(1)} %get-tuple-element.49.below, f32[8,80,128]{2,1,0:T(8,128)S(1)} %all_to_all.26.mine, f32[8,80,128]{2,1,0:T(8,128)S(1)} %collective-permute-done.2.other, ...), custom_call_target="tpu_custom_call" | custom-call | tf_op jit(solution)/shard_map/pallas_call | solution.py:30
  40.0 11.1 %all_to_all.27.got = f32[8,16,128]{2,1,0:T(8,128)S(1)} all-to-all(f32[8,16,128]{2,1,0:T(8,128)S(1)} %broadcast_in_dim.12), channel_id=1, replica_groups=mesh['gx'=8,'gy'=16] {'gx'}, dimensions={0} | all-to-all | bytes 131072 | tf_op jit(solution)/shard_map/all_to_all | solution.py:658
  51.0 0.5 shard_map.91
  51.5 10.3 %all_to_all.28.got = f32[16,32,128]{2,1,0:T(8,128)S(1)} all-to-all(f32[16,32,128]{2,1,0:T(8,128)S(1)} %broadcast_in_dim.13), channel_id=1, replica_groups=mesh['gx'=8,'gy'=16] {'gy'}, dimensions={0} | all-to-all | bytes 524288 | tf_op jit(solution)/shard_map/all_to_all | solution.py:658
  61.8 0.6 shard_map.92
  62.4 0.2 collective-permute-start.3
  62.6 0.8 %collective-permute-start.4 = (f32[16,128]{1,0:T(8,128)S(1)}, f32[16,128]{1,0:T(8,128)S(1)}, u32[]{:S(2)}, u32[]{:S(2)}) collective-permute-start(f32[16,128]{1,0:T(8,128)S(1)} %get-tuple-element.72), channel_id=1, source_target_pairs={{0,15},{1,2},{2,1},{3,4},{4,3},{5,6},{6,5},{7,8},{8,7},{9,10},{10,... | collective-permute-start | bytes 24584 | tf_op jit(solution)/shard_map/ppermute | solution.py:671
  63.4 0.7 shard_map.93.order
  64.1 0.0 collective-permute-done.3.near
  64.1 3.6 %collective-permute-done.4.far = f32[16,128]{1,0:T(8,128)S(1)} collective-permute-done((f32[16,128]{1,0:T(8,128)S(1)}, f32[16,128]{1,0:T(8,128)S(1)}, u32[]{:S(2)}, u32[]{:S(2)}) %collective-permute-start.4) | collective-permute-done | bytes 8224 | tf_op jit(solution)/shard_map/ppermute | solution.py:671
  67.8 0.2 shard_map.94
  68.0 10.9 %all_to_all.29.got = f32[8,48,128]{2,1,0:T(8,128)S(1)} all-to-all(f32[8,48,128]{2,1,0:T(8,128)S(1)} %broadcast_in_dim.14), channel_id=1, replica_groups=mesh['gx'=8,'gy'=16] {'gx'}, dimensions={0} | all-to-all | bytes 393216 | tf_op jit(solution)/shard_map/all_to_all | solution.py:658
  78.9 1.4 %shard_map.95 = (f32[64,64]{1,0:T(8,128)}, f32[64,512]{1,0:T(8,128)}) custom-call(f32[8,48,128]{2,1,0:T(8,128)S(1)} %all_to_all.29.got, f32[64,128]{1,0:T(8,128)S(1)} %get-tuple-element.73.coarse, f32[7,96,128]{2,1,0:T(8,128)S(1)} %get-tuple-element.60.order.matrix), custom_call_target="tpu_custom_call" | custom-call | tf_op jit(solution)/shard_map/pallas_call | solution.py:30
  (5 shorter events, 0.1 us)
Async XLA Ops:
  2.3 6.6 %collective-permute-start = (f32[80,128]{1,0:T(8,128)S(1)}, f32[80,128]{1,0:T(8,128)S(1)}, u32[]{:S(2)}, u32[]{:S(2)}) collective-permute-start(f32[80,128]{1,0:T(8,128)S(1)} %get-tuple-element.41), channel_id=1, source_target_pairs={{0,1},{1,0},{2,3},{3,2},{4,5},{5,4},{6,7},{7,6},{8,9},{9,8},{10,11... | collective-permute-start | bytes 122888 | tf_op jit(solution)/shard_map/ppermute | solution.py:671
  2.4 6.5 %collective-permute-start.1 = (f32[80,128]{1,0:T(8,128)S(1)}, f32[80,128]{1,0:T(8,128)S(1)}, u32[]{:S(2)}, u32[]{:S(2)}) collective-permute-start(f32[80,128]{1,0:T(8,128)S(1)} %get-tuple-element.42), channel_id=1, source_target_pairs={{0,15},{1,2},{2,1},{3,4},{4,3},{5,6},{6,5},{7,8},{8,7},{9,10},{10,... | collective-permute-start | bytes 122888 | tf_op jit(solution)/shard_map/ppermute | solution.py:671
  37.3 1.6 %collective-permute-start.2 = (f32[8,80,128]{2,1,0:T(8,128)S(1)}, f32[8,80,128]{2,1,0:T(8,128)S(1)}, u32[]{:S(2)}, u32[]{:S(2)}) collective-permute-start(f32[8,80,128]{2,1,0:T(8,128)S(1)} %all_to_all.26.mine), channel_id=1, source_target_pairs={{0,1},{1,0},{2,3},{3,2},{4,5},{5,4},{6,7},{7,6},{8,9},{9,8},{10,11... | collective-permute-start | bytes 983048 | tf_op jit(solution)/shard_map/ppermute | solution.py:665
  62.4 1.7 %collective-permute-start.3 = (f32[16,128]{1,0:T(8,128)S(1)}, f32[16,128]{1,0:T(8,128)S(1)}, u32[]{:S(2)}, u32[]{:S(2)}) collective-permute-start(f32[16,128]{1,0:T(8,128)S(1)} %get-tuple-element.71), channel_id=1, source_target_pairs={{0,1},{1,0},{2,3},{3,2},{4,5},{5,4},{6,7},{7,6},{8,9},{9,8},{10,11... | collective-permute-start | bytes 24584 | tf_op jit(solution)/shard_map/ppermute | solution.py:671
  62.6 5.2 %collective-permute-start.4 = (f32[16,128]{1,0:T(8,128)S(1)}, f32[16,128]{1,0:T(8,128)S(1)}, u32[]{:S(2)}, u32[]{:S(2)}) collective-permute-start(f32[16,128]{1,0:T(8,128)S(1)} %get-tuple-element.72), channel_id=1, source_target_pairs={{0,15},{1,2},{2,1},{3,4},{4,3},{5,6},{6,5},{7,8},{8,7},{9,10},{10,... | collective-permute-start | bytes 24584 | tf_op jit(solution)/shard_map/ppermute | solution.py:671

commit v8 on v7

--- a/solution.py
+++ b/solution.py
@@ -11,6 +11,7 @@
 NK, NJ, NI = 16, 16, 128
 ROWS = NK * NJ
 GX, GY = 8, 16
+CHIPS = GY // 2
 STEPS = (1, 2, 4, 8, 16, 32, 64)
 F32 = jnp.float32
 
@@ -90,11 +91,22 @@
     return jnp.where(row == 0, halo[pl.ds(k, 1), :], rolled(level(yc, k), 1, 0))
 
 
+def exact_dot(values, matrix):
+    matrix = matrix.astype(jnp.bfloat16)
+    total = None
+    for _ in range(3):
+        piece = values.astype(jnp.bfloat16)
+        values = values - piece.astype(F32)
+        part = jnp.dot(piece, matrix, preferred_element_type=F32)
+        total = part if total is None else total + part
+    return total
+
+
 def squeeze(values, scale=0.125, start=0):
     source = lax.broadcasted_iota(jnp.int32, (NI, NI), 0)
     target = lax.broadcasted_iota(jnp.int32, (NI, NI), 1)
     matrix = jnp.where(source // 2 + start == target, scale, 0.0).astype(F32)
-    return jnp.dot(values, matrix, precision=lax.Precision.HIGHEST, preferred_element_type=F32)
+    return exact_dot(values, matrix)
 
 
 def edges(values, scale=0.125):
@@ -102,7 +114,7 @@
     target = lax.broadcasted_iota(jnp.int32, (NI, NI), 1)
     hit = ((source == NI - 1) & (target == 64)) | ((source == 0) & (target == NI - 1))
     matrix = jnp.where(hit, scale, 0.0).astype(F32)
-    return jnp.dot(values, matrix, precision=lax.Precision.HIGHEST, preferred_element_type=F32)
+    return exact_dot(values, matrix)
 
 
 def store_coarse(out, base, tmp):
@@ -395,20 +407,61 @@
 
 def y_fluxes(fs, source, low, inv, up):
     zero = jnp.zeros((NK, NI), F32)
-    fs[0], fs[GY] = zero, zero
+    fs[0], fs[CHIPS] = zero, zero
     forward = [source(0)]
-    for n in range(1, GY - 1):
+    for n in range(1, CHIPS - 1):
         forward.append(source(n) + low(n) * forward[-1])
-    value = forward[-1] * inv(GY - 2)
-    fs[GY - 1] = value
-    for n in range(GY - 3, -1, -1):
+    value = forward[-1] * inv(CHIPS - 2)
+    fs[CHIPS - 1] = value
+    for n in range(CHIPS - 3, -1, -1):
         value = forward[n] * inv(n) + up(n) * value
         fs[1 + n] = value
 
 
-def y_finish(fs, yc, below, yg, ya, yb, field, terms):
+def own_fluxes(fs, joint, inner):
     e = lax.axis_index("gy")
-    flux_left, flux_right = fs[e], fs[e + 1]
+    outer_left, outer_right = fs[e // 2], fs[e // 2 + 1]
+    between = inner[...] + joint[1] * outer_left + joint[2] * outer_right
+    odd = lax.rem(e, 2) == 1
+    return jnp.where(odd, between, outer_left), jnp.where(odd, outer_right, between)
+
+
+def join_first_kernel(order, mine, theirs, send, joint, inner):
+    odd = lax.rem(lax.axis_index("gy"), 2) == 1
+    block = lambda ref, q: ref[pl.ds(q * NK, NK), :]
+    low = [jnp.where(odd, block(theirs, q), block(mine, q)) for q in range(5)]
+    high = [jnp.where(odd, block(mine, q), block(theirs, q)) for q in range(5)]
+    inv = 1.0 / (low[4] + high[2])
+    from_low, from_high = low[3] * inv, high[3] * inv
+    base = (high[0] - low[1]) * inv
+    values = (
+        low[0] + low[3] * base,
+        high[1] - high[3] * base,
+        low[2] - low[3] * from_low,
+        low[3] * from_high,
+        high[4] - high[3] * from_high,
+    )
+    for q, value in enumerate(values):
+        send[pl.ds(q * NK, NK), :] = value
+    for n, value in enumerate((inv, from_low, from_high, low[3], high[3])):
+        joint[n] = value
+    inner[...] = base
+
+
+def join_again_kernel(mine, theirs, joint, send, inner):
+    odd = lax.rem(lax.axis_index("gy"), 2) == 1
+    block = lambda ref, q: ref[pl.ds(q * NK, NK), :]
+    low = [jnp.where(odd, block(theirs, q), block(mine, q)) for q in range(2)]
+    high = [jnp.where(odd, block(mine, q), block(theirs, q)) for q in range(2)]
+    base = (high[0] - low[1]) * joint[0]
+    send[pl.ds(0, NK), :] = low[0] + joint[3] * base
+    send[pl.ds(NK, NK), :] = high[1] - joint[4] * base
+    inner[...] = base
+
+
+def y_finish(fluxes, yc, below, yg, ya, yb, field, terms):
+    e = lax.axis_index("gy")
+    flux_left, flux_right = fluxes
     block = lambda ref, j: ref[pl.ds(j * NK, NK), :]
     p = [block(yg, j) - block(ya, j) * flux_left + block(yb, j) * flux_right for j in range(NJ)]
     for j in range(NJ):
@@ -425,16 +478,11 @@
         terms[pl.ds(j, NK, stride=NJ), :] = before + after
 
 
-def x_again_kernel(xs, below, mine, other, yg, ya, yb, mult, order, g, yred, send, fs, field, terms):
+def x_again_kernel(xs, below, got, joint, inner, yg, ya, yb, mult, g, yred, send, fs, field, terms):
     f, p, xc, yc, zc, dp = parts(xs)
-    odd = lax.rem(lax.axis_index("gy"), 2) == 1
-
-    def part(n, q):
-        one, two = mine[n // 2, pl.ds(q * NK, NK), :], other[n // 2, pl.ds(q * NK, NK), :]
-        return jnp.where(odd, one, two) if n % 2 else jnp.where(odd, two, one)
-
+    part = lambda n, q: got[n, pl.ds(q * NK, NK), :]
     prev = None
-    for n in range(GY - 1):
+    for n in range(CHIPS - 1):
         dd = part(n, 4) + part(n + 1, 2)
         if n:
             m = part(n, 3)
@@ -444,19 +492,18 @@
         else:
             yred[n] = jnp.zeros_like(dd)
         prev = 1.0 / dd
-        yred[GY + n] = prev
-        yred[2 * GY + n] = part(n + 1, 3) * prev
-    yred[GY - 1] = jnp.zeros((NK, NI), F32)
-    yred[2 * GY - 1] = jnp.zeros((NK, NI), F32)
-    yred[3 * GY - 1] = jnp.zeros((NK, NI), F32)
+        yred[CHIPS + n] = prev
+        yred[2 * CHIPS + n] = part(n + 1, 3) * prev
+    for n in range(1, 4):
+        yred[n * CHIPS - 1] = jnp.zeros((NK, NI), F32)
     y_fluxes(
         fs,
         lambda n: part(n + 1, 0) - part(n, 1),
         lambda n: yred[n],
-        lambda n: yred[GY + n],
-        lambda n: yred[2 * GY + n],
-    )
-    y_finish(fs, yc, below, yg, ya, yb, field, terms)
+        lambda n: yred[CHIPS + n],
+        lambda n: yred[2 * CHIPS + n],
+    )
+    y_finish(own_fluxes(fs, joint, inner), yc, below, yg, ya, yb, field, terms)
     lane = lanes(NJ)
     packed = jnp.zeros((NJ, NI), F32)
     group = 2
@@ -471,12 +518,12 @@
             mine = rhs[(k - k0) * NJ : (k - k0 + 1) * NJ]
             packed = jnp.where(lane == k, column(mine, 0), packed)
             packed = jnp.where(lane == NK + k, column(mine, NI - 1), packed)
-    send[...] = packed
+    send[...] = jnp.where(lanes(8) < 2 * NK, packed[:8], rolled(packed[8:], 2 * NK, 1))
 
 
 def y_again_kernel(xs, got, g, a, b, xred, cl, yw, yinv, yg, send, fs, field, src):
     f, p, xc, yc, zc, dp = parts(xs)
-    part = lambda n, q: rolled(got[n], -NK * q, 1)
+    part = lambda n, q: jnp.concatenate([rolled(got[n], -NK * q, 1), rolled(got[n], -NK * (q + 2), 1)], axis=0)
     x_fluxes(
         fs,
         lambda n: part(n + 1, 0) - part(n, 1),
@@ -505,7 +552,7 @@
     send[pl.ds(0, NK), :] = value
 
 
-def residual_kernel(xs, below, got, yg, ya, yb, yred, cl, fluxes, coarse, near, far, fs, terms, tmp, field):
+def residual_kernel(xs, below, got, joint, inner, yg, ya, yb, yred, cl, fluxes, coarse, near, far, fs, terms, tmp, field):
     f, p, xc, yc, zc, dp = parts(xs)
     d = lax.axis_index("gx")
     lane = lanes(NJ)
@@ -514,12 +561,13 @@
         fs,
         lambda n: part(n + 1, 0) - part(n, 1),
         lambda n: yred[n],
-        lambda n: yred[GY + n],
-        lambda n: yred[2 * GY + n],
+        lambda n: yred[CHIPS + n],
+        lambda n: yred[2 * CHIPS + n],
     )
     e = lax.axis_index("gy")
-    fluxes[0], fluxes[1] = fs[e], fs[e + 1]
-    y_finish(fs, yc, below, yg, ya, yb, field, terms)
+    ends = own_fluxes(fs, joint, inner)
+    fluxes[0], fluxes[1] = ends
+    y_finish(ends, yc, below, yg, ya, yb, field, terms)
     c_left = cl[...]
     main, rim = [], []
     for k in range(NK):
@@ -658,11 +706,14 @@
     return lax.all_to_all(many, axis, split_axis=0, concat_axis=0, tiled=True)
 
 
+def other_core(value):
+    return lax.ppermute(value, "gy", [(n, n ^ 1) for n in range(GY)])
+
+
 def spread_by_core(value):
     groups = [list(range(0, GY, 2)), list(range(1, GY, 2))]
-    many = jnp.broadcast_to(value[None], (GY // 2,) + value.shape)
-    mine = lax.all_to_all(many, "gy", split_axis=0, concat_axis=0, tiled=True, axis_index_groups=groups)
-    return mine, lax.ppermute(mine, "gy", [(n, n ^ 1) for n in range(GY)])
+    many = jnp.broadcast_to(value[None], (CHIPS,) + value.shape)
+    return lax.all_to_all(many, "gy", split_axis=0, concat_axis=0, tiled=True, axis_index_groups=groups)
 
 
 def swap(near, far):
@@ -698,13 +749,17 @@
         xs, got, g, a, b,
         scratch=[(GX + 1, NJ, NI), (GX + 1, NJ, NI), (ROWS, NI), (ROWS, NI), (ROWS, NI)],
     )
+    theirs = other_core(send)
+    own, ends = call(coarse_matrix_kernel, [sds(7, 96, NI)] * 2, ext, got_coef, flops=10**7)
+    send, joint, inner = call(
+        join_first_kernel, [sds(5 * NK, NI), sds(5, NK, NI), sds(NK, NI)], ends, send, theirs
+    )
     got = spread_by_core(send)
-    own, joint = call(coarse_matrix_kernel, [sds(7, 96, NI)] * 2, ext, got_coef, flops=10**7)
     g, yred, send = call(
         x_again_kernel,
-        [whole, sds(3 * GY, NK, NI), sds(NJ, NI)],
-        xs, below, *got, yg, ya, yb, mult, joint,
-        scratch=[(GY + 1, NK, NI), (ROWS, NI), (ROWS, NI)],
+        [whole, sds(3 * CHIPS, NK, NI), sds(8, NI)],
+        xs, below, got, joint, inner, yg, ya, yb, mult,
+        scratch=[(CHIPS + 1, NK, NI), (ROWS, NI), (ROWS, NI)],
     )
     got = spread(send, "gx", GX)
     yg, send = call(
@@ -713,19 +768,20 @@
         xs, got, g, a, b, xred, cl, yw, yinv,
         scratch=[(GX + 1, NJ, NI), (ROWS, NI), (ROWS, NI)],
     )
-    got = spread(send, "gy", GY)
+    send, inner = call(join_again_kernel, [sds(2 * NK, NI), sds(NK, NI)], send, other_core(send), joint)
+    got = spread_by_core(send)
     fluxes, coarse, near, far = call(
         residual_kernel,
         [sds(2, NK, NI), sds(64, NI), sds(16, NI), sds(16, NI)],
-        xs, below, got, yg, ya, yb, yred, cl,
-        scratch=[(GY + 1, NK, NI), (ROWS, NI), (128, NI), (ROWS, NI)],
+        xs, below, got, joint, inner, yg, ya, yb, yred, cl,
+        scratch=[(CHIPS + 1, NK, NI), (ROWS, NI), (128, NI), (ROWS, NI)],
     )
     near, far = swap(near, far)
     (field,) = call(field_kernel, [whole], fluxes, yg, ya, yb, flops=10**7)
     (send,) = call(coarse_own_kernel, [sds(48, NI)], field, near, far, coarse, own, hbm=1)
     got = spread(send, "gx", GX)
     res, cor = call(
-        coarse_last_kernel, [sds(64, 64), sds(64, 4 * NI)], got, coarse, joint, scratch=[(4, 64, NI), (64, NI)]
+        coarse_last_kernel, [sds(64, 64), sds(64, 4 * NI)], got, coarse, ends, scratch=[(4, 64, NI), (64, NI)]
     )
     return field.reshape(NK, NJ, NI), res.reshape(8, 8, 64), cor.reshape(8, 8, 512)
 

time: 80.7 us -> 80.1 us (level)
  blocking collectives: 59 us -> 57.6 us
  starting transfers between devices: 5.05 us -> 5.87 us
    all_to_all x4 -> x3, blocking collectives: 48.2 us -> 37.6 us  [spread(): return lax.all_to_all(many, axis, split_axis=0, concat_axis=0, tiled=True)]
    all_to_all x1 -> x2, blocking collectives: 10.8 us -> 20 us  [spread_by_core(): lax.all_to_all(many, 'gy', split_axis=0, concat_axis=0, tiled=True, axis_...]
    pallas_call x11 -> x13, Pallas kernels: 11.1 us -> 11 us  [call(): pl.pallas_call(kernel, out_shape=outs, in_specs=[outside] * hbm + [spec]...]
  transfers between devices with their start and end apart: 5 -> 6, of which waited for: 2 -> 3; matrix products, arithmetic and copies ran while one was open for 0% -> 0% of each run, Pallas kernels for 5% -> 5%
where the time goes in v8:
time: 80.1 us; the launch traced here: 79.8 us
  blocking collectives  57.6 us (72%)
  Pallas kernels  11 us (14%)
  starting transfers between devices  5.87 us (7%)
  waiting for transfers between devices  4.51 us (6%)
    all_to_all x3, blocking collectives, spread(): return lax.all_to_all(many, axis, split_axis=0, concat_axis=0, tiled=True)  37.6 us
    all_to_all x2, blocking collectives, spread_by_core(): lax.all_to_all(many, 'gy', split_axis=0, concat_axis=0, tiled=True, axis_...  20 us
    pallas_call x13, Pallas kernels, call(): pl.pallas_call(kernel, out_shape=outs, in_specs=[outside] * hbm + [spec]...  11 us
    ppermute x4, starting transfers between devices, swap(): return (lax.ppermute(near, 'gy', pairs), lax.ppermute(far, 'gy', others))  5.7 us
    ppermute x4, waiting for transfers between devices, swap(): return (lax.ppermute(near, 'gy', pairs), lax.ppermute(far, 'gy', others))  2.99 us
  transfers between devices with their start and end apart: 6, of which 3 were waited for; matrix products, arithmetic and copies ran while one was open for 0% of the time, Pallas kernels for 5%

profile of v8, /device:TPU:0, one launch (start us, length us, event | category | flops | bytes accessed | tf_op | source)
XLA Modules:
  0.0 79.8 jit_solution(11924431916784217261)
XLA Ops:
  0.6 1.6 %shard_map.85 = (f32[1536,128]{1,0:T(8,128)S(1)}, f32[80,128]{1,0:T(8,128)S(1)}, f32[80,128]{1,0:T(8,128)S(1)}, f32[128,128]{1,0:T(8,128)S(1)}) custom-call(f32[256,128]{1,0:T(8,128)} %bitcast.10, f32[256,128]{1,0:T(8,128)} %bitcast.11, f32[256,128]{1,0:T(8,128)} %bitcast.12, f32[256,128]{1,0:T(8,128)} %bitcast.13, f32[256,128]{1,0:T(8,128)} %bitcast.14, ...), custom_call_target="tpu_custom_call" | custom-call | tf_op jit(solution)/shard_map/pallas_call | solution.py:31
  2.2 0.1 collective-permute-start
  2.3 4.0 %collective-permute-start.1 = (f32[80,128]{1,0:T(8,128)S(1)}, f32[80,128]{1,0:T(8,128)S(1)}, u32[]{:S(2)}, u32[]{:S(2)}) collective-permute-start(f32[80,128]{1,0:T(8,128)S(1)} %get-tuple-element.47), channel_id=1, source_target_pairs={{0,15},{1,2},{2,1},{3,4},{4,3},{5,6},{6,5},{7,8},{8,7},{9,10},{10,... | collective-permute-start | bytes 122888 | tf_op jit(solution)/shard_map/ppermute | solution.py:722
  6.3 2.6 %shard_map.86 = (f32[256,128]{1,0:T(8,128)S(1)}, f32[256,128]{1,0:T(8,128)S(1)}, f32[256,128]{1,0:T(8,128)S(1)}, f32[3840,128]{1,0:T(8,128)S(1)}, f32[16,128]{1,0:T(8,128)S(1)}) custom-call(f32[1536,128]{1,0:T(8,128)S(1)} %get-tuple-element.45.xs), custom_call_target="tpu_custom_call" | custom-call | flops 100000000 | bytes 1048576 | tf_op jit(solution)/shard_map/pallas_call | solution.py:31
  8.8 0.0 collective-permute-done.near
  8.8 0.0 collective-permute-done.1.far
  8.8 1.0 %shard_map.87 = (f32[16,128]{1,0:T(8,128)S(1)}, f32[256,128]{1,0:T(8,128)S(1)}, f32[256,128]{1,0:T(8,128)S(1)}, f32[256,128]{1,0:T(8,128)S(1)}, f32[3840,128]{1,...) custom-call(f32[1536,128]{1,0:T(8,128)S(1)} %get-tuple-element.45.xs, ...), custom_call_target="tpu_custom_call", output_to_operand_aliasing={{1}: (5, {}), {2}: (6, {}), {3}: (7, {}), {4}: (8, {})} | custom-call | tf_op jit(solution)/shard_map/pallas_call | solution.py:31
  9.9 15.9 %all_to_all.25.got = f32[8,48,128]{2,1,0:T(8,128)S(1)} all-to-all(f32[8,48,128]{2,1,0:T(8,128)S(1)} %broadcast_in_dim.10), channel_id=1, replica_groups=mesh['gx'=8,'gy'=16] {'gx'}, dimensions={0} | all-to-all | bytes 393216 | tf_op jit(solution)/shard_map/all_to_all | solution.py:706
  25.8 0.7 shard_map.89
  26.5 0.1 collective-permute-start.2
  26.6 0.8 %shard_map.88 = (f32[7,96,128]{2,1,0:T(8,128)S(1)}, f32[7,96,128]{2,1,0:T(8,128)S(1)}) custom-call(f32[384,128]{1,0:T(8,128)S(1)} %get-tuple-element.55.ext, f32[8,48,128]{2,1,0:T(8,128)S(1)} %all_to_all.25.got), custom_call_target="tpu_custom_call" | custom-call | flops 10000000 | bytes 1048576 | tf_op jit(solution)/shard_map/pallas_call | solution.py:31
  27.4 0.4 collective-permute-done.2.theirs
  27.8 11.0 %all_to_all.26.got = f32[8,80,128]{2,1,0:T(8,128)S(1)} all-to-all(f32[8,80,128]{2,1,0:T(8,128)S(1)} %broadcast_in_dim.11), channel_id=1, replica_groups={{0,2,4,6,8,10,12,14},{1,3,5,7,9,11,13,15},{16,18,20,22,24,26,28,30},{17..., dimensions={0} | all-to-all | bytes 655360 | tf_op jit(solution)/shard_map/all_to_all | solution.py:716
  38.8 1.0 %shard_map.91 = (f32[256,128]{1,0:T(8,128)S(1)}, f32[24,16,128]{2,1,0:T(8,128)S(1)}, f32[8,128]{1,0:T(8,128)S(1)}) custom-call(f32[1536,128]{1,0:T(8,128)S(1)} %get-tuple-element.45.xs, f32[16,128]{1,0:T(8,128)S(1)} %get-tuple-element.54.below, f32[8,80,128]{2,1,0:T(8,128)S(1)} %all_to_all.26.got, f32[5,16,128]{2,1,0:T(8,128)S(1)} %get-tuple-element.63.joint, ...), custom_call_target="tpu_custom_call" | custom-call | tf_op jit(solution)/shard_map/pallas_call | solution.py:31
  39.8 10.8 %all_to_all.27.got = f32[8,8,128]{2,1,0:T(8,128)S(1)} all-to-all(f32[8,8,128]{2,1,0:T(8,128)S(1)} %broadcast_in_dim.12), channel_id=1, replica_groups=mesh['gx'=8,'gy'=16] {'gx'}, dimensions={0} | all-to-all | bytes 65536 | tf_op jit(solution)/shard_map/all_to_all | solution.py:706
  50.6 0.5 shard_map.92
  51.1 0.1 collective-permute-start.3
  51.2 1.2 %collective-permute-done.3.theirs = f32[32,128]{1,0:T(8,128)S(1)} collective-permute-done((f32[32,128]{1,0:T(8,128)S(1)}, f32[32,128]{1,0:T(8,128)S(1)}, u32[]{:S(2)}, u32[]{:S(2)}) %collective-permute-start.3) | collective-permute-done | bytes 16416 | tf_op jit(solution)/shard_map/ppermute | solution.py:710
  52.4 9.0 %all_to_all.28.got = f32[8,32,128]{2,1,0:T(8,128)S(1)} all-to-all(f32[8,32,128]{2,1,0:T(8,128)S(1)} %broadcast_in_dim.13), channel_id=1, replica_groups={{0,2,4,6,8,10,12,14},{1,3,5,7,9,11,13,15},{16,18,20,22,24,26,28,30},{17..., dimensions={0} | all-to-all | bytes 262144 | tf_op jit(solution)/shard_map/all_to_all | solution.py:716
  61.4 0.5 shard_map.94
  61.9 0.1 collective-permute-start.4
  62.0 1.6 %collective-permute-start.5 = (f32[16,128]{1,0:T(8,128)S(1)}, f32[16,128]{1,0:T(8,128)S(1)}, u32[]{:S(2)}, u32[]{:S(2)}) collective-permute-start(f32[16,128]{1,0:T(8,128)S(1)} %get-tuple-element.82), channel_id=1, source_target_pairs={{0,15},{1,2},{2,1},{3,4},{4,3},{5,6},{6,5},{7,8},{8,7},{9,10},{10,... | collective-permute-start | bytes 24584 | tf_op jit(solution)/shard_map/ppermute | solution.py:722
  63.6 0.7 shard_map.95.order
  64.3 0.0 collective-permute-done.4.near
  64.3 3.0 %collective-permute-done.5.far = f32[16,128]{1,0:T(8,128)S(1)} collective-permute-done((f32[16,128]{1,0:T(8,128)S(1)}, f32[16,128]{1,0:T(8,128)S(1)}, u32[]{:S(2)}, u32[]{:S(2)}) %collective-permute-start.5) | collective-permute-done | bytes 8224 | tf_op jit(solution)/shard_map/ppermute | solution.py:722
  67.3 0.2 shard_map.96
  67.5 10.9 %all_to_all.29.got = f32[8,48,128]{2,1,0:T(8,128)S(1)} all-to-all(f32[8,48,128]{2,1,0:T(8,128)S(1)} %broadcast_in_dim.14), channel_id=1, replica_groups=mesh['gx'=8,'gy'=16] {'gx'}, dimensions={0} | all-to-all | bytes 393216 | tf_op jit(solution)/shard_map/all_to_all | solution.py:706
  78.4 1.4 %shard_map.97 = (f32[64,64]{1,0:T(8,128)}, f32[64,512]{1,0:T(8,128)}) custom-call(f32[8,48,128]{2,1,0:T(8,128)S(1)} %all_to_all.29.got, f32[64,128]{1,0:T(8,128)S(1)} %get-tuple-element.83.coarse, f32[7,96,128]{2,1,0:T(8,128)S(1)} %get-tuple-element.57.order.matrix), custom_call_target="tpu_custom_call" | custom-call | tf_op jit(solution)/shard_map/pallas_call | solution.py:31
  (7 shorter events, 0.1 us)
Async XLA Ops:
  2.2 6.6 %collective-permute-start = (f32[80,128]{1,0:T(8,128)S(1)}, f32[80,128]{1,0:T(8,128)S(1)}, u32[]{:S(2)}, u32[]{:S(2)}) collective-permute-start(f32[80,128]{1,0:T(8,128)S(1)} %get-tuple-element.46), channel_id=1, source_target_pairs={{0,1},{1,0},{2,3},{3,2},{4,5},{5,4},{6,7},{7,6},{8,9},{9,8},{10,11... | collective-permute-start | bytes 122888 | tf_op jit(solution)/shard_map/ppermute | solution.py:722
  2.3 6.5 %collective-permute-start.1 = (f32[80,128]{1,0:T(8,128)S(1)}, f32[80,128]{1,0:T(8,128)S(1)}, u32[]{:S(2)}, u32[]{:S(2)}) collective-permute-start(f32[80,128]{1,0:T(8,128)S(1)} %get-tuple-element.47), channel_id=1, source_target_pairs={{0,15},{1,2},{2,1},{3,4},{4,3},{5,6},{6,5},{7,8},{8,7},{9,10},{10,... | collective-permute-start | bytes 122888 | tf_op jit(solution)/shard_map/ppermute | solution.py:722
  26.5 1.3 %collective-permute-start.2 = (f32[80,128]{1,0:T(8,128)S(1)}, f32[80,128]{1,0:T(8,128)S(1)}, u32[]{:S(2)}, u32[]{:S(2)}) collective-permute-start(f32[80,128]{1,0:T(8,128)S(1)} %get-tuple-element.61.mine), channel_id=1, source_target_pairs={{0,1},{1,0},{2,3},{3,2},{4,5},{5,4},{6,7},{7,6},{8,9},{9,8},{10,11... | collective-permute-start | bytes 122888 | tf_op jit(solution)/shard_map/ppermute | solution.py:710
  51.1 1.3 %collective-permute-start.3 = (f32[32,128]{1,0:T(8,128)S(1)}, f32[32,128]{1,0:T(8,128)S(1)}, u32[]{:S(2)}, u32[]{:S(2)}) collective-permute-start(f32[32,128]{1,0:T(8,128)S(1)} %get-tuple-element.75.mine), channel_id=1, source_target_pairs={{0,1},{1,0},{2,3},{3,2},{4,5},{5,4},{6,7},{7,6},{8,9},{9,8},{10,11... | collective-permute-start | bytes 49160 | tf_op jit(solution)/shard_map/ppermute | solution.py:710
  61.9 2.4 %collective-permute-start.4 = (f32[16,128]{1,0:T(8,128)S(1)}, f32[16,128]{1,0:T(8,128)S(1)}, u32[]{:S(2)}, u32[]{:S(2)}) collective-permute-start(f32[16,128]{1,0:T(8,128)S(1)} %get-tuple-element.81), channel_id=1, source_target_pairs={{0,1},{1,0},{2,3},{3,2},{4,5},{5,4},{6,7},{7,6},{8,9},{9,8},{10,11... | collective-permute-start | bytes 24584 | tf_op jit(solution)/shard_map/ppermute | solution.py:722
  62.0 5.3 %collective-permute-start.5 = (f32[16,128]{1,0:T(8,128)S(1)}, f32[16,128]{1,0:T(8,128)S(1)}, u32[]{:S(2)}, u32[]{:S(2)}) collective-permute-start(f32[16,128]{1,0:T(8,128)S(1)} %get-tuple-element.82), channel_id=1, source_target_pairs={{0,15},{1,2},{2,1},{3,4},{4,3},{5,6},{6,5},{7,8},{8,7},{9,10},{10,... | collective-permute-start | bytes 24584 | tf_op jit(solution)/shard_map/ppermute | solution.py:722

commit v9 on v8

--- a/solution.py
+++ b/solution.py
@@ -197,7 +197,7 @@
     return column(g, 0), column(g, NI - 1), column(a, 0), column(b, 0), column(b, NI - 1), column(x, NI - 1)
 
 
-def x_first_kernel(xs, g, a, b, mult, packed_out):
+def x_first_kernel(xs, order, g, a, b, mult, packed_out):
     f, p, xc, yc, zc, dp = parts(xs)
     lane = lanes(NJ)
     row = lax.broadcasted_iota(jnp.int32, (NJ, NI), 0)
@@ -596,6 +596,12 @@
 def coarse_matrix_kernel(ext, got, *outs):
     e = lax.axis_index("gy")
     lane = lanes(8)
+    source = lax.broadcasted_iota(jnp.int32, (NI, 4 * NI), 0)
+    target = lax.broadcasted_iota(jnp.int32, (NI, 4 * NI), 1)
+    device, at_column = target >> 6, target & 63
+    hit = jnp.logical_and(at_column < 3, source == 10 * device + at_column)
+    hit = jnp.logical_or(hit, jnp.logical_and(at_column > 60, source == 10 * device + at_column - 54))
+    outs[2][...] = jnp.where(hit, 1.0, 0.0).astype(jnp.bfloat16)
 
     def joint(n, J):
         value = jnp.zeros((8, NI), F32)
@@ -645,57 +651,55 @@
     lower, upper = sorted_out(near, far, pl.ds(0, 16))
     res = [lower[:8], lower[8:], *(eight(coarse, J) for J in range(8)), upper[:8], upper[8:]]
     done = relaxed(res, matrix)
+    d = lax.axis_index("gx")
+    odd = lax.rem(d, 2) == 1
     for t in range(4):
-        send[pl.ds(t * 8, 8), :] = jnp.where(lane < 64, done[t], rolled(done[t + 4], 64, 1))
+        both = jnp.where(lane < 64, done[t], rolled(done[t + 4], 64, 1))
+        send[pl.ds(t * 8, 8), :] = jnp.where(odd, rolled(both, 64, 1), both)
     strips = [jnp.zeros((8, NI), F32)] * 2
     for J in range(12):
         at = 16 * (J % 8)
         strip = jnp.where(jnp.logical_and(lane >= at, lane < at + 6), rolled(res[J], at + 1, 1), strips[J // 8])
         strips[J // 8] = jnp.where(jnp.logical_and(lane >= at + 6, lane < at + 12), rolled(res[J], at + 6 - 59, 1), strip)
-    send[pl.ds(32, 8), :] = strips[0]
-    send[pl.ds(40, 8), :] = strips[1]
-
-
-def coarse_last_kernel(got, coarse, matrix, res_out, cor_out, tmp, res_tmp):
+    turn = lax.rem(10 * d + NI - 1, NI)
+    send[pl.ds(32, 8), :] = pltpu.roll(strips[0], turn, 1)
+    send[pl.ds(40, 8), :] = pltpu.roll(strips[1], turn, 1)
+
+
+def coarse_last_kernel(got, coarse, matrix, places, res_out, cor_out, tmp, res_tmp):
     d_own = lax.axis_index("gx")
     lane = lanes(8)
     joint = []
     for J in range(12):
         value = jnp.zeros((8, NI), F32)
+        at = (lane - 16 * (J % 8)) & (NI - 1)
         for d in range(GX):
-            low = 10 * d - 1
-            moved = rolled(got[d, pl.ds(32 + 8 * (J // 8), 8), :], low - 16 * (J % 8), 1)
-            value = value + jnp.where(jnp.logical_and(lane >= low, lane < low + 12), moved, 0.0)
-        joint.append(value)
-    done = relaxed(joint, matrix)
+            strip = got[d, pl.ds(32 + 8 * (J // 8), 8), :]
+            value = value + jnp.where(jnp.logical_and(at >= 10 * d - 1, at < 10 * d + 11), strip, 0.0)
+        joint.append(rolled(value, -16 * (J % 8), 1))
+    done = jnp.concatenate(relaxed(joint, matrix), axis=0)
+    placed = exact_dot(done, places[...])
+    end = jnp.logical_or((lane & 63) < 3, (lane & 63) > 60)
+    turn = lax.rem(NI - 10 * d_own, NI)
     for J in range(8):
-        ends = joint[J + 2]
-        mine = rolled(ends, 0, 1)
-        for d in range(1, GX):
-            mine = jnp.where(d_own == d, rolled(ends, -10 * d, 1), mine)
+        mine = pltpu.roll(joint[J + 2], turn, 1)
         mine = jnp.where(lane == 0, mine, jnp.where(lane == 63, rolled(mine, 54, 1), eight(coarse, J)))
         res_tmp[pl.ds(J, 8, stride=8), :] = mine
         rows = pl.ds((J % 4) * 8, 8)
         for m in range(4):
             even, odd = got[2 * m, rows, :], got[2 * m + 1, rows, :]
             if J < 4:
-                odd = rolled(odd, 64, 1)
+                value = jnp.where(lane < 64, even, odd)
             else:
-                even = rolled(even, 64, 1)
-            value = jnp.where(lane < 64, even, odd)
-            for d in (2 * m, 2 * m + 1):
-                start = 64 * (d % 2)
-                left = jnp.logical_and(lane >= start, lane < start + 3)
-                right = jnp.logical_and(lane >= start + 61, lane < start + 64)
-                value = jnp.where(left, rolled(done[J], start - 10 * d, 1), value)
-                value = jnp.where(right, rolled(done[J], start + 54 - 10 * d, 1), value)
-            tmp[m, pl.ds(J, 8, stride=8), :] = value
+                value = rolled(jnp.where(lane < 64, odd, even), 64, 1)
+            right = placed[J * 8 : J * 8 + 8, m * NI : (m + 1) * NI]
+            tmp[m, pl.ds(J, 8, stride=8), :] = jnp.where(end, right, value)
     for m in range(4):
         cor_out[:, pl.ds(m * NI, NI)] = tmp[m]
     res_out[...] = res_tmp[:, :64]
 
 
-def field_kernel(fluxes, yg, ya, yb, field):
+def field_kernel(order, fluxes, yg, ya, yb, field):
     for j in range(NJ):
         place = pl.ds(j * NK, NK)
         field[pl.ds(j, NK, stride=NJ), :] = yg[place, :] - ya[place, :] * fluxes[0] + yb[place, :] * fluxes[1]
@@ -734,8 +738,9 @@
         hbm=6,
         sems=6,
     )
+    mine = near
     near, far = swap(near, far)
-    g, a, b, mult, packed = call(x_first_kernel, [whole, whole, whole, kept, sds(NJ, NI)], xs, flops=10**8)
+    g, a, b, mult, packed = call(x_first_kernel, [whole, whole, whole, kept, sds(NJ, NI)], xs, mine, flops=10**8)
     below, g, a, b, mult, send, ext = call(
         x_rim_kernel,
         [sds(NK, NI), whole, whole, whole, kept, sds(NJ + 32, NI), sds(4 * 96, NI)],
@@ -750,7 +755,9 @@
         scratch=[(GX + 1, NJ, NI), (GX + 1, NJ, NI), (ROWS, NI), (ROWS, NI), (ROWS, NI)],
     )
     theirs = other_core(send)
-    own, ends = call(coarse_matrix_kernel, [sds(7, 96, NI)] * 2, ext, got_coef, flops=10**7)
+    own, ends, places = call(
+        coarse_matrix_kernel, [sds(7, 96, NI)] * 2 + [jax.ShapeDtypeStruct((NI, 4 * NI), jnp.bfloat16)], ext, got_coef, flops=10**7
+    )
     send, joint, inner = call(
         join_first_kernel, [sds(5 * NK, NI), sds(5, NK, NI), sds(NK, NI)], ends, send, theirs
     )
@@ -776,12 +783,13 @@
         xs, below, got, joint, inner, yg, ya, yb, yred, cl,
         scratch=[(CHIPS + 1, NK, NI), (ROWS, NI), (128, NI), (ROWS, NI)],
     )
+    mine = near
     near, far = swap(near, far)
-    (field,) = call(field_kernel, [whole], fluxes, yg, ya, yb, flops=10**7)
+    (field,) = call(field_kernel, [whole], mine, fluxes, yg, ya, yb, flops=10**7)
     (send,) = call(coarse_own_kernel, [sds(48, NI)], field, near, far, coarse, own, hbm=1)
     got = spread(send, "gx", GX)
     res, cor = call(
-        coarse_last_kernel, [sds(64, 64), sds(64, 4 * NI)], got, coarse, ends, scratch=[(4, 64, NI), (64, NI)]
+        coarse_last_kernel, [sds(64, 64), sds(64, 4 * NI)], got, coarse, ends, places, scratch=[(4, 64, NI), (64, NI)]
     )
     return field.reshape(NK, NJ, NI), res.reshape(8, 8, 64), cor.reshape(8, 8, 512)
 

time: 80.1 us -> 79.4 us (level)
  starting transfers between devices: 5.87 us -> 4.62 us
    ppermute x4, starting transfers between devices: 5.7 us -> 4.45 us  [swap(): return (lax.ppermute(near, 'gy', pairs), lax.ppermute(far, 'gy', others))]
where the time goes in v9:
time: 79.4 us; the launch traced here: 79.1 us
  blocking collectives  57.8 us (73%)
  Pallas kernels  10.9 us (14%)
  waiting for transfers between devices  4.94 us (6%)
  starting transfers between devices  4.62 us (6%)
    all_to_all x3, blocking collectives, spread(): return lax.all_to_all(many, axis, split_axis=0, concat_axis=0, tiled=True)  37.8 us
    all_to_all x2, blocking collectives, spread_by_core(): lax.all_to_all(many, 'gy', split_axis=0, concat_axis=0, tiled=True, axis_...  20.1 us
    pallas_call x13, Pallas kernels, call(): pl.pallas_call(kernel, out_shape=outs, in_specs=[outside] * hbm + [spec]...  10.9 us
    ppermute x4, starting transfers between devices, swap(): return (lax.ppermute(near, 'gy', pairs), lax.ppermute(far, 'gy', others))  4.45 us
    ppermute x4, waiting for transfers between devices, swap(): return (lax.ppermute(near, 'gy', pairs), lax.ppermute(far, 'gy', others))  3.49 us
  transfers between devices with their start and end apart: 6, of which 3 were waited for; matrix products, arithmetic and copies ran while one was open for 0% of the time, Pallas kernels for 5%

profile of v9, /device:TPU:0, one launch (start us, length us, event | category | flops | bytes accessed | tf_op | source)
XLA Modules:
  0.0 79.1 jit_solution(3615786321123959257)
XLA Ops:
  0.6 1.6 %shard_map.85 = (f32[1536,128]{1,0:T(8,128)S(1)}, f32[80,128]{1,0:T(8,128)S(1)}, f32[80,128]{1,0:T(8,128)S(1)}, f32[128,128]{1,0:T(8,128)S(1)}) custom-call(f32[256,128]{1,0:T(8,128)} %bitcast.10, f32[256,128]{1,0:T(8,128)} %bitcast.11, f32[256,128]{1,0:T(8,128)} %bitcast.12, f32[256,128]{1,0:T(8,128)} %bitcast.13, f32[256,128]{1,0:T(8,128)} %bitcast.14, ...), custom_call_target="tpu_custom_call" | custom-call | tf_op jit(solution)/shard_map/pallas_call | solution.py:31
  2.2 3.4 %collective-permute-start.1 = (f32[80,128]{1,0:T(8,128)S(1)}, f32[80,128]{1,0:T(8,128)S(1)}, u32[]{:S(2)}, u32[]{:S(2)}) collective-permute-start(f32[80,128]{1,0:T(8,128)S(1)} %get-tuple-element.48), channel_id=1, source_target_pairs={{0,15},{1,2},{2,1},{3,4},{4,3},{5,6},{6,5},{7,8},{8,7},{9,10},{10,... | collective-permute-start | bytes 122888 | tf_op jit(solution)/shard_map/ppermute | solution.py:726
  5.6 0.0 collective-permute-start
  5.6 2.6 %shard_map.86 = (f32[256,128]{1,0:T(8,128)S(1)}, f32[256,128]{1,0:T(8,128)S(1)}, f32[256,128]{1,0:T(8,128)S(1)}, f32[3840,128]{1,0:T(8,128)S(1)}, f32[16,128]{1,0:T(8,128)S(1)}) custom-call(f32[1536,128]{1,0:T(8,128)S(1)} %get-tuple-element.46.xs, f32[80,128]{1,0:T(8,128)S(1)} %get-tuple-element.47.order), custom_call_target="tpu_custom_call" | custom-call | flops 100000000 | bytes 1048576 | tf_op jit(solution)/shard_map/pallas_call | solution.py:31
  8.2 0.0 collective-permute-done.1.far
  8.2 0.0 collective-permute-done.near
  8.2 1.0 %shard_map.87 = (f32[16,128]{1,0:T(8,128)S(1)}, f32[256,128]{1,0:T(8,128)S(1)}, f32[256,128]{1,0:T(8,128)S(1)}, f32[256,128]{1,0:T(8,128)S(1)}, f32[3840,128]{1,...) custom-call(f32[1536,128]{1,0:T(8,128)S(1)} %get-tuple-element.46.xs, ...), custom_call_target="tpu_custom_call", output_to_operand_aliasing={{1}: (5, {}), {2}: (6, {}), {3}: (7, {}), {4}: (8, {})} | custom-call | tf_op jit(solution)/shard_map/pallas_call | solution.py:31
  9.2 16.2 %all_to_all.25.got = f32[8,48,128]{2,1,0:T(8,128)S(1)} all-to-all(f32[8,48,128]{2,1,0:T(8,128)S(1)} %broadcast_in_dim.10), channel_id=1, replica_groups=mesh['gx'=8,'gy'=16] {'gx'}, dimensions={0} | all-to-all | bytes 393216 | tf_op jit(solution)/shard_map/all_to_all | solution.py:710
  25.4 0.7 shard_map.89
  26.1 0.1 collective-permute-start.2
  26.2 0.9 %shard_map.88 = (f32[7,96,128]{2,1,0:T(8,128)S(1)}, f32[7,96,128]{2,1,0:T(8,128)S(1)}, bf16[128,512]{1,0:T(8,128)(2,1)S(1)}) custom-call(f32[384,128]{1,0:T(8,128)S(1)} %get-tuple-element.56.ext, f32[8,48,128]{2,1,0:T(8,128)S(1)} %all_to_all.25.got), custom_call_target="tpu_custom_call" | custom-call | flops 10000000 | bytes 1048576 | tf_op jit(solution)/shard_map/pallas_call | solution.py:31
  27.1 0.3 collective-permute-done.2.theirs
  27.4 11.1 %all_to_all.26.got = f32[8,80,128]{2,1,0:T(8,128)S(1)} all-to-all(f32[8,80,128]{2,1,0:T(8,128)S(1)} %broadcast_in_dim.11), channel_id=1, replica_groups={{0,2,4,6,8,10,12,14},{1,3,5,7,9,11,13,15},{16,18,20,22,24,26,28,30},{17..., dimensions={0} | all-to-all | bytes 655360 | tf_op jit(solution)/shard_map/all_to_all | solution.py:720
  38.5 1.0 %shard_map.91 = (f32[256,128]{1,0:T(8,128)S(1)}, f32[24,16,128]{2,1,0:T(8,128)S(1)}, f32[8,128]{1,0:T(8,128)S(1)}) custom-call(f32[1536,128]{1,0:T(8,128)S(1)} %get-tuple-element.46.xs, f32[16,128]{1,0:T(8,128)S(1)} %get-tuple-element.55.below, f32[8,80,128]{2,1,0:T(8,128)S(1)} %all_to_all.26.got, f32[5,16,128]{2,1,0:T(8,128)S(1)} %get-tuple-element.64.joint, ...), custom_call_target="tpu_custom_call" | custom-call | tf_op jit(solution)/shard_map/pallas_call | solution.py:31
  39.5 10.7 %all_to_all.27.got = f32[8,8,128]{2,1,0:T(8,128)S(1)} all-to-all(f32[8,8,128]{2,1,0:T(8,128)S(1)} %broadcast_in_dim.12), channel_id=1, replica_groups=mesh['gx'=8,'gy'=16] {'gx'}, dimensions={0} | all-to-all | bytes 65536 | tf_op jit(solution)/shard_map/all_to_all | solution.py:710
  50.2 0.5 shard_map.92
  50.7 0.1 collective-permute-start.3
  50.8 1.2 %collective-permute-done.3.theirs = f32[32,128]{1,0:T(8,128)S(1)} collective-permute-done((f32[32,128]{1,0:T(8,128)S(1)}, f32[32,128]{1,0:T(8,128)S(1)}, u32[]{:S(2)}, u32[]{:S(2)}) %collective-permute-start.3) | collective-permute-done | bytes 16416 | tf_op jit(solution)/shard_map/ppermute | solution.py:714
  52.0 9.0 %all_to_all.28.got = f32[8,32,128]{2,1,0:T(8,128)S(1)} all-to-all(f32[8,32,128]{2,1,0:T(8,128)S(1)} %broadcast_in_dim.13), channel_id=1, replica_groups={{0,2,4,6,8,10,12,14},{1,3,5,7,9,11,13,15},{16,18,20,22,24,26,28,30},{17..., dimensions={0} | all-to-all | bytes 262144 | tf_op jit(solution)/shard_map/all_to_all | solution.py:720
  61.0 0.5 shard_map.94
  61.5 0.1 collective-permute-start.5
  61.6 0.9 %collective-permute-start.4 = (f32[16,128]{1,0:T(8,128)S(1)}, f32[16,128]{1,0:T(8,128)S(1)}, u32[]{:S(2)}, u32[]{:S(2)}) collective-permute-start(f32[16,128]{1,0:T(8,128)S(1)} %get-tuple-element.81.order), channel_id=1, source_target_pairs={{0,1},{1,0},{2,3},{3,2},{4,5},{5,4},{6,7},{7,6},{8,9},{9,8},{10,11... | collective-permute-start | bytes 24584 | tf_op jit(solution)/shard_map/ppermute | solution.py:726
  62.6 0.7 shard_map.95.order
  63.3 3.5 %collective-permute-done.5.far = f32[16,128]{1,0:T(8,128)S(1)} collective-permute-done((f32[16,128]{1,0:T(8,128)S(1)}, f32[16,128]{1,0:T(8,128)S(1)}, u32[]{:S(2)}, u32[]{:S(2)}) %collective-permute-start.5) | collective-permute-done | bytes 8224 | tf_op jit(solution)/shard_map/ppermute | solution.py:726
  66.8 0.0 collective-permute-done.4.near
  66.8 0.3 shard_map.96
  67.1 10.9 %all_to_all.29.got = f32[8,48,128]{2,1,0:T(8,128)S(1)} all-to-all(f32[8,48,128]{2,1,0:T(8,128)S(1)} %broadcast_in_dim.14), channel_id=1, replica_groups=mesh['gx'=8,'gy'=16] {'gx'}, dimensions={0} | all-to-all | bytes 393216 | tf_op jit(solution)/shard_map/all_to_all | solution.py:710
  78.0 1.1 %shard_map.97 = (f32[64,64]{1,0:T(8,128)}, f32[64,512]{1,0:T(8,128)}) custom-call(f32[8,48,128]{2,1,0:T(8,128)S(1)} %all_to_all.29.got, f32[64,128]{1,0:T(8,128)S(1)} %get-tuple-element.84.coarse, f32[7,96,128]{2,1,0:T(8,128)S(1)} %get-tuple-element.58.order.matrix, bf16[128,512]{1,0:T(8,128)(2,1)S(1)} %get-tuple-element.86.places), custom_call_target="tpu_custom_call" | custom-call | tf_op jit(solution)/shard_map/pallas_call | solution.py:31
  (7 shorter events, 0.1 us)
Async XLA Ops:
  2.2 5.9 %collective-permute-start.1 = (f32[80,128]{1,0:T(8,128)S(1)}, f32[80,128]{1,0:T(8,128)S(1)}, u32[]{:S(2)}, u32[]{:S(2)}) collective-permute-start(f32[80,128]{1,0:T(8,128)S(1)} %get-tuple-element.48), channel_id=1, source_target_pairs={{0,15},{1,2},{2,1},{3,4},{4,3},{5,6},{6,5},{7,8},{8,7},{9,10},{10,... | collective-permute-start | bytes 122888 | tf_op jit(solution)/shard_map/ppermute | solution.py:726
  5.6 2.6 %collective-permute-start = (f32[80,128]{1,0:T(8,128)S(1)}, f32[80,128]{1,0:T(8,128)S(1)}, u32[]{:S(2)}, u32[]{:S(2)}) collective-permute-start(f32[80,128]{1,0:T(8,128)S(1)} %get-tuple-element.47.order), channel_id=1, source_target_pairs={{0,1},{1,0},{2,3},{3,2},{4,5},{5,4},{6,7},{7,6},{8,9},{9,8},{10,11... | collective-permute-start | bytes 122888 | tf_op jit(solution)/shard_map/ppermute | solution.py:726
  26.1 1.3 %collective-permute-start.2 = (f32[80,128]{1,0:T(8,128)S(1)}, f32[80,128]{1,0:T(8,128)S(1)}, u32[]{:S(2)}, u32[]{:S(2)}) collective-permute-start(f32[80,128]{1,0:T(8,128)S(1)} %get-tuple-element.62.mine), channel_id=1, source_target_pairs={{0,1},{1,0},{2,3},{3,2},{4,5},{5,4},{6,7},{7,6},{8,9},{9,8},{10,11... | collective-permute-start | bytes 122888 | tf_op jit(solution)/shard_map/ppermute | solution.py:714
  50.7 1.3 %collective-permute-start.3 = (f32[32,128]{1,0:T(8,128)S(1)}, f32[32,128]{1,0:T(8,128)S(1)}, u32[]{:S(2)}, u32[]{:S(2)}) collective-permute-start(f32[32,128]{1,0:T(8,128)S(1)} %get-tuple-element.76.mine), channel_id=1, source_target_pairs={{0,1},{1,0},{2,3},{3,2},{4,5},{5,4},{6,7},{7,6},{8,9},{9,8},{10,11... | collective-permute-start | bytes 49160 | tf_op jit(solution)/shard_map/ppermute | solution.py:714
  61.5 5.3 %collective-permute-start.5 = (f32[16,128]{1,0:T(8,128)S(1)}, f32[16,128]{1,0:T(8,128)S(1)}, u32[]{:S(2)}, u32[]{:S(2)}) collective-permute-start(f32[16,128]{1,0:T(8,128)S(1)} %get-tuple-element.83), channel_id=1, source_target_pairs={{0,15},{1,2},{2,1},{3,4},{4,3},{5,6},{6,5},{7,8},{8,7},{9,10},{10,... | collective-permute-start | bytes 24584 | tf_op jit(solution)/shard_map/ppermute | solution.py:726
  61.6 5.1 %collective-permute-start.4 = (f32[16,128]{1,0:T(8,128)S(1)}, f32[16,128]{1,0:T(8,128)S(1)}, u32[]{:S(2)}, u32[]{:S(2)}) collective-permute-start(f32[16,128]{1,0:T(8,128)S(1)} %get-tuple-element.81.order), channel_id=1, source_target_pairs={{0,1},{1,0},{2,3},{3,2},{4,5},{5,4},{6,7},{7,6},{8,9},{9,8},{10,11... | collective-permute-start | bytes 24584 | tf_op jit(solution)/shard_map/ppermute | solution.py:726

commit v10 on v9

--- a/solution.py
+++ b/solution.py
@@ -228,7 +228,7 @@
     packed_out[...] = packed
 
 
-def x_rim_kernel(xs, near, far, coarse, packed, g_in, a_in, b_in, mult_in, below, g, a, b, mult, send, ext):
+def x_rim_kernel(xs, near, far, coarse, packed, g_in, a_in, b_in, mult_in, below, g, a, b, mult, send, near_out, far_out, coarse_out):
     f, p, xc, yc, zc, dp = parts(xs)
     lane = lanes(NK)
     row = lax.broadcasted_iota(jnp.int32, (NK, NI), 0)
@@ -239,6 +239,9 @@
         low = rolled(top, 1, 0)
         return low, top, low * rolled(v, 1, 0) + top * rolled(v, -1, 0)
 
+    near_out[...] = near[pl.ds(2 * NK, 48), :]
+    far_out[...] = far[pl.ds(2 * NK, 48), :]
+    coarse_out[...] = coarse[...]
     p_below, p_above = sorted_out(near, far, pl.ds(0, NK))
     y_left, _ = sorted_out(near, far, pl.ds(NK, NK))
     below[...] = y_left
@@ -269,15 +272,14 @@
     was = packed[...]
     was = jnp.where(row == 0, line, was)
     send[pl.ds(0, NJ), :] = jnp.where(jnp.logical_and(row == NJ - 1, lane < 2 * NK), last, was)
-    coarse_share(near, far, coarse, send, ext)
-
-
-def coarse_share(near, far, coarse, send, ext):
+
+
+def coarse_share_kernel(near, far, coarse, send, ext):
     wide = lanes(8)
     level_k = lax.broadcasted_iota(jnp.int32, (8, NI), 0)
     fields = [[], [], [], []]
     for q in range(2):
-        lower, upper = sorted_out(near, far, pl.ds(2 * NK + q * 24, 24))
+        lower, upper = sorted_out(near, far, pl.ds(q * 24, 24))
         rows = [lower[n * 8 : n * 8 + 8] for n in range(3)]
         rows += [coarse[pl.ds(q * 64 + n * 8, 8), :] for n in range(8)]
         rows += [upper[n * 8 : n * 8 + 8] for n in range(2)]
@@ -296,7 +298,7 @@
             share = jnp.where(jnp.logical_and(wide >= at, wide < at + 5), first, shares[n])
             shares[n] = jnp.where(jnp.logical_and(wide >= at + 5, wide < at + 10), last, share)
     for n in range(4):
-        send[pl.ds(NJ + n * 8, 8), :] = shares[n]
+        send[pl.ds(n * 8, 8), :] = shares[n]
 
 
 def x_second_solve(rhs, kept):
@@ -448,7 +450,7 @@
     inner[...] = base
 
 
-def join_again_kernel(mine, theirs, joint, send, inner):
+def join_again_kernel(order, mine, theirs, joint, send, inner):
     odd = lax.rem(lax.axis_index("gy"), 2) == 1
     block = lambda ref, q: ref[pl.ds(q * NK, NK), :]
     low = [jnp.where(odd, block(theirs, q), block(mine, q)) for q in range(2)]
@@ -478,7 +480,7 @@
         terms[pl.ds(j, NK, stride=NJ), :] = before + after
 
 
-def x_again_kernel(xs, below, got, joint, inner, yg, ya, yb, mult, g, yred, send, fs, field, terms):
+def x_again_kernel(xs, below, got, joint, inner, share, yg, ya, yb, mult, g, yred, send, fs, field, terms):
     f, p, xc, yc, zc, dp = parts(xs)
     part = lambda n, q: got[n, pl.ds(q * NK, NK), :]
     prev = None
@@ -518,12 +520,15 @@
             mine = rhs[(k - k0) * NJ : (k - k0 + 1) * NJ]
             packed = jnp.where(lane == k, column(mine, 0), packed)
             packed = jnp.where(lane == NK + k, column(mine, NI - 1), packed)
-    send[...] = jnp.where(lanes(8) < 2 * NK, packed[:8], rolled(packed[8:], 2 * NK, 1))
+    send[pl.ds(0, 8), :] = jnp.where(lanes(8) < 2 * NK, packed[:8], rolled(packed[8:], 2 * NK, 1))
+    send[pl.ds(8, 32), :] = share[...]
 
 
 def y_again_kernel(xs, got, g, a, b, xred, cl, yw, yinv, yg, send, fs, field, src):
     f, p, xc, yc, zc, dp = parts(xs)
-    part = lambda n, q: jnp.concatenate([rolled(got[n], -NK * q, 1), rolled(got[n], -NK * (q + 2), 1)], axis=0)
+    part = lambda n, q: jnp.concatenate(
+        [rolled(got[n, pl.ds(0, 8), :], -NK * q, 1), rolled(got[n, pl.ds(0, 8), :], -NK * (q + 2), 1)], axis=0
+    )
     x_fluxes(
         fs,
         lambda n: part(n + 1, 0) - part(n, 1),
@@ -606,7 +611,7 @@
     def joint(n, J):
         value = jnp.zeros((8, NI), F32)
         for d in range(GX):
-            moved = rolled(got[d, pl.ds(NJ + n * 8, 8), :], 10 * (d - J), 1)
+            moved = rolled(got[d, pl.ds(8 + n * 8, 8), :], 10 * (d - J), 1)
             value = jnp.where(jnp.logical_and(lane >= 10 * d, lane < 10 * d + 10), moved, value)
         return value
 
@@ -741,13 +746,13 @@
     mine = near
     near, far = swap(near, far)
     g, a, b, mult, packed = call(x_first_kernel, [whole, whole, whole, kept, sds(NJ, NI)], xs, mine, flops=10**8)
-    below, g, a, b, mult, send, ext = call(
+    below, g, a, b, mult, send, *sides = call(
         x_rim_kernel,
-        [sds(NK, NI), whole, whole, whole, kept, sds(NJ + 32, NI), sds(4 * 96, NI)],
+        [sds(NK, NI), whole, whole, whole, kept, sds(NJ, NI), sds(48, NI), sds(48, NI), sds(128, NI)],
         xs, near, far, coef, packed, g, a, b, mult,
         aliases={5: 1, 6: 2, 7: 3, 8: 4},
     )
-    got_coef = got = spread(send, "gx", GX)
+    got = spread(send, "gx", GX)
     yg, ya, yb, yw, yinv, xred, cl, send = call(
         y_first_kernel,
         [whole] * 5 + [sds(3 * GX, NJ, NI), sds(NJ, NI), sds(5 * NK, NI)],
@@ -755,17 +760,15 @@
         scratch=[(GX + 1, NJ, NI), (GX + 1, NJ, NI), (ROWS, NI), (ROWS, NI), (ROWS, NI)],
     )
     theirs = other_core(send)
-    own, ends, places = call(
-        coarse_matrix_kernel, [sds(7, 96, NI)] * 2 + [jax.ShapeDtypeStruct((NI, 4 * NI), jnp.bfloat16)], ext, got_coef, flops=10**7
-    )
+    share, ext = call(coarse_share_kernel, [sds(32, NI), sds(4 * 96, NI)], *sides, flops=10**7)
     send, joint, inner = call(
-        join_first_kernel, [sds(5 * NK, NI), sds(5, NK, NI), sds(NK, NI)], ends, send, theirs
+        join_first_kernel, [sds(5 * NK, NI), sds(5, NK, NI), sds(NK, NI)], share, send, theirs
     )
     got = spread_by_core(send)
     g, yred, send = call(
         x_again_kernel,
-        [whole, sds(3 * CHIPS, NK, NI), sds(8, NI)],
-        xs, below, got, joint, inner, yg, ya, yb, mult,
+        [whole, sds(3 * CHIPS, NK, NI), sds(40, NI)],
+        xs, below, got, joint, inner, share, yg, ya, yb, mult,
         scratch=[(CHIPS + 1, NK, NI), (ROWS, NI), (ROWS, NI)],
     )
     got = spread(send, "gx", GX)
@@ -775,7 +778,11 @@
         xs, got, g, a, b, xred, cl, yw, yinv,
         scratch=[(GX + 1, NJ, NI), (ROWS, NI), (ROWS, NI)],
     )
-    send, inner = call(join_again_kernel, [sds(2 * NK, NI), sds(NK, NI)], send, other_core(send), joint)
+    theirs = other_core(send)
+    own, ends, places = call(
+        coarse_matrix_kernel, [sds(7, 96, NI)] * 2 + [jax.ShapeDtypeStruct((NI, 4 * NI), jnp.bfloat16)], ext, got, flops=10**7
+    )
+    send, inner = call(join_again_kernel, [sds(2 * NK, NI), sds(NK, NI)], ends, send, theirs, joint)
     got = spread_by_core(send)
     fluxes, coarse, near, far = call(
         residual_kernel,

time: 79.4 us -> 79.2 us (level)
    pallas_call x13 -> x14, Pallas kernels: 10.9 us -> 11 us  [call(): pl.pallas_call(kernel, out_shape=outs, in_specs=[outside] * hbm + [spec]...]
  transfers between devices with their start and end apart: 6 -> 6, of which waited for: 3 -> 3; matrix products, arithmetic and copies ran while one was open for 0% -> 0% of each run, Pallas kernels for 5% -> 6%
where the time goes in v10:
time: 79.2 us; the launch traced here: 78.9 us
  blocking collectives  57.8 us (73%)
  Pallas kernels  11 us (14%)
  waiting for transfers between devices  4.71 us (6%)
  starting transfers between devices  4.59 us (6%)
    all_to_all x3, blocking collectives, spread(): return lax.all_to_all(many, axis, split_axis=0, concat_axis=0, tiled=True)  37.6 us
    all_to_all x2, blocking collectives, spread_by_core(): lax.all_to_all(many, 'gy', split_axis=0, concat_axis=0, tiled=True, axis_...  20.2 us
    pallas_call x14, Pallas kernels, call(): pl.pallas_call(kernel, out_shape=outs, in_specs=[outside] * hbm + [spec]...  11 us
    ppermute x4, starting transfers between devices, swap(): return (lax.ppermute(near, 'gy', pairs), lax.ppermute(far, 'gy', others))  4.42 us
    ppermute x4, waiting for transfers between devices, swap(): return (lax.ppermute(near, 'gy', pairs), lax.ppermute(far, 'gy', others))  3.52 us
  transfers between devices with their start and end apart: 6, of which 3 were waited for; matrix products, arithmetic and copies ran while one was open for 0% of the time, Pallas kernels for 6%

profile of v10, /device:TPU:0, one launch (start us, length us, event | category | flops | bytes accessed | tf_op | source)
XLA Modules:
  0.0 78.9 jit_solution(17616416733798018499)
XLA Ops:
  0.6 1.6 %shard_map.85 = (f32[1536,128]{1,0:T(8,128)S(1)}, f32[80,128]{1,0:T(8,128)S(1)}, f32[80,128]{1,0:T(8,128)S(1)}, f32[128,128]{1,0:T(8,128)S(1)}) custom-call(f32[256,128]{1,0:T(8,128)} %bitcast.10, f32[256,128]{1,0:T(8,128)} %bitcast.11, f32[256,128]{1,0:T(8,128)} %bitcast.12, f32[256,128]{1,0:T(8,128)} %bitcast.13, f32[256,128]{1,0:T(8,128)} %bitcast.14, ...), custom_call_target="tpu_custom_call" | custom-call | tf_op jit(solution)/shard_map/pallas_call | solution.py:31
  2.2 3.4 %collective-permute-start.1 = (f32[80,128]{1,0:T(8,128)S(1)}, f32[80,128]{1,0:T(8,128)S(1)}, u32[]{:S(2)}, u32[]{:S(2)}) collective-permute-start(f32[80,128]{1,0:T(8,128)S(1)} %get-tuple-element.52), channel_id=1, source_target_pairs={{0,15},{1,2},{2,1},{3,4},{4,3},{5,6},{6,5},{7,8},{8,7},{9,10},{10,... | collective-permute-start | bytes 122888 | tf_op jit(solution)/shard_map/ppermute | solution.py:731
  5.6 0.0 collective-permute-start
  5.6 2.6 %shard_map.86 = (f32[256,128]{1,0:T(8,128)S(1)}, f32[256,128]{1,0:T(8,128)S(1)}, f32[256,128]{1,0:T(8,128)S(1)}, f32[3840,128]{1,0:T(8,128)S(1)}, f32[16,128]{1,0:T(8,128)S(1)}) custom-call(f32[1536,128]{1,0:T(8,128)S(1)} %get-tuple-element.50.xs, f32[80,128]{1,0:T(8,128)S(1)} %get-tuple-element.51.order), custom_call_target="tpu_custom_call" | custom-call | flops 100000000 | bytes 1048576 | tf_op jit(solution)/shard_map/pallas_call | solution.py:31
  8.2 0.0 collective-permute-done.1.far
  8.2 0.0 collective-permute-done.near
  8.2 0.8 %shard_map.87 = (f32[16,128]{1,0:T(8,128)S(1)}, f32[256,128]{1,0:T(8,128)S(1)}, f32[256,128]{1,0:T(8,128)S(1)}, f32[256,128]{1,0:T(8,128)S(1)}, f32[3840,128]{1,...) custom-call(f32[1536,128]{1,0:T(8,128)S(1)} %get-tuple-element.50.xs, ...), custom_call_target="tpu_custom_call", output_to_operand_aliasing={{1}: (5, {}), {2}: (6, {}), {3}: (7, {}), {4}: (8, {})} | custom-call | tf_op jit(solution)/shard_map/pallas_call | solution.py:31
  9.0 15.3 %all_to_all.25.got = f32[8,16,128]{2,1,0:T(8,128)S(1)} all-to-all(f32[8,16,128]{2,1,0:T(8,128)S(1)} %broadcast_in_dim.10), channel_id=1, replica_groups=mesh['gx'=8,'gy'=16] {'gx'}, dimensions={0} | all-to-all | bytes 131072 | tf_op jit(solution)/shard_map/all_to_all | solution.py:715
  24.3 0.7 shard_map.89
  25.0 0.1 collective-permute-start.2
  25.1 0.3 shard_map.88
  25.3 1.0 %collective-permute-done.2.theirs = f32[80,128]{1,0:T(8,128)S(1)} collective-permute-done((f32[80,128]{1,0:T(8,128)S(1)}, f32[80,128]{1,0:T(8,128)S(1)}, u32[]{:S(2)}, u32[]{:S(2)}) %collective-permute-start.2) | collective-permute-done | bytes 40992 | tf_op jit(solution)/shard_map/ppermute | solution.py:719
  26.3 11.2 %all_to_all.26.got = f32[8,80,128]{2,1,0:T(8,128)S(1)} all-to-all(f32[8,80,128]{2,1,0:T(8,128)S(1)} %broadcast_in_dim.11), channel_id=1, replica_groups={{0,2,4,6,8,10,12,14},{1,3,5,7,9,11,13,15},{16,18,20,22,24,26,28,30},{17..., dimensions={0} | all-to-all | bytes 655360 | tf_op jit(solution)/shard_map/all_to_all | solution.py:725
  37.6 1.0 %shard_map.91 = (f32[256,128]{1,0:T(8,128)S(1)}, f32[24,16,128]{2,1,0:T(8,128)S(1)}, f32[40,128]{1,0:T(8,128)S(1)}) custom-call(f32[1536,128]{1,0:T(8,128)S(1)} %get-tuple-element.50.xs, f32[16,128]{1,0:T(8,128)S(1)} %get-tuple-element.59.below, f32[8,80,128]{2,1,0:T(8,128)S(1)} %all_to_all.26.got, f32[5,16,128]{2,1,0:T(8,128)S(1)} %get-tuple-element.71.joint, ...), custom_call_target="tpu_custom_call" | custom-call | tf_op jit(solution)/shard_map/pallas_call | solution.py:31
  38.6 11.2 %all_to_all.27.got = f32[8,40,128]{2,1,0:T(8,128)S(1)} all-to-all(f32[8,40,128]{2,1,0:T(8,128)S(1)} %broadcast_in_dim.12), channel_id=1, replica_groups=mesh['gx'=8,'gy'=16] {'gx'}, dimensions={0} | all-to-all | bytes 327680 | tf_op jit(solution)/shard_map/all_to_all | solution.py:715
  49.8 0.5 shard_map.93
  50.3 0.1 collective-permute-start.3
  50.4 0.9 %shard_map.92 = (f32[7,96,128]{2,1,0:T(8,128)S(1)}, f32[7,96,128]{2,1,0:T(8,128)S(1)}, bf16[128,512]{1,0:T(8,128)(2,1)S(1)}) custom-call(f32[384,128]{1,0:T(8,128)S(1)} %get-tuple-element.63.ext, f32[8,40,128]{2,1,0:T(8,128)S(1)} %all_to_all.27.got), custom_call_target="tpu_custom_call" | custom-call | flops 10000000 | bytes 1048576 | tf_op jit(solution)/shard_map/pallas_call | solution.py:31
  51.3 0.2 collective-permute-done.3.theirs
  51.6 9.0 %all_to_all.28.got = f32[8,32,128]{2,1,0:T(8,128)S(1)} all-to-all(f32[8,32,128]{2,1,0:T(8,128)S(1)} %broadcast_in_dim.13), channel_id=1, replica_groups={{0,2,4,6,8,10,12,14},{1,3,5,7,9,11,13,15},{16,18,20,22,24,26,28,30},{17..., dimensions={0} | all-to-all | bytes 262144 | tf_op jit(solution)/shard_map/all_to_all | solution.py:725
  60.6 0.5 shard_map.95
  61.1 0.2 collective-permute-start.5
  61.4 0.8 %collective-permute-start.4 = (f32[16,128]{1,0:T(8,128)S(1)}, f32[16,128]{1,0:T(8,128)S(1)}, u32[]{:S(2)}, u32[]{:S(2)}) collective-permute-start(f32[16,128]{1,0:T(8,128)S(1)} %get-tuple-element.89.order), channel_id=1, source_target_pairs={{0,1},{1,0},{2,3},{3,2},{4,5},{5,4},{6,7},{7,6},{8,9},{9,8},{10,11... | collective-permute-start | bytes 24584 | tf_op jit(solution)/shard_map/ppermute | solution.py:731
  62.2 0.7 shard_map.96.order
  62.9 3.5 %collective-permute-done.5.far = f32[16,128]{1,0:T(8,128)S(1)} collective-permute-done((f32[16,128]{1,0:T(8,128)S(1)}, f32[16,128]{1,0:T(8,128)S(1)}, u32[]{:S(2)}, u32[]{:S(2)}) %collective-permute-start.5) | collective-permute-done | bytes 8224 | tf_op jit(solution)/shard_map/ppermute | solution.py:731
  66.4 0.0 collective-permute-done.4.near
  66.4 0.3 shard_map.97
  66.7 11.0 %all_to_all.29.got = f32[8,48,128]{2,1,0:T(8,128)S(1)} all-to-all(f32[8,48,128]{2,1,0:T(8,128)S(1)} %broadcast_in_dim.14), channel_id=1, replica_groups=mesh['gx'=8,'gy'=16] {'gx'}, dimensions={0} | all-to-all | bytes 393216 | tf_op jit(solution)/shard_map/all_to_all | solution.py:715
  77.8 1.1 %shard_map.98 = (f32[64,64]{1,0:T(8,128)}, f32[64,512]{1,0:T(8,128)}) custom-call(f32[8,48,128]{2,1,0:T(8,128)S(1)} %all_to_all.29.got, f32[64,128]{1,0:T(8,128)S(1)} %get-tuple-element.92.coarse, f32[7,96,128]{2,1,0:T(8,128)S(1)} %get-tuple-element.78.order.matrix, bf16[128,512]{1,0:T(8,128)(2,1)S(1)} %get-tuple-element.94.places), custom_call_target="tpu_custom_call" | custom-call | tf_op jit(solution)/shard_map/pallas_call | solution.py:31
  (7 shorter events, 0.1 us)
Async XLA Ops:
  2.2 5.9 %collective-permute-start.1 = (f32[80,128]{1,0:T(8,128)S(1)}, f32[80,128]{1,0:T(8,128)S(1)}, u32[]{:S(2)}, u32[]{:S(2)}) collective-permute-start(f32[80,128]{1,0:T(8,128)S(1)} %get-tuple-element.52), channel_id=1, source_target_pairs={{0,15},{1,2},{2,1},{3,4},{4,3},{5,6},{6,5},{7,8},{8,7},{9,10},{10,... | collective-permute-start | bytes 122888 | tf_op jit(solution)/shard_map/ppermute | solution.py:731
  5.6 2.6 %collective-permute-start = (f32[80,128]{1,0:T(8,128)S(1)}, f32[80,128]{1,0:T(8,128)S(1)}, u32[]{:S(2)}, u32[]{:S(2)}) collective-permute-start(f32[80,128]{1,0:T(8,128)S(1)} %get-tuple-element.51.order), channel_id=1, source_target_pairs={{0,1},{1,0},{2,3},{3,2},{4,5},{5,4},{6,7},{7,6},{8,9},{9,8},{10,11... | collective-permute-start | bytes 122888 | tf_op jit(solution)/shard_map/ppermute | solution.py:731
  25.0 1.3 %collective-permute-start.2 = (f32[80,128]{1,0:T(8,128)S(1)}, f32[80,128]{1,0:T(8,128)S(1)}, u32[]{:S(2)}, u32[]{:S(2)}) collective-permute-start(f32[80,128]{1,0:T(8,128)S(1)} %get-tuple-element.69.mine), channel_id=1, source_target_pairs={{0,1},{1,0},{2,3},{3,2},{4,5},{5,4},{6,7},{7,6},{8,9},{9,8},{10,11... | collective-permute-start | bytes 122888 | tf_op jit(solution)/shard_map/ppermute | solution.py:719
  50.3 1.3 %collective-permute-start.3 = (f32[32,128]{1,0:T(8,128)S(1)}, f32[32,128]{1,0:T(8,128)S(1)}, u32[]{:S(2)}, u32[]{:S(2)}) collective-permute-start(f32[32,128]{1,0:T(8,128)S(1)} %get-tuple-element.84.mine), channel_id=1, source_target_pairs={{0,1},{1,0},{2,3},{3,2},{4,5},{5,4},{6,7},{7,6},{8,9},{9,8},{10,11... | collective-permute-start | bytes 49160 | tf_op jit(solution)/shard_map/ppermute | solution.py:719
  61.1 5.3 %collective-permute-start.5 = (f32[16,128]{1,0:T(8,128)S(1)}, f32[16,128]{1,0:T(8,128)S(1)}, u32[]{:S(2)}, u32[]{:S(2)}) collective-permute-start(f32[16,128]{1,0:T(8,128)S(1)} %get-tuple-element.91), channel_id=1, source_target_pairs={{0,15},{1,2},{2,1},{3,4},{4,3},{5,6},{6,5},{7,8},{8,7},{9,10},{10,... | collective-permute-start | bytes 24584 | tf_op jit(solution)/shard_map/ppermute | solution.py:731
  61.4 5.0 %collective-permute-start.4 = (f32[16,128]{1,0:T(8,128)S(1)}, f32[16,128]{1,0:T(8,128)S(1)}, u32[]{:S(2)}, u32[]{:S(2)}) collective-permute-start(f32[16,128]{1,0:T(8,128)S(1)} %get-tuple-element.89.order), channel_id=1, source_target_pairs={{0,1},{1,0},{2,3},{3,2},{4,5},{5,4},{6,7},{7,6},{8,9},{9,8},{10,11... | collective-permute-start | bytes 24584 | tf_op jit(solution)/shard_map/ppermute | solution.py:731

commit v11 on v10

--- a/solution.py
+++ b/solution.py
@@ -178,8 +178,11 @@
         low = rolled(off, s, 1)
         alpha = -low * rolled(inv, s, 1)
         beta = -off * rolled(inv, -s, 1)
-        keep(2 * n, alpha)
-        keep(2 * n + 1, beta)
+        if s < NI // 2:
+            keep(2 * n, alpha)
+            keep(2 * n + 1, beta)
+        else:
+            keep(2 * n, alpha + beta)
         diag = diag + alpha * low + beta * off
         rhs = rhs + alpha * rolled(rhs, s, 1) + beta * rolled(rhs, -s, 1)
         if s < NI // 2:
@@ -302,8 +305,9 @@
 
 
 def x_second_solve(rhs, kept):
-    for n, s in enumerate(STEPS):
+    for n, s in enumerate(STEPS[:-1]):
         rhs = rhs + kept(2 * n) * rolled(rhs, s, 1) + kept(2 * n + 1) * rolled(rhs, -s, 1)
+    rhs = rhs + kept(2 * len(STEPS) - 2) * rolled(rhs, NI // 2, 1)
     return rhs * kept(2 * len(STEPS))
 
 

time: 79.2 us -> 79.2 us (level)
  no operation moved by 1% of the time
where the time goes in v11:
time: 79.2 us; the launch traced here: 78.9 us
  blocking collectives  57.8 us (73%)
  Pallas kernels  11 us (14%)
  waiting for transfers between devices  4.71 us (6%)
  starting transfers between devices  4.6 us (6%)
    all_to_all x3, blocking collectives, spread(): return lax.all_to_all(many, axis, split_axis=0, concat_axis=0, tiled=True)  37.6 us
    all_to_all x2, blocking collectives, spread_by_core(): lax.all_to_all(many, 'gy', split_axis=0, concat_axis=0, tiled=True, axis_...  20.2 us
    pallas_call x14, Pallas kernels, call(): pl.pallas_call(kernel, out_shape=outs, in_specs=[outside] * hbm + [spec]...  11 us
    ppermute x4, starting transfers between devices, swap(): return (lax.ppermute(near, 'gy', pairs), lax.ppermute(far, 'gy', others))  4.43 us
    ppermute x4, waiting for transfers between devices, swap(): return (lax.ppermute(near, 'gy', pairs), lax.ppermute(far, 'gy', others))  3.51 us
  transfers between devices with their start and end apart: 6, of which 3 were waited for; matrix products, arithmetic and copies ran while one was open for 0% of the time, Pallas kernels for 6%

profile of v11, /device:TPU:0, one launch (start us, length us, event | category | flops | bytes accessed | tf_op | source)
XLA Modules:
  0.0 78.9 jit_solution(10249142316960268618)
XLA Ops:
  0.6 1.6 %shard_map.85 = (f32[1536,128]{1,0:T(8,128)S(1)}, f32[80,128]{1,0:T(8,128)S(1)}, f32[80,128]{1,0:T(8,128)S(1)}, f32[128,128]{1,0:T(8,128)S(1)}) custom-call(f32[256,128]{1,0:T(8,128)} %bitcast.10, f32[256,128]{1,0:T(8,128)} %bitcast.11, f32[256,128]{1,0:T(8,128)} %bitcast.12, f32[256,128]{1,0:T(8,128)} %bitcast.13, f32[256,128]{1,0:T(8,128)} %bitcast.14, ...), custom_call_target="tpu_custom_call" | custom-call | tf_op jit(solution)/shard_map/pallas_call | solution.py:31
  2.2 3.4 %collective-permute-start.1 = (f32[80,128]{1,0:T(8,128)S(1)}, f32[80,128]{1,0:T(8,128)S(1)}, u32[]{:S(2)}, u32[]{:S(2)}) collective-permute-start(f32[80,128]{1,0:T(8,128)S(1)} %get-tuple-element.52), channel_id=1, source_target_pairs={{0,15},{1,2},{2,1},{3,4},{4,3},{5,6},{6,5},{7,8},{8,7},{9,10},{10,... | collective-permute-start | bytes 122888 | tf_op jit(solution)/shard_map/ppermute | solution.py:735
  5.6 0.0 collective-permute-start
  5.6 2.6 %shard_map.86 = (f32[256,128]{1,0:T(8,128)S(1)}, f32[256,128]{1,0:T(8,128)S(1)}, f32[256,128]{1,0:T(8,128)S(1)}, f32[3840,128]{1,0:T(8,128)S(1)}, f32[16,128]{1,0:T(8,128)S(1)}) custom-call(f32[1536,128]{1,0:T(8,128)S(1)} %get-tuple-element.50.xs, f32[80,128]{1,0:T(8,128)S(1)} %get-tuple-element.51.order), custom_call_target="tpu_custom_call" | custom-call | flops 100000000 | bytes 1048576 | tf_op jit(solution)/shard_map/pallas_call | solution.py:31
  8.1 0.0 collective-permute-done.1.far
  8.2 0.0 collective-permute-done.near
  8.2 0.8 %shard_map.87 = (f32[16,128]{1,0:T(8,128)S(1)}, f32[256,128]{1,0:T(8,128)S(1)}, f32[256,128]{1,0:T(8,128)S(1)}, f32[256,128]{1,0:T(8,128)S(1)}, f32[3840,128]{1,...) custom-call(f32[1536,128]{1,0:T(8,128)S(1)} %get-tuple-element.50.xs, ...), custom_call_target="tpu_custom_call", output_to_operand_aliasing={{1}: (5, {}), {2}: (6, {}), {3}: (7, {}), {4}: (8, {})} | custom-call | tf_op jit(solution)/shard_map/pallas_call | solution.py:31
  9.0 15.3 %all_to_all.25.got = f32[8,16,128]{2,1,0:T(8,128)S(1)} all-to-all(f32[8,16,128]{2,1,0:T(8,128)S(1)} %broadcast_in_dim.10), channel_id=1, replica_groups=mesh['gx'=8,'gy'=16] {'gx'}, dimensions={0} | all-to-all | bytes 131072 | tf_op jit(solution)/shard_map/all_to_all | solution.py:719
  24.3 0.7 shard_map.89
  25.0 0.1 collective-permute-start.2
  25.1 0.3 shard_map.88
  25.3 1.0 %collective-permute-done.2.theirs = f32[80,128]{1,0:T(8,128)S(1)} collective-permute-done((f32[80,128]{1,0:T(8,128)S(1)}, f32[80,128]{1,0:T(8,128)S(1)}, u32[]{:S(2)}, u32[]{:S(2)}) %collective-permute-start.2) | collective-permute-done | bytes 40992 | tf_op jit(solution)/shard_map/ppermute | solution.py:723
  26.3 11.2 %all_to_all.26.got = f32[8,80,128]{2,1,0:T(8,128)S(1)} all-to-all(f32[8,80,128]{2,1,0:T(8,128)S(1)} %broadcast_in_dim.11), channel_id=1, replica_groups={{0,2,4,6,8,10,12,14},{1,3,5,7,9,11,13,15},{16,18,20,22,24,26,28,30},{17..., dimensions={0} | all-to-all | bytes 655360 | tf_op jit(solution)/shard_map/all_to_all | solution.py:729
  37.6 1.0 %shard_map.91 = (f32[256,128]{1,0:T(8,128)S(1)}, f32[24,16,128]{2,1,0:T(8,128)S(1)}, f32[40,128]{1,0:T(8,128)S(1)}) custom-call(f32[1536,128]{1,0:T(8,128)S(1)} %get-tuple-element.50.xs, f32[16,128]{1,0:T(8,128)S(1)} %get-tuple-element.59.below, f32[8,80,128]{2,1,0:T(8,128)S(1)} %all_to_all.26.got, f32[5,16,128]{2,1,0:T(8,128)S(1)} %get-tuple-element.71.joint, ...), custom_call_target="tpu_custom_call" | custom-call | tf_op jit(solution)/shard_map/pallas_call | solution.py:31
  38.6 11.2 %all_to_all.27.got = f32[8,40,128]{2,1,0:T(8,128)S(1)} all-to-all(f32[8,40,128]{2,1,0:T(8,128)S(1)} %broadcast_in_dim.12), channel_id=1, replica_groups=mesh['gx'=8,'gy'=16] {'gx'}, dimensions={0} | all-to-all | bytes 327680 | tf_op jit(solution)/shard_map/all_to_all | solution.py:719
  49.8 0.5 shard_map.93
  50.3 0.1 collective-permute-start.3
  50.4 0.9 %shard_map.92 = (f32[7,96,128]{2,1,0:T(8,128)S(1)}, f32[7,96,128]{2,1,0:T(8,128)S(1)}, bf16[128,512]{1,0:T(8,128)(2,1)S(1)}) custom-call(f32[384,128]{1,0:T(8,128)S(1)} %get-tuple-element.63.ext, f32[8,40,128]{2,1,0:T(8,128)S(1)} %all_to_all.27.got), custom_call_target="tpu_custom_call" | custom-call | flops 10000000 | bytes 1048576 | tf_op jit(solution)/shard_map/pallas_call | solution.py:31
  51.3 0.2 collective-permute-done.3.theirs
  51.6 9.0 %all_to_all.28.got = f32[8,32,128]{2,1,0:T(8,128)S(1)} all-to-all(f32[8,32,128]{2,1,0:T(8,128)S(1)} %broadcast_in_dim.13), channel_id=1, replica_groups={{0,2,4,6,8,10,12,14},{1,3,5,7,9,11,13,15},{16,18,20,22,24,26,28,30},{17..., dimensions={0} | all-to-all | bytes 262144 | tf_op jit(solution)/shard_map/all_to_all | solution.py:729
  60.6 0.5 shard_map.95
  61.1 0.2 collective-permute-start.5
  61.4 0.8 %collective-permute-start.4 = (f32[16,128]{1,0:T(8,128)S(1)}, f32[16,128]{1,0:T(8,128)S(1)}, u32[]{:S(2)}, u32[]{:S(2)}) collective-permute-start(f32[16,128]{1,0:T(8,128)S(1)} %get-tuple-element.89.order), channel_id=1, source_target_pairs={{0,1},{1,0},{2,3},{3,2},{4,5},{5,4},{6,7},{7,6},{8,9},{9,8},{10,11... | collective-permute-start | bytes 24584 | tf_op jit(solution)/shard_map/ppermute | solution.py:735
  62.2 0.7 shard_map.96.order
  62.9 3.5 %collective-permute-done.5.far = f32[16,128]{1,0:T(8,128)S(1)} collective-permute-done((f32[16,128]{1,0:T(8,128)S(1)}, f32[16,128]{1,0:T(8,128)S(1)}, u32[]{:S(2)}, u32[]{:S(2)}) %collective-permute-start.5) | collective-permute-done | bytes 8224 | tf_op jit(solution)/shard_map/ppermute | solution.py:735
  66.4 0.0 collective-permute-done.4.near
  66.4 0.3 shard_map.97
  66.7 11.0 %all_to_all.29.got = f32[8,48,128]{2,1,0:T(8,128)S(1)} all-to-all(f32[8,48,128]{2,1,0:T(8,128)S(1)} %broadcast_in_dim.14), channel_id=1, replica_groups=mesh['gx'=8,'gy'=16] {'gx'}, dimensions={0} | all-to-all | bytes 393216 | tf_op jit(solution)/shard_map/all_to_all | solution.py:719
  77.7 1.1 %shard_map.98 = (f32[64,64]{1,0:T(8,128)}, f32[64,512]{1,0:T(8,128)}) custom-call(f32[8,48,128]{2,1,0:T(8,128)S(1)} %all_to_all.29.got, f32[64,128]{1,0:T(8,128)S(1)} %get-tuple-element.92.coarse, f32[7,96,128]{2,1,0:T(8,128)S(1)} %get-tuple-element.78.order.matrix, bf16[128,512]{1,0:T(8,128)(2,1)S(1)} %get-tuple-element.94.places), custom_call_target="tpu_custom_call" | custom-call | tf_op jit(solution)/shard_map/pallas_call | solution.py:31
  (7 shorter events, 0.1 us)
Async XLA Ops:
  2.2 5.9 %collective-permute-start.1 = (f32[80,128]{1,0:T(8,128)S(1)}, f32[80,128]{1,0:T(8,128)S(1)}, u32[]{:S(2)}, u32[]{:S(2)}) collective-permute-start(f32[80,128]{1,0:T(8,128)S(1)} %get-tuple-element.52), channel_id=1, source_target_pairs={{0,15},{1,2},{2,1},{3,4},{4,3},{5,6},{6,5},{7,8},{8,7},{9,10},{10,... | collective-permute-start | bytes 122888 | tf_op jit(solution)/shard_map/ppermute | solution.py:735
  5.6 2.6 %collective-permute-start = (f32[80,128]{1,0:T(8,128)S(1)}, f32[80,128]{1,0:T(8,128)S(1)}, u32[]{:S(2)}, u32[]{:S(2)}) collective-permute-start(f32[80,128]{1,0:T(8,128)S(1)} %get-tuple-element.51.order), channel_id=1, source_target_pairs={{0,1},{1,0},{2,3},{3,2},{4,5},{5,4},{6,7},{7,6},{8,9},{9,8},{10,11... | collective-permute-start | bytes 122888 | tf_op jit(solution)/shard_map/ppermute | solution.py:735
  25.0 1.3 %collective-permute-start.2 = (f32[80,128]{1,0:T(8,128)S(1)}, f32[80,128]{1,0:T(8,128)S(1)}, u32[]{:S(2)}, u32[]{:S(2)}) collective-permute-start(f32[80,128]{1,0:T(8,128)S(1)} %get-tuple-element.69.mine), channel_id=1, source_target_pairs={{0,1},{1,0},{2,3},{3,2},{4,5},{5,4},{6,7},{7,6},{8,9},{9,8},{10,11... | collective-permute-start | bytes 122888 | tf_op jit(solution)/shard_map/ppermute | solution.py:723
  50.3 1.3 %collective-permute-start.3 = (f32[32,128]{1,0:T(8,128)S(1)}, f32[32,128]{1,0:T(8,128)S(1)}, u32[]{:S(2)}, u32[]{:S(2)}) collective-permute-start(f32[32,128]{1,0:T(8,128)S(1)} %get-tuple-element.84.mine), channel_id=1, source_target_pairs={{0,1},{1,0},{2,3},{3,2},{4,5},{5,4},{6,7},{7,6},{8,9},{9,8},{10,11... | collective-permute-start | bytes 49160 | tf_op jit(solution)/shard_map/ppermute | solution.py:723
  61.1 5.3 %collective-permute-start.5 = (f32[16,128]{1,0:T(8,128)S(1)}, f32[16,128]{1,0:T(8,128)S(1)}, u32[]{:S(2)}, u32[]{:S(2)}) collective-permute-start(f32[16,128]{1,0:T(8,128)S(1)} %get-tuple-element.91), channel_id=1, source_target_pairs={{0,15},{1,2},{2,1},{3,4},{4,3},{5,6},{6,5},{7,8},{8,7},{9,10},{10,... | collective-permute-start | bytes 24584 | tf_op jit(solution)/shard_map/ppermute | solution.py:735
  61.4 5.0 %collective-permute-start.4 = (f32[16,128]{1,0:T(8,128)S(1)}, f32[16,128]{1,0:T(8,128)S(1)}, u32[]{:S(2)}, u32[]{:S(2)}) collective-permute-start(f32[16,128]{1,0:T(8,128)S(1)} %get-tuple-element.89.order), channel_id=1, source_target_pairs={{0,1},{1,0},{2,3},{3,2},{4,5},{5,4},{6,7},{7,6},{8,9},{9,8},{10,11... | collective-permute-start | bytes 24584 | tf_op jit(solution)/shard_map/ppermute | solution.py:735
